TPU v7x, 32 devices: a whole 2x2x4 slice. The times are simulated.
32 devices in a mesh: by: 4 (over z), bx: 8 (over y, x, core).
Axes of the slice: x: 2, y: 2, z: 4, core: 2. Of those that a mesh axis runs over, the one named last changes fastest.
Arguments:
- tracers: float32 [20, 128, 16, 2048], P(None, ('by', 'bx')), may hold values from 0 to 1
- vertical_speed: float32 [20, 128, 2048], P(None, ('by', 'bx')), may hold values from -0.4 to 0.4
- diffusivity: float32 [20, 128, 2048], P(None, ('by', 'bx')), may hold values from 0.02 to 2
- buoyancy_force: bfloat16 [20, 128, 2048], P(None, ('by', 'bx')), may hold values from -2.1 to 2.1
- wet_levels: int32 [128, 2048], P(('by', 'bx')), may hold values from 0 to 20
- surface_patch: int32 [128, 2048], P(('by', 'bx')), may hold values from 0 to 15
- prior_height: float32 [128, 2048], P(('by', 'bx')), may hold values from -5 to 5
- land_mask: int32 [128, 16, 128], P(('by', 'bx')), may hold values 0 or 1
- baroclinic_map: int32 [128], replicated, may hold values from 0 to 127, as said below
- barotropic_map: int32 [128], replicated, may hold values from 0 to 127, as said below
Outputs:
- new_tracers: float32 [20, 128, 16, 2048], P(None, ('by', 'bx'))
- surface_height: float32 [128, 16, 128], P(('by', 'bx'))
Inputs may be any that keep to these rules, and one draw needn't show every extreme that they name: baroclinic_map[s] is the geographic block held in baroclinic slot s, blocks numbered row by row with 32 to a block row; it lies in block row s // 32, and every block appears once. barotropic_map[s] is the geographic block held in barotropic slot s, blocks numbered row by row with 32 to a block row; it lies in block row s // 32, and every block appears once.
All inputs are finite; a program needn't handle non-finite values. No bound on the sum of `land_mask` on one device may be relied on, other than what follows from the above.
Results may differ from a plain program's by a relative error of at most 0.0003.
Values sent between devices are 32-bit elements; how exact they have to be, the bound alone decides.
No kernel may reach another device: no remote copies, remote signals or barrier semaphores. Data moves between devices by JAX's collectives and lax.ppermute only.
A program may use at most 128 MiB of HBM per device.

v0:
```python
import jax
import jax.numpy as jnp
from jax import lax
from jax.sharding import PartitionSpec as P

ITERS = 6


RESTORE = 0.5
SURFACE = 0.1
FACE_SCALE = 2.0
PRECISE = lax.Precision.HIGHEST


def padded_2(block, sides, width):
    for axis, dim in sides:
        count = lax.axis_size(axis)
        forward = [(i, i + 1) for i in range(count - 1)]
        backward = [(target, source) for source, target in forward]
        low = lax.ppermute(
            lax.slice_in_dim(block, block.shape[dim] - width, None, axis=dim), axis, forward
        )
        high = lax.ppermute(lax.slice_in_dim(block, 0, width, axis=dim), axis, backward)
        block = jnp.concatenate([low, block, high], axis=dim)
    return block


def column_step(tracers, vertical_speed, diffusivity, wet_levels, surface_patch):
    depth_index = lax.broadcasted_iota(jnp.int32, vertical_speed.shape, 0)
    wet_level = (depth_index < wet_levels[None]).astype(jnp.float32)
    open_faces = (depth_index + 1 < wet_levels[None]).astype(jnp.float32)
    speed_open = (vertical_speed * open_faces)[:, :, None]
    shifted_up = jnp.concatenate([tracers[1:], jnp.zeros_like(tracers[:1])], axis=0)
    flux_below = jnp.maximum(speed_open, 0.0) * shifted_up + jnp.minimum(speed_open, 0.0) * tracers
    flux_above = jnp.concatenate([jnp.zeros_like(flux_below[:1]), flux_below[:-1]], axis=0)
    advected = wet_level[:, :, None] * (tracers + flux_below - flux_above)
    mixing = diffusivity * open_faces
    mixing_above = jnp.concatenate([jnp.zeros_like(mixing[:1]), mixing[:-1]], axis=0)
    surface_row = (depth_index == 0).astype(jnp.float32) * wet_level * RESTORE
    diagonal = 1.0 + mixing + mixing_above + surface_row
    tracer_ids = lax.broadcasted_iota(jnp.int32, (1, tracers.shape[2], 1), 1)
    targets = (surface_patch[:, None, :] == tracer_ids).astype(jnp.float32)
    right_side = advected + surface_row[:, :, None] * targets[None]

    def forward(carry, layer):
        ratio_prev, value_prev = carry
        lower_band, diag_now, upper_band, right_now = layer
        pivot_now = diag_now - lower_band * ratio_prev
        ratio_now = upper_band / pivot_now
        value_now = (right_now - lower_band[:, None] * value_prev) / pivot_now[:, None]
        return ((ratio_now, value_now), (ratio_now, value_now))

    start_carry = (
        jnp.zeros(mixing.shape[1:], jnp.float32),
        jnp.zeros(tracers.shape[1:], jnp.float32),
    )
    ignored, (ratios, values) = lax.scan(
        forward, start_carry, (-mixing_above, diagonal, -mixing, right_side)
    )

    def backward(following, layer):
        ratio_now, value_now = layer
        solved_now = value_now - ratio_now[:, None] * following
        return (solved_now, solved_now)

    ignored_too, solved = lax.scan(
        backward, jnp.zeros(tracers.shape[1:], jnp.float32), (ratios, values), reverse=True
    )
    return solved


def local(
    tracers,
    vertical_speed,
    diffusivity,
    buoyancy_force,
    wet_levels,
    surface_patch,
    prior_height,
    land_mask,
    baroclinic_map,
    barotropic_map,
):
    blocks = wet_levels.shape[0]
    block_rows = land_mask.shape[1]
    block_cols = land_mask.shape[2]
    levels = vertical_speed.shape[0]
    band_row = lax.axis_index("by")
    column = lax.axis_index("bx")
    band_width = blocks * lax.axis_size("bx")
    band_first_slot = band_row * band_width
    clinic_band = (
        lax.dynamic_slice_in_dim(baroclinic_map, band_first_slot, band_width) - band_first_slot
    )
    tropic_band = (
        lax.dynamic_slice_in_dim(barotropic_map, band_first_slot, band_width) - band_first_slot
    )
    my_columns = lax.dynamic_slice_in_dim(tropic_band, column * blocks, blocks)
    depth_index = lax.broadcasted_iota(jnp.int32, buoyancy_force.shape, 0)
    wet_level = (depth_index < wet_levels[None]).astype(jnp.float32)
    forcing = jnp.sum(wet_level * buoyancy_force.astype(jnp.float32), axis=0)
    payload = jnp.stack([forcing, wet_levels.astype(jnp.float32), prior_height], axis=0)
    selector = (clinic_band[None, :] == my_columns[:, None]).astype(jnp.float32)
    relaid = jnp.einsum(
        "jt,qtc->qjc",
        selector,
        lax.all_gather(payload, "bx", axis=1, tiled=True),
        precision=PRECISE,
    )
    new_tracers = column_step(tracers, vertical_speed, diffusivity, wet_levels, surface_patch)
    shape_flat = (blocks, block_rows, block_cols)
    ocean_mask = land_mask.astype(jnp.float32)
    depth_field = relaid[1].reshape(shape_flat)
    source = ocean_mask * relaid[0].reshape(shape_flat)
    first_guess = ocean_mask * relaid[2].reshape(shape_flat)
    west_pick = (tropic_band[None, :] == (my_columns[:, None] - 1) % band_width).astype(jnp.float32)
    east_pick = (tropic_band[None, :] == (my_columns[:, None] + 1) % band_width).astype(jnp.float32)
    band_slots = lax.broadcasted_iota(jnp.int32, (band_width, 1), 0)
    geo_pick = (tropic_band[None, :] == band_slots).astype(jnp.float32)
    my_pick = (band_slots[:, 0][None, :] == my_columns[:, None]).astype(jnp.float32)

    def extend(field_blocks):
        edge_cols = jnp.stack([field_blocks[..., 0], field_blocks[..., -1]], axis=2)
        edge_rows = jnp.stack([field_blocks[..., 0, :], field_blocks[..., -1, :]], axis=2)
        gathered_cols, gathered_rows = (
            lax.all_gather(edge_cols, "bx", axis=1, tiled=True),
            lax.all_gather(edge_rows, "bx", axis=1, tiled=True),
        )
        geo_rows = jnp.einsum("ct,qtsw->sqcw", geo_pick, gathered_rows, precision=PRECISE)
        beside = padded_2(geo_rows, (("by", 0),), 1)
        north_side = jnp.einsum("jc,qcw->qjw", my_pick, beside[0], precision=PRECISE)
        south_side = jnp.einsum("jc,qcw->qjw", my_pick, beside[3], precision=PRECISE)
        west_side = jnp.einsum("jt,qth->qjh", west_pick, gathered_cols[:, :, 1], precision=PRECISE)
        east_side = jnp.einsum("jt,qth->qjh", east_pick, gathered_cols[:, :, 0], precision=PRECISE)
        middle = jnp.concatenate([west_side[..., None], field_blocks, east_side[..., None]], axis=3)
        north_row = jnp.pad(north_side, ((0, 0), (0, 0), (1, 1)))[:, :, None, :]
        south_row = jnp.pad(south_side, ((0, 0), (0, 0), (1, 1)))[:, :, None, :]
        return jnp.concatenate([north_row, middle, south_row], axis=2)

    statics = extend(jnp.stack([depth_field, ocean_mask], axis=0))
    depth_padded = statics[0]
    ocean_padded = statics[1]
    face_factor = FACE_SCALE / levels

    def face_weight(depth_other, ocean_other):
        return face_factor * jnp.minimum(depth_field, depth_other) * ocean_mask * ocean_other

    east_face = face_weight(depth_padded[:, 1:-1, 2:], ocean_padded[:, 1:-1, 2:])
    west_face = face_weight(depth_padded[:, 1:-1, :-2], ocean_padded[:, 1:-1, :-2])
    south_face = face_weight(depth_padded[:, 2:, 1:-1], ocean_padded[:, 2:, 1:-1])
    north_face = face_weight(depth_padded[:, :-2, 1:-1], ocean_padded[:, :-2, 1:-1])
    centre_weight = SURFACE * ocean_mask + (1.0 - ocean_mask)
    precond_diagonal = centre_weight + east_face + west_face + south_face + north_face

    def operate(field_blocks):
        padded = extend(field_blocks[None])[0]
        centre = centre_weight * field_blocks
        result = centre + east_face * (field_blocks - padded[:, 1:-1, 2:])
        result = result + west_face * (field_blocks - padded[:, 1:-1, :-2])
        result = result + south_face * (field_blocks - padded[:, 2:, 1:-1])
        return result + north_face * (field_blocks - padded[:, :-2, 1:-1])

    solution = first_guess
    residual = source - operate(solution)
    precond = residual / precond_diagonal

    def two_sums(residual_now, precond_now, image_now):
        return lax.psum(
            (jnp.sum(residual_now * precond_now), jnp.sum(precond_now * image_now)), ("by", "bx")
        )

    image_field = operate(precond)
    norm_now, curvature_now = two_sums(residual, precond, image_field)
    step_size = norm_now / curvature_now
    direction = precond
    along = image_field
    for step_index in range(ITERS):
        solution = solution + step_size * direction
        residual = residual - step_size * along
        if step_index + 1 < ITERS:
            precond = residual / precond_diagonal
            image_field = operate(precond)
            norm_next, curvature_now = two_sums(residual, precond, image_field)
            step_ratio = norm_next / norm_now
            step_size = norm_next / (curvature_now - step_ratio * norm_next / step_size)
            direction = precond + step_ratio * direction
            along = image_field + step_ratio * along
            norm_now = norm_next
    return (new_tracers, solution)


def solution(mesh):
    return jax.shard_map(
        local,
        mesh=mesh,
        in_specs=(
            P(None, ("by", "bx"), None, None),
            P(None, ("by", "bx"), None),
            P(None, ("by", "bx"), None),
            P(None, ("by", "bx"), None),
            P(("by", "bx"), None),
            P(("by", "bx"), None),
            P(("by", "bx"), None),
            P(("by", "bx"), None, None),
            P(),
            P(),
        ),
        out_specs=(P(None, ("by", "bx"), None, None), P(("by", "bx"), None, None)),
        check_vma=False,
    )
```

profile of v0, /device:TPU:0, one launch (start us, length us, event | category | flops | bytes accessed | tf_op | source)
XLA Modules:
  0.0 655.1 jit_solution(5793878280645844204)
XLA Ops:
  9.6 12.4 %all_gather.51 = f32[3,32,2048]{2,0,1:T(4,128)S(1)} all-gather(f32[3,4,2048]{2,0,1:T(4,128)S(1)} %pad_maximum_fusion.1), channel_id=1, replica_groups=mesh['by'=4,'bx'=8] {'bx'}, dimensions={1}, use_global_device_ids=true | all-gather | bytes 884736 | tf_op jit(solution)/shard_map/all_gather | solution.py:107
  22.9 9.1 %all_gather.54 = f32[1,32,2,128]{3,2,0,1:T(2,128)S(1)} all-gather(f32[1,4,2,128]{3,2,0,1:T(2,128)S(1)} %maximum_bitcast_fusion.7), channel_id=1, replica_groups=mesh['by'=4,'bx'=8] {'bx'}, dimensions={1}, use_global_device_ids=true | all-gather | bytes 36864 | tf_op jit(solution)/shard_map/all_gather | solution.py:127
  37.6 8.3 %all_gather.52 = f32[2,32,2,128]{3,2,0,1:T(2,128)S(1)} all-gather(f32[2,4,2,128]{3,2,0,1:T(2,128)S(1)} %fusion.121), channel_id=1, replica_groups=mesh['by'=4,'bx'=8] {'bx'}, dimensions={1}, use_global_device_ids=true | all-gather | bytes 73728 | tf_op jit(solution)/shard_map/all_gather | solution.py:127
  53.5 9.1 %all_gather.55 = f32[1,32,2,16]{3,2,0,1:T(2,128)S(1)} all-gather(f32[1,4,2,16]{3,2,0,1:T(2,128)S(1)} %copy.201), channel_id=1, replica_groups=mesh['by'=4,'bx'=8] {'bx'}, dimensions={1}, use_global_device_ids=true | all-gather | bytes 4608 | tf_op jit(solution)/shard_map/all_gather | solution.py:126
  62.9 8.4 %all_gather.53 = f32[2,32,2,16]{3,2,0,1:T(2,128)S(1)} all-gather(f32[2,4,2,16]{3,2,0,1:T(2,128)S(1)} %copy.191), channel_id=1, replica_groups=mesh['by'=4,'bx'=8] {'bx'}, dimensions={1}, use_global_device_ids=true | all-gather | bytes 9216 | tf_op jit(solution)/shard_map/all_gather | solution.py:126
  77.2 9.8 %multiply_add_fusion.1 = f32[20,4,16,2048]{3,2,1,0:T(8,128)} fusion(f32[20,4,16,2048]{3,2,1,0:T(8,128)} %param.14, f32[19,4,16,2048]{3,2,1,0:T(8,128)S(1)} %slice-done, f32[20,4,2048]{2,1,0:T(4,128)S(1)} %get-tuple-element.308, f32[20,4,2048]{2,1,0:T(4,128)S(1)} %get-tuple-element.307), kind=kLoop, calls=%fused_computation.14 | loop fusion | flops 7864320 | bytes 32243712 | tf_op jit(solution)/shard_map/add | solution.py:34
  90.9 13.4 %multiply_add_fusion = f32[20,4,16,2048]{3,2,1,0:T(8,128)} fusion(f32[19,4,16,2048]{3,2,1,0:T(8,128)S(1)} %slice-done.1, f32[20,4,16,2048]{3,2,1,0:T(8,128)} %param.14, f32[20,4,16,2048]{3,2,1,0:T(8,128)} %multiply_add_fusion.1, f32[4,16,2048]{2,1,0:T(8,128)S(1)} %fusion.3, f32[20,4,2048]{2,1,0:T(4,128)S(1)} %copy-done.1, f32[20,4,2048]{2,1,0:T(4,128)S(1)} %fusion.2), kind=kLoop, calls=%fused_computation.13 | loop fusion | flops 13107200 | bytes 43253760 | tf_op jit(solution)/shard_map/add | solution.py:43
  109.8 58.2 %while.34 = (s32[]{:T(128)}, f32[4,2048]{1,0:T(4,128)S(1)}, f32[4,16,2048]{2,1,0:T(8,128)S(1)}, f32[20,4,2048]{2,1,0:T(4,128)S(1)}, f32[20,4,16,2048]{3,2,1,0:T(...) while((s32[]{:T(128)}, f32[4,2048]{1,0:T(4,128)S(1)}, ...), condition=%wide.region_1.2_spmd.clone, body=%wide.region_0.0_spmd.clone.sunk | while | flops 557059 | bytes 2425468 | solution.py:57
  173.4 43.3 %while.35 = (s32[]{:T(128)}, f32[4,16,2048]{2,1,0:T(8,128)S(1)}, f32[20,4,16,2048]{3,2,1,0:T(8,128)}, f32[20,4,16,2048]{3,2,1,0:T(8,128)}, f32[20,4,2048]{2,1,0:T(4,128)S(1)}, /*index=5*/s32[]{:T(128)}, s32[]{:T(128)}, s32[]{:T(128)}) while((s32[]{:T(128)}, f32[4,16,2048]{2,1,0:T(8,128)S(1)}, f32[20,4,16,2048]{3,2,1,0:T(8,128)}, ...), condition=%wide.region_3.4_spmd.clone, body=%wide.region_2.3_spmd.clone.sunk | while | flops 393220 | bytes 2195571 | solution.py:66
  222.3 9.1 %all_gather.57 = f32[1,32,2,16]{3,2,0,1:T(2,128)S(1)} all-gather(f32[1,4,2,16]{3,2,0,1:T(2,128)S(1)} %copy.208), channel_id=1, replica_groups=mesh['by'=4,'bx'=8] {'bx'}, dimensions={1}, use_global_device_ids=true | all-gather | bytes 4608 | tf_op jit(solution)/shard_map/all_gather | solution.py:126
  251.5 39.7 %all-reduce.24 = (f32[]{:T(128)}, f32[]{:T(128)}) all-reduce(f32[]{:T(128)} %get-tuple-element.227, f32[]{:T(128)} %get-tuple-element.226), channel_id=1, replica_groups=mesh['by'=4,'bx'=8] {'by','bx'}, use_global_device_ids=true, to_apply=%region_6.7 | all-reduce | flops 2 | bytes 16 | tf_op jit(solution)/shard_map/psum | solution.py:168
  292.8 10.1 %all_gather.59 = f32[1,32,2,16]{3,2,0,1:T(2,128)S(1)} all-gather(f32[1,4,2,16]{3,2,0,1:T(2,128)S(1)} %copy.215), channel_id=1, replica_groups=mesh['by'=4,'bx'=8] {'bx'}, dimensions={1}, use_global_device_ids=true | all-gather | bytes 4608 | tf_op jit(solution)/shard_map/all_gather | solution.py:126
  303.2 9.1 %all_gather.58 = f32[1,32,2,128]{3,2,0,1:T(2,128)S(1)} all-gather(f32[1,4,2,128]{3,2,0,1:T(2,128)S(1)} %maximum_bitcast_fusion.9), channel_id=1, replica_groups=mesh['by'=4,'bx'=8] {'bx'}, dimensions={1}, use_global_device_ids=true | all-gather | bytes 36864 | tf_op jit(solution)/shard_map/all_gather | solution.py:127
  321.7 39.7 %all-reduce.23 = (f32[]{:T(128)}, f32[]{:T(128)}) all-reduce(f32[]{:T(128)} %get-tuple-element.223, f32[]{:T(128)} %get-tuple-element.222), channel_id=1, replica_groups=mesh['by'=4,'bx'=8] {'by','bx'}, use_global_device_ids=true, to_apply=%region_10.11 | all-reduce | flops 2 | bytes 16 | tf_op jit(solution)/shard_map/psum | solution.py:168
  366.1 10.1 %all_gather.61 = f32[1,32,2,16]{3,2,0,1:T(2,128)S(1)} all-gather(f32[1,4,2,16]{3,2,0,1:T(2,128)S(1)} %copy.222), channel_id=1, replica_groups=mesh['by'=4,'bx'=8] {'bx'}, dimensions={1}, use_global_device_ids=true | all-gather | bytes 4608 | tf_op jit(solution)/shard_map/all_gather | solution.py:126
  393.9 39.7 %all-reduce.22 = (f32[]{:T(128)}, f32[]{:T(128)}) all-reduce(f32[]{:T(128)} %get-tuple-element.219, f32[]{:T(128)} %get-tuple-element.218), channel_id=1, replica_groups=mesh['by'=4,'bx'=8] {'by','bx'}, use_global_device_ids=true, to_apply=%region_14.15 | all-reduce | flops 2 | bytes 16 | tf_op jit(solution)/shard_map/psum | solution.py:168
  437.8 10.1 %all_gather.63 = f32[1,32,2,16]{3,2,0,1:T(2,128)S(1)} all-gather(f32[1,4,2,16]{3,2,0,1:T(2,128)S(1)} %copy.229), channel_id=1, replica_groups=mesh['by'=4,'bx'=8] {'bx'}, dimensions={1}, use_global_device_ids=true | all-gather | bytes 4608 | tf_op jit(solution)/shard_map/all_gather | solution.py:126
  448.1 9.1 %all_gather.62 = f32[1,32,2,128]{3,2,0,1:T(2,128)S(1)} all-gather(f32[1,4,2,128]{3,2,0,1:T(2,128)S(1)} %maximum_bitcast_fusion.11), channel_id=1, replica_groups=mesh['by'=4,'bx'=8] {'bx'}, dimensions={1}, use_global_device_ids=true | all-gather | bytes 36864 | tf_op jit(solution)/shard_map/all_gather | solution.py:127
  466.7 39.7 %all-reduce.21 = (f32[]{:T(128)}, f32[]{:T(128)}) all-reduce(f32[]{:T(128)} %get-tuple-element.215, f32[]{:T(128)} %get-tuple-element.214), channel_id=1, replica_groups=mesh['by'=4,'bx'=8] {'by','bx'}, use_global_device_ids=true, to_apply=%region_18.19 | all-reduce | flops 2 | bytes 16 | tf_op jit(solution)/shard_map/psum | solution.py:168
  510.4 10.0 %all_gather.65 = f32[1,32,2,16]{3,2,0,1:T(2,128)S(1)} all-gather(f32[1,4,2,16]{3,2,0,1:T(2,128)S(1)} %copy.236), channel_id=1, replica_groups=mesh['by'=4,'bx'=8] {'bx'}, dimensions={1}, use_global_device_ids=true | all-gather | bytes 4608 | tf_op jit(solution)/shard_map/all_gather | solution.py:126
  538.2 39.7 %all-reduce.20 = (f32[]{:T(128)}, f32[]{:T(128)}) all-reduce(f32[]{:T(128)} %get-tuple-element.211, f32[]{:T(128)} %get-tuple-element.210), channel_id=1, replica_groups=mesh['by'=4,'bx'=8] {'by','bx'}, use_global_device_ids=true, to_apply=%region_22.23 | all-reduce | flops 2 | bytes 16 | tf_op jit(solution)/shard_map/psum | solution.py:168
  582.1 10.1 %all_gather.67 = f32[1,32,2,16]{3,2,0,1:T(2,128)S(1)} all-gather(f32[1,4,2,16]{3,2,0,1:T(2,128)S(1)} %copy.243), channel_id=1, replica_groups=mesh['by'=4,'bx'=8] {'bx'}, dimensions={1}, use_global_device_ids=true | all-gather | bytes 4608 | tf_op jit(solution)/shard_map/all_gather | solution.py:126
  592.4 9.1 %all_gather.66 = f32[1,32,2,128]{3,2,0,1:T(2,128)S(1)} all-gather(f32[1,4,2,128]{3,2,0,1:T(2,128)S(1)} %maximum_bitcast_fusion.13), channel_id=1, replica_groups=mesh['by'=4,'bx'=8] {'bx'}, dimensions={1}, use_global_device_ids=true | all-gather | bytes 36864 | tf_op jit(solution)/shard_map/all_gather | solution.py:127
  611.0 39.7 %all-reduce.19 = (f32[]{:T(128)}, f32[]{:T(128)}) all-reduce(f32[]{:T(128)} %get-tuple-element.207, f32[]{:T(128)} %get-tuple-element.206), channel_id=1, replica_groups=mesh['by'=4,'bx'=8] {'by','bx'}, use_global_device_ids=true, to_apply=%region_26.27 | all-reduce | flops 2 | bytes 16 | tf_op jit(solution)/shard_map/psum | solution.py:168
  (325 shorter events, 236.8 us)
Async XLA Ops:
  0.6 52.7 %copy-start.2 = (s32[4,2048]{1,0:T(4,128)S(1)}, s32[4,2048]{1,0:T(4,128)}, u32[]{:S(2)}) copy-start(s32[4,2048]{1,0:T(4,128)} %param.18) | copy-start | bytes 98308
  0.6 22.3 %copy-start = (s32[4,16,128]{2,1,0:T(8,128)S(1)}, s32[4,16,128]{2,1,0:T(8,128)}, u32[]{:S(2)}) copy-start(s32[4,16,128]{2,1,0:T(8,128)} %param.21) | copy-start | bytes 98308
  32.2 185.4 %collective-permute-start.2 = (f32[1,1,32,128]{3,2,0,1:T(8,128)S(1)}, f32[1,1,32,128]{3,2,0,1:T(8,128)}, u32[]{:S(2)}, u32[]{:S(2)}) collective-permute-start(f32[1,1,32,128]{3,2,0,1:T(8,128)S(1)} %get-tuple-element.362), channel_id=1, source_target_pairs={{0,8},{8,16},{16,24},{1,9},{9,17},{17,25},{2,10},{10,18},{18,26},{... | collective-permute-start | bytes 49160 | tf_op jit(solution)/shard_map/ppermute | solution.py:20
  36.3 182.3 %collective-permute-start.3 = (f32[1,1,32,128]{3,2,0,1:T(8,128)S(1)}, f32[1,1,32,128]{3,2,0,1:T(8,128)}, u32[]{:S(2)}, u32[]{:S(2)}) collective-permute-start(f32[1,1,32,128]{3,2,0,1:T(8,128)S(1)} %get-tuple-element.363), channel_id=1, source_target_pairs={{8,0},{16,8},{24,16},{9,1},{17,9},{25,17},{10,2},{18,10},{26,18},{... | collective-permute-start | bytes 49160 | tf_op jit(solution)/shard_map/ppermute | solution.py:23
  46.0 173.6 %collective-permute-start = (f32[1,2,32,128]{3,2,0,1:T(8,128)S(1)}, f32[1,2,32,128]{3,2,0,1:T(8,128)}, u32[]{:S(2)}, u32[]{:S(2)}) collective-permute-start(f32[1,2,32,128]{3,2,0,1:T(8,128)S(1)} %get-tuple-element.316), channel_id=1, source_target_pairs={{0,8},{8,16},{16,24},{1,9},{9,17},{17,25},{2,10},{10,18},{18,26},{... | collective-permute-start | bytes 98312 | tf_op jit(solution)/shard_map/ppermute | solution.py:20
  51.2 169.5 %collective-permute-start.1 = (f32[1,2,32,128]{3,2,0,1:T(8,128)S(1)}, f32[1,2,32,128]{3,2,0,1:T(8,128)}, u32[]{:S(2)}, u32[]{:S(2)}) collective-permute-start(f32[1,2,32,128]{3,2,0,1:T(8,128)S(1)} %get-tuple-element.317), channel_id=1, source_target_pairs={{8,0},{16,8},{24,16},{9,1},{17,9},{25,17},{10,2},{18,10},{26,18},{... | collective-permute-start | bytes 98312 | tf_op jit(solution)/shard_map/ppermute | solution.py:23
  73.3 3.9 slice-start
  87.0 0.8 copy-start.3
  87.0 3.8 slice-start.1
  87.0 3.9 copy-start.1
  168.0 76.4 %copy-start.4 = (s32[4]{0:T(128)S(1)}, s32[4]{0:T(128)}, u32[]{:S(2)}) copy-start(s32[4]{0:T(128)} %and_select_fusion) | copy-start | bytes 52
  239.8 6.3 collective-permute-start.4
  244.8 5.6 collective-permute-start.5
  312.4 3.9 collective-permute-start.6
  314.9 5.6 collective-permute-start.7
  384.6 4.1 collective-permute-start.8
  387.2 5.6 collective-permute-start.9
  457.4 3.9 collective-permute-start.10
  459.9 5.6 collective-permute-start.11
  528.9 3.9 collective-permute-start.12
  531.5 5.6 collective-permute-start.13
  601.7 3.8 collective-permute-start.14
  604.2 5.6 collective-permute-start.15
where the time goes:
time: 661 us; the launch traced here: 655 us
  blocking collectives  396 us (60%)
  other arithmetic  140 us (21%)
  starting transfers between devices  35.1 us (5%)
  local copies, waits for them, and re-layouts  24.5 us (4%)
  waiting for transfers between devices  24.1 us (4%)
  between operations  22.8 us (3%)
  matrix products  12.1 us (2%)
    psum x6, blocking collectives, two_sums(): lax.psum((jnp.sum(residual_now * precond_now), jnp.sum(precond_now * imag...  238 us
    dynamic_update_slice x60, other arithmetic, column_step(): lax.scan(forward, start_carry, (-mixing_above, diagonal, -mixing, right_s...  101 us
    all_gather x8, blocking collectives, extend(): lax.all_gather(edge_cols, 'bx', axis=1, tiled=True)  76.9 us
    all_gather x8, blocking collectives, extend(): lax.all_gather(edge_rows, 'bx', axis=1, tiled=True)  68.8 us
    ppermute x8, starting transfers between devices, padded_2(): lax.ppermute(lax.slice_in_dim(block, block.shape[dim] - width, None, axis...  24.6 us
    ppermute x8, waiting for transfers between devices, padded_2(): lax.ppermute(lax.slice_in_dim(block, 0, width, axis=dim), axis, backward)  24.1 us
    add x1, other arithmetic, column_step(): right_side = advected + surface_row[:, :, None] * targets[None]  13.4 us
  transfers between devices with their start and end apart: 16, of which 6 were waited for; matrix products, arithmetic and copies ran while one was open for 22% of the time, Pallas kernels for 0%

commit v1 on v0

v1 whole, which is shorter than its diff:
```python
import functools

import jax
import jax.numpy as jnp
from jax import lax
from jax.experimental import pallas as pl
from jax.experimental.pallas import tpu as pltpu
from jax.sharding import PartitionSpec as P

ITERS = 6
RESTORE = 0.5
SURFACE = 0.1
FACE_SCALE = 2.0
SHIFTS = (0.0, 2.0, 1.0, 0.4, 1.6)
PIVOT_FLOOR = 1e-11
HALO = 8
LANES = 128
FIELDS = 4
CHUNK = 256
F32 = jnp.float32
VMEM = pl.BlockSpec(memory_space=pltpu.VMEM)
SMEM = pl.BlockSpec(memory_space=pltpu.SMEM)


def params(mebibytes):
    return pltpu.CompilerParams(vmem_limit_bytes=mebibytes * 2**20)


def columns_kernel(
    tracers, speed, mixing, wet, patch, *rest
):
    out, carry_in, carry_own, carry_up, carry_low, carry_high = rest[-6:]
    levels, blocks, count, width = tracers.shape
    wet_now = wet[...]
    shape = wet_now.shape
    zero = jnp.zeros(shape, F32)
    mix_above, up_above, down_above, inverse = zero, zero, zero, zero
    for k in range(levels):
        is_wet = (k < wet_now).astype(F32)
        is_open = (k + 1 < wet_now).astype(F32)
        flow = speed[k] * is_open
        up, down = jnp.maximum(flow, 0.0), jnp.minimum(flow, 0.0)
        mix = mixing[k] * is_open
        diagonal = 1.0 + mix + mix_above
        if k == 0:
            source = RESTORE * is_wet
            diagonal = diagonal + source
        inverse = 1.0 / (diagonal - mix_above * (mix_above * inverse))
        scaled_wet = is_wet * inverse
        carry_own[k] = scaled_wet * (1.0 + down - up_above)
        carry_up[k] = scaled_wet * up
        carry_low[k] = mix * inverse
        if k == 0:
            carry_in[k] = source * inverse
            carry_high[k] = zero
        else:
            carry_in[k] = mix_above * inverse
            carry_high[k] = scaled_wet * down_above
        mix_above, up_above, down_above = mix, up, down
    tracer_ids = lax.broadcasted_iota(jnp.int32, (count, width), 0)

    def row(ref, k, b):
        return jnp.broadcast_to(ref[k, b : b + 1, :], (count, width))

    for b in range(blocks):
        above = None
        here = tracers[0, b]
        value = None
        for k in range(levels):
            result = row(carry_own, k, b) * here
            if k + 1 < levels:
                below = tracers[k + 1, b]
                result = result + row(carry_up, k, b) * below
            if k == 0:
                target = (patch[b : b + 1, :] == tracer_ids).astype(F32)
                result = result + row(carry_in, k, b) * target
            else:
                result = result - row(carry_high, k, b) * above
                result = result + row(carry_in, k, b) * value
            value = result
            if k + 1 < levels:
                out[k, b] = value
                above, here = here, below
        out[levels - 1, b] = value
        for k in range(levels - 2, -1, -1):
            value = out[k, b] + row(carry_low, k, b) * value
            out[k, b] = value


def columns(tracers, speed, mixing, wet, patch, begin, end, previous):
    levels, blocks, count, cells = tracers.shape
    start = begin // CHUNK
    steps = (end - begin) // CHUNK
    wide = pl.BlockSpec((levels, blocks, count, CHUNK), lambda i: (0, 0, 0, i + start))
    flat = pl.BlockSpec((levels, blocks, CHUNK), lambda i: (0, 0, i + start))
    thin = pl.BlockSpec((blocks, CHUNK), lambda i: (0, i + start))
    in_specs = [wide, flat, flat, thin, thin]
    operands = [tracers, speed, mixing, wet, patch]
    aliases = {}
    if previous is not None:
        in_specs.append(pl.BlockSpec(memory_space=pl.ANY))
        operands.append(previous)
        aliases = {5: 0}
    part = steps * CHUNK * blocks * levels
    return pl.pallas_call(
        columns_kernel,
        grid=(steps,),
        in_specs=in_specs,
        out_specs=wide,
        out_shape=jax.ShapeDtypeStruct(tracers.shape, F32),
        scratch_shapes=[pltpu.VMEM((levels, blocks, CHUNK), F32)] * 5,
        input_output_aliases=aliases,
        compiler_params=params(32),
        cost_estimate=pl.CostEstimate(
            flops=part * count * 10, bytes_accessed=part * (count * 8 + 8), transcendentals=0
        ),
    )(*operands)


def payload_kernel(buoyancy, wet, prior, land, out):
    levels, blocks, cells = buoyancy.shape
    rows = cells // LANES
    wet_now = wet[...]
    total = jnp.zeros(wet_now.shape, F32)
    for k in range(levels):
        total = total + (k < wet_now).astype(F32) * buoyancy[k].astype(F32)
    depth = wet_now.astype(F32)
    first = prior[...]
    for r in range(rows):
        lanes = slice(r * LANES, (r + 1) * LANES)
        out[0, :, r, :] = total[:, lanes]
        out[1, :, r, :] = depth[:, lanes]
        out[2, :, r, :] = first[:, lanes]
    out[3] = land[...].astype(F32)


def payload_of(buoyancy, wet, prior, land):
    blocks, rows, lanes = land.shape
    return pl.pallas_call(
        payload_kernel,
        in_specs=[VMEM] * 4,
        out_specs=VMEM,
        out_shape=jax.ShapeDtypeStruct((FIELDS, blocks, rows, lanes), F32),
        compiler_params=params(16),
    )(buoyancy, wet, prior, land)


def select_kernel(spread, *refs):
    parts = refs[: len(spread)]
    clinic, tropic, place, own, to_south, to_north, band = refs[len(spread) :]
    blocks, rows = own.shape[1], own.shape[2]
    band_width = band.shape[1]
    band_row, column, band_rows = place[0], place[1], place[2]
    first_slot = band_row * band_width
    for part, (hop, ref) in enumerate(zip(spread, parts)):
        holder = (column ^ hop) * blocks
        for s in range(blocks):
            slot = first_slot + holder + s
            at = clinic[slot] - first_slot
            for f in range(FIELDS - 1):
                band[f, at] = ref[f, s]
            band[FIELDS - 1, tropic[slot] - first_slot] = ref[FIELDS - 1, s]

    lane = lax.broadcasted_iota(jnp.int32, (rows, LANES), 1)

    def sides(f, at, rows_from, rows_to):
        east = lax.rem(at + 1, band_width)
        west = lax.rem(at + band_width - 1, band_width)
        pick = lane[rows_from:rows_to]
        return jnp.where(
            pick < HALO,
            band[f, east, rows_from:rows_to],
            jnp.where(pick >= LANES - HALO, band[f, west, rows_from:rows_to], 0.0),
        )

    for i in range(blocks):
        at = tropic[first_slot + column * blocks + i] - first_slot
        for f in range(FIELDS):
            own[f, i, :, 0:LANES] = band[f, at]
            own[f, i, :, LANES : 2 * LANES] = sides(f, at, 0, rows)

    for out, move, rows_from in ((to_south, 1, rows - HALO), (to_north, -1, 0)):
        other = lax.rem(band_row + move + band_rows, band_rows) * band_width
        packed = [None] * FIELDS
        for i in range(blocks):
            at = tropic[other + column * blocks + i] - other
            for f in range(FIELDS):
                out[f, i] = band[f, at, rows_from : rows_from + HALO]
                beside = sides(f, at, rows_from, rows_from + HALO)
                if i:
                    beside = pltpu.roll(beside, 2 * HALO * i, 1)
                packed[f] = beside if i == 0 else packed[f] + beside
        for f in range(FIELDS):
            out[f, blocks] = packed[f]


def select(spread, parts, clinic, tropic, place, band_width):
    blocks, rows, lanes = parts[0].shape[1:]
    edge = jax.ShapeDtypeStruct((FIELDS, blocks + 1, HALO, lanes), F32)
    return pl.pallas_call(
        functools.partial(select_kernel, spread),
        in_specs=[VMEM] * len(parts) + [SMEM] * 3,
        out_specs=[VMEM] * 3,
        out_shape=[jax.ShapeDtypeStruct((FIELDS, blocks, rows, 2 * lanes), F32), edge, edge],
        scratch_shapes=[pltpu.VMEM((FIELDS, band_width, rows, lanes), F32)],
        compiler_params=params(16),
    )(*parts, clinic, tropic, place)


def two_sum(a, b):
    total = a + b
    part = total - a
    return total, (a - (total - part)) + (b - part)


def split(a):
    scaled = a * 4097.0
    high = scaled - (scaled - a)
    return high, a - high


def pair_add(a, b):
    high, low = two_sum(a[0], b[0])
    low = low + (a[1] + b[1])
    total = high + low
    return total, low - (total - high)


def product(a, b):
    value = a * b
    a_high, a_low = split(a)
    b_high, b_low = split(b)
    error = ((a_high * b_high - value) + a_high * b_low + a_low * b_high) + a_low * b_low
    return value, error


def pair_mul(a, b):
    value, error = product(a[0], b[0])
    error = error + (a[0] * b[1] + a[1] * b[0])
    total = value + error
    return total, error - (total - value)


def pair_inverse(a):
    guess = 1.0 / a[0]
    value, error = product(guess, a[0])
    rest = (1.0 - value) - error - guess * a[1]
    low = guess * rest
    total = guess + low
    return total, low - (total - guess)


def fold(pair, axis, steps):
    for step in steps:
        pair = pair_add(pair, tuple(pltpu.roll(part, step, axis) for part in pair))
    return pair


def basis_kernel(levels, own, north, south, vectors, guess, sums, images):
    blocks, rows = own.shape[1], own.shape[2]
    tall = rows + 2 * HALO
    inner = slice(HALO, HALO + rows)
    lane = lax.broadcasted_iota(jnp.int32, (HALO, LANES), 1)
    beside = (lane < HALO) | (lane >= LANES - HALO)

    def edge(ref, f, i):
        packed = ref[f, blocks]
        if i:
            packed = pltpu.roll(packed, LANES - 2 * HALO * i, 1)
        return jnp.concatenate([ref[f, i], jnp.where(beside, packed, 0.0)], axis=1)

    def east(v):
        return pltpu.roll(v, 2 * LANES - 1, 1)

    def west(v):
        return pltpu.roll(v, 1, 1)

    def below(v):
        return pltpu.roll(v, tall - 1, 0)

    def above(v):
        return pltpu.roll(v, 1, 0)

    for i in range(blocks):
        forcing, depth, prior, ocean = (
            jnp.concatenate([edge(north, f, i), own[f, i], edge(south, f, i)], axis=0)
            for f in range(FIELDS)
        )
        scale = FACE_SCALE / levels
        east_face = scale * jnp.minimum(depth, east(depth)) * ocean * east(ocean)
        west_face = west(east_face)
        south_face = scale * jnp.minimum(depth, below(depth)) * ocean * below(ocean)
        north_face = above(south_face)
        centre = SURFACE * ocean + (1.0 - ocean)
        diagonal = centre + east_face + west_face + south_face + north_face
        inverse = 1.0 / diagonal

        def operate(v):
            result = centre * v + east_face * (v - east(v))
            result = result + west_face * (v - west(v))
            result = result + south_face * (v - below(v))
            return result + north_face * (v - above(v))

        first = ocean * prior
        residual = ocean * forcing - operate(first)
        v = residual * inverse
        guess[i] = first[inner, 0:LANES]
        place = slice(i * rows, (i + 1) * rows)
        images[ITERS, place] = residual[inner, 0:LANES]
        for k in range(ITERS):
            image = operate(v)
            vectors[k, place] = v[inner, 0:LANES]
            images[k, place] = image[inner, 0:LANES]
            if k + 1 < ITERS:
                following = image * inverse
                v = following - SHIFTS[k] * v if SHIFTS[k] else following

    row_id = lax.broadcasted_iota(jnp.int32, (8, LANES), 0)
    lane_id = lax.broadcasted_iota(jnp.int32, (8, LANES), 1)
    entries = [(a, b) for a in range(ITERS) for b in range(a, ITERS + 1)]
    spots = [(8 * a + b, 8 * b + a if b < ITERS else -1) for a, b in entries]
    placed = None
    for begin in range(0, len(entries), 8):
        packed = (jnp.zeros((8, LANES), F32),) * 2
        spot = jnp.full((8, LANES), -1, jnp.int32)
        twin = jnp.full((8, LANES), -1, jnp.int32)
        for offset, (a, b) in enumerate(entries[begin : begin + 8]):
            total = error = None
            for r in range(0, blocks * rows, 8):
                value, rest = product(vectors[a, r : r + 8], images[b, r : r + 8])
                if total is None:
                    total, error = value, rest
                else:
                    total, extra = two_sum(total, value)
                    error = error + (rest + extra)
            pair = fold((total, error), 0, (4, 2, 1))
            mine = row_id == offset
            packed = tuple(jnp.where(mine, new, old) for new, old in zip(pair, packed))
            spot = jnp.where(mine, spots[begin + offset][0], spot)
            twin = jnp.where(mine, spots[begin + offset][1], twin)
        packed = fold(packed, 1, (64, 32, 16, 8, 4, 2, 1))
        high = jnp.where((lane_id == spot) | (lane_id == twin), packed[0], 0.0)
        low = jnp.where((lane_id == spot + 64) | ((lane_id == twin + 64) & (twin >= 0)), packed[1], 0.0)
        placed = high + low if placed is None else placed + high + low
    for step in (4, 2, 1):
        placed = placed + pltpu.roll(placed, step, 0)
    sums[...] = jnp.broadcast_to(placed[None], sums.shape)


def basis(levels, own, north, south, devices):
    fields, blocks, rows, _ = own.shape
    return pl.pallas_call(
        functools.partial(basis_kernel, levels),
        in_specs=[VMEM] * 3,
        out_specs=[VMEM] * 3,
        out_shape=[
            jax.ShapeDtypeStruct((ITERS, blocks * rows, LANES), F32),
            jax.ShapeDtypeStruct((blocks, rows, LANES), F32),
            jax.ShapeDtypeStruct((devices, 8, LANES), F32),
        ],
        scratch_shapes=[pltpu.VMEM((ITERS + 1, blocks * rows, LANES), F32)],
        compiler_params=params(16),
    )(own, north, south)


def finish_kernel(sums, vectors, guess, out):
    devices = sums.shape[0]
    blocks, rows = guess.shape[0], guess.shape[1]
    pairs = [(sums[d], jnp.zeros((8, LANES), F32)) for d in range(devices)]
    while len(pairs) > 1:
        pairs = [pair_add(pairs[j], pairs[j + 1]) for j in range(0, len(pairs), 2)]
    total, error = pairs[0]
    low = error + pltpu.roll(total, 64, 1)
    row_id = lax.broadcasted_iota(jnp.int32, (8, LANES), 0)
    lane_id = lax.broadcasted_iota(jnp.int32, (8, LANES), 1)
    keep = (row_id < ITERS) & (lane_id < ITERS + 1)

    def rows_of(vector):
        moved = vector
        for i in range(1, ITERS):
            moved = jnp.where(row_id == i, pltpu.roll(vector, LANES - 8 * i, 1), moved)
        return jnp.where(keep, moved, 0.0)

    matrix = (rows_of(total), rows_of(low))
    energy = matrix[0]
    for k in range(ITERS):
        column = tuple(jnp.broadcast_to(part[:, k : k + 1], (8, LANES)) for part in matrix)
        pivot_row = tuple(jnp.broadcast_to(part[k : k + 1, :], (8, LANES)) for part in matrix)
        pivot = tuple(jnp.broadcast_to(part[k : k + 1, :], (8, LANES)) for part in column)
        full = jnp.broadcast_to(energy[k : k + 1, k : k + 1], (8, LANES))
        good = pivot[0] > PIVOT_FLOOR * full
        safe = (jnp.where(good, pivot[0], 1.0), jnp.where(good, pivot[1], 0.0))
        inverse = tuple(jnp.where(good, part, 0.0) for part in pair_inverse(safe))
        scaled = pair_mul(pivot_row, inverse)
        change = pair_mul(column, scaled)
        moved = pair_add(matrix, (-change[0], -change[1]))
        matrix = tuple(
            jnp.where(row_id == k, new, jnp.where(keep, old, 0.0)) for new, old in zip(scaled, moved)
        )
    weights = matrix[0]
    result = guess[...]
    for k in range(ITERS):
        weight = jnp.broadcast_to(weights[k : k + 1, ITERS : ITERS + 1], (rows, LANES))
        result = result + weight[None] * vectors[k].reshape(blocks, rows, LANES)
    out[...] = result


def finish(sums, vectors, guess):
    return pl.pallas_call(
        finish_kernel,
        in_specs=[VMEM] * 3,
        out_specs=VMEM,
        out_shape=jax.ShapeDtypeStruct(guess.shape, F32),
        compiler_params=params(16),
    )(sums, vectors, guess)


def swap(array, axis, hop):
    count = lax.axis_size(axis)
    return lax.ppermute(array, axis, [(i, i ^ hop) for i in range(count)])


def local(
    tracers,
    vertical_speed,
    diffusivity,
    buoyancy_force,
    wet_levels,
    surface_patch,
    prior_height,
    land_mask,
    baroclinic_map,
    barotropic_map,
):
    levels, blocks, _, cells = tracers.shape
    band_rows, holders = lax.axis_size("by"), lax.axis_size("bx")
    place = jnp.stack(
        [lax.axis_index("by"), lax.axis_index("bx"), jnp.int32(band_rows)]
    ).astype(jnp.int32)

    payload = payload_of(buoyancy_force, wet_levels, prior_height, land_mask)
    spread = list(range(0, holders, 2))
    parts = [payload] + [swap(payload, "bx", hop) for hop in spread[1:]]
    parts = parts + [swap(part, "bx", 1) for part in parts]
    spread = spread + [hop + 1 for hop in spread]

    own, to_south, to_north = select(
        tuple(spread), parts, baroclinic_map, barotropic_map, place, holders * blocks
    )
    north = lax.ppermute(to_south, "by", [(i, i + 1) for i in range(band_rows - 1)])
    south = lax.ppermute(to_north, "by", [(i + 1, i) for i in range(band_rows - 1)])

    half = cells // 2
    stepped = columns(
        tracers, vertical_speed, diffusivity, wet_levels, surface_patch, 0, half, None
    )
    stepped = columns(
        tracers, vertical_speed, diffusivity, wet_levels, surface_patch, half, cells, stepped
    )

    vectors, guess, sums = basis(levels, own, north, south, band_rows * holders)
    gathered = lax.all_to_all(sums, ("by", "bx"), 0, 0, tiled=True)
    return stepped, finish(gathered, vectors, guess)


def solution(mesh):
    slots = ("by", "bx")
    return jax.shard_map(
        local,
        mesh=mesh,
        in_specs=(
            P(None, slots, None, None),
            P(None, slots, None),
            P(None, slots, None),
            P(None, slots, None),
            P(slots, None),
            P(slots, None),
            P(slots, None),
            P(slots, None, None),
            P(),
            P(),
        ),
        out_specs=(P(None, slots, None, None), P(slots, None, None)),
        check_vma=False,
    )
```

time: 661 us -> 53.3 us (0.08)
  blocking collectives: 396 us -> 0 us
  other arithmetic: 140 us -> 0.08 us
  between operations: 22.8 us -> 0.7 us
  starting transfers between devices: 35.1 us -> 13.7 us
  Pallas kernels: 0 us -> 13.7 us
  local copies, waits for them, and re-layouts: 24.5 us -> 12.2 us
  matrix products: 12.1 us -> 0 us
  waiting for transfers between devices: 24.1 us -> 12.2 us
    psum x6 -> x0, blocking collectives: 238 us -> none  [two_sums(): lax.psum((jnp.sum(residual_now * precond_now), jnp.sum(precond_now * imag...]
    all_gather x17 -> x0, blocking collectives: 158 us -> none  [the longest x8 76.9 us: extend(): lax.all_gather(edge_cols, 'bx', axis=1, tiled=True)]
    dynamic_update_slice x60 -> x0, other arithmetic: 101 us -> none  [column_step(): lax.scan(forward, start_carry, (-mixing_above, diagonal, -mixing, right_s...]
    ppermute x16 -> x9, starting transfers between devices: 35.1 us -> 9.84 us  [the longest x7 5.06 us: swap(): return lax.ppermute(array, axis, [(i, i ^ hop) for i in range(count)])]
    add x4 -> x0, other arithmetic: 23.9 us -> none  [the longest x1 13.4 us: column_step(): right_side = advected + surface_row[:, :, None] * targets[None]]
    pallas_call x0 -> x6, Pallas kernels: none -> 13.7 us  [the longest x2 8.27 us: columns(): pl.pallas_call(columns_kernel, grid=(steps,), in_specs=in_specs, out_spec...]
    dot_general x41 -> x0, matrix products: 12.1 us -> none  [the longest x8 2.95 us: extend(): jnp.einsum('jc,qcw->qjw', my_pick, beside[0], precision=PRECISE)]
    ppermute x16 -> x9, waiting for transfers between devices: 24.1 us -> 12.2 us  [the longest x7 7.17 us: swap(): return lax.ppermute(array, axis, [(i, i ^ hop) for i in range(count)])]
  transfers between devices with their start and end apart: 16 -> 10, of which waited for: 6 -> 6; matrix products, arithmetic and copies ran while one was open for 22% -> 0% of each run, Pallas kernels for 0% -> 16%
where the time goes in v1:
time: 53.3 us; the launch traced here: 52.6 us
  Pallas kernels  13.7 us (26%)
  starting transfers between devices  13.7 us (26%)
  local copies, waits for them, and re-layouts  12.2 us (23%)
  waiting for transfers between devices  12.2 us (23%)
  between operations  0.7 us (1%)
    unnamed x22, local copies, waits for them, and re-layouts  12.2 us
    pallas_call x2, Pallas kernels, columns(): pl.pallas_call(columns_kernel, grid=(steps,), in_specs=in_specs, out_spec...  8.27 us
    ppermute x7, waiting for transfers between devices, swap(): return lax.ppermute(array, axis, [(i, i ^ hop) for i in range(count)])  7.17 us
    ppermute x7, starting transfers between devices, swap(): return lax.ppermute(array, axis, [(i, i ^ hop) for i in range(count)])  5.06 us
    ppermute x1, waiting for transfers between devices, local(): lax.ppermute(to_north, 'by', [(i + 1, i) for i in range(band_rows - 1)])  4.16 us
    all_to_all x1, starting transfers between devices, local(): gathered = lax.all_to_all(sums, ('by', 'bx'), 0, 0, tiled=True)  3.9 us
    ppermute x1, starting transfers between devices, local(): lax.ppermute(to_south, 'by', [(i, i + 1) for i in range(band_rows - 1)])  3.48 us
    pallas_call x1, Pallas kernels, basis(): pl.pallas_call(functools.partial(basis_kernel, levels), in_specs=[VMEM] *...  2.66 us
  transfers between devices with their start and end apart: 10, of which 6 were waited for; matrix products, arithmetic and copies ran while one was open for 0% of the time, Pallas kernels for 16%

profile of v1, /device:TPU:0, one launch (start us, length us, event | category | flops | bytes accessed | tf_op | source)
XLA Modules:
  0.0 52.6 jit_solution(13232404819101044898)
XLA Ops:
  0.6 1.0 %copy-done.3 = bf16[20,4,2048]{2,1,0:T(4,128)(2,1)S(1)} copy-done((bf16[20,4,2048]{2,1,0:T(4,128)(2,1)S(1)}, bf16[20,4,2048]{2,1,0:T(4,128)(2,1)}, u32[]{:S(2)}) %copy-start.3) | copy-done | bytes 327704
  1.6 0.8 %copy-done.4 = s32[4,2048]{1,0:T(4,128)S(1)} copy-done((s32[4,2048]{1,0:T(4,128)S(1)}, s32[4,2048]{1,0:T(4,128)}, u32[]{:S(2)}) %copy-start.4) | copy-done | bytes 32792
  2.4 0.8 %copy-done.7 = f32[4,2048]{1,0:T(4,128)S(1)} copy-done((f32[4,2048]{1,0:T(4,128)S(1)}, f32[4,2048]{1,0:T(4,128)}, u32[]{:S(2)}) %copy-start.7) | copy-done | bytes 32792
  3.1 0.8 %copy-done.8 = s32[4,16,128]{2,1,0:T(8,128)S(1)} copy-done((s32[4,16,128]{2,1,0:T(8,128)S(1)}, s32[4,16,128]{2,1,0:T(8,128)}, u32[]{:S(2)}) %copy-start.8) | copy-done | bytes 32792
  4.0 3.0 %collective-permute-start = (f32[4,4,16,128]{3,2,1,0:T(8,128)S(1)}, f32[4,4,16,128]{3,2,1,0:T(8,128)S(1)}, u32[]{:S(2)}, u32[]{:S(2)}) collective-permute-start(f32[4,4,16,128]{3,2,1,0:T(8,128)S(1)} %shard_map.115.refs_0_), channel_id=1, source_target_pairs={{0,2},{1,3},{2,0},{3,1},{4,6},{5,7},{6,4},{7,5},{8,10},{9,11},{10,... | collective-permute-start | bytes 393224 | tf_op jit(solution)/shard_map/ppermute | solution.py:420
  7.0 1.5 %collective-permute-start.1 = (f32[4,4,16,128]{3,2,1,0:T(8,128)S(1)}, f32[4,4,16,128]{3,2,1,0:T(8,128)S(1)}, u32[]{:S(2)}, u32[]{:S(2)}) collective-permute-start(f32[4,4,16,128]{3,2,1,0:T(8,128)S(1)} %shard_map.115.refs_0_), channel_id=1, source_target_pairs={{0,4},{1,5},{2,6},{3,7},{4,0},{5,1},{6,2},{7,3},{8,12},{9,13},{10,... | collective-permute-start | bytes 393224 | tf_op jit(solution)/shard_map/ppermute | solution.py:420
  8.6 2.4 %collective-permute-done.refs_1_ = f32[4,4,16,128]{3,2,1,0:T(8,128)S(1)} collective-permute-done((f32[4,4,16,128]{3,2,1,0:T(8,128)S(1)}, f32[4,4,16,128]{3,2,1,0:T(8,128)S(1)}, u32[]{:S(2)}, u32[]{:S(2)}) %collective-permute-start) | collective-permute-done | bytes 131104 | tf_op jit(solution)/shard_map/ppermute | solution.py:420
  10.9 3.9 %collective-permute-done.1.refs_2_ = f32[4,4,16,128]{3,2,1,0:T(8,128)S(1)} collective-permute-done((f32[4,4,16,128]{3,2,1,0:T(8,128)S(1)}, f32[4,4,16,128]{3,2,1,0:T(8,128)S(1)}, u32[]{:S(2)}, u32[]{:S(2)}) %collective-permute-start.1) | collective-permute-done | bytes 131104 | tf_op jit(solution)/shard_map/ppermute | solution.py:420
  15.4 0.8 %collective-permute-done.5.refs_6_ = f32[4,4,16,128]{3,2,1,0:T(8,128)S(1)} collective-permute-done((f32[4,4,16,128]{3,2,1,0:T(8,128)S(1)}, f32[4,4,16,128]{3,2,1,0:T(8,128)S(1)}, u32[]{:S(2)}, u32[]{:S(2)}) %collective-permute-start.5) | collective-permute-done | bytes 131104 | tf_op jit(solution)/shard_map/ppermute | solution.py:420
  17.7 0.8 %shard_map.116 = (f32[4,4,16,256]{3,2,1,0:T(8,128)S(1)}, f32[4,5,8,128]{3,2,1,0:T(8,128)S(1)}, f32[4,5,8,128]{3,2,1,0:T(8,128)S(1)}) custom-call(f32[4,4,16,128]{3,2,1,0:T(8,128)S(1)} %shard_map.115.refs_0_, f32[4,4,16,128]{3,2,1,0:T(8,128)S(1)} %collective-permute-done.refs_1_, f32[4,4,16,128]{3,2,1,0:T(8,128)S(1)} %collective-permute-done.1.refs_2_, ...), custom_call_target="tpu_custom_call" | custom-call | tf_op jit(solution)/shard_map/pallas_call | solution.py:200
  18.5 3.5 %collective-permute-start.7 = (f32[4,5,8,128]{3,2,1,0:T(8,128)S(1)}, f32[4,5,8,128]{3,2,1,0:T(8,128)S(1)}, u32[]{:S(2)}, u32[]{:S(2)}) collective-permute-start(f32[4,5,8,128]{3,2,1,0:T(8,128)S(1)} %get-tuple-element.9), channel_id=1, source_target_pairs={{0,8},{8,16},{16,24},{1,9},{9,17},{17,25},{2,10},{10,18},{18,26},{... | collective-permute-start | bytes 245768 | tf_op jit(solution)/shard_map/ppermute | solution.py:450
  21.9 1.3 %collective-permute-start.8 = (f32[4,5,8,128]{3,2,1,0:T(8,128)S(1)}, f32[4,5,8,128]{3,2,1,0:T(8,128)S(1)}, u32[]{:S(2)}, u32[]{:S(2)}) collective-permute-start(f32[4,5,8,128]{3,2,1,0:T(8,128)S(1)} %get-tuple-element.10), channel_id=1, source_target_pairs={{8,0},{16,8},{24,16},{9,1},{17,9},{25,17},{10,2},{18,10},{26,18},{... | collective-permute-start | bytes 245768 | tf_op jit(solution)/shard_map/ppermute | solution.py:451
  23.2 0.9 %collective-permute-done.7.north = f32[4,5,8,128]{3,2,1,0:T(8,128)S(1)} collective-permute-done((f32[4,5,8,128]{3,2,1,0:T(8,128)S(1)}, f32[4,5,8,128]{3,2,1,0:T(8,128)S(1)}, u32[]{:S(2)}, u32[]{:S(2)}) %collective-permute-start.7) | collective-permute-done | bytes 81952 | tf_op jit(solution)/shard_map/ppermute | solution.py:450
  24.1 4.2 %collective-permute-done.8.south = f32[4,5,8,128]{3,2,1,0:T(8,128)S(1)} collective-permute-done((f32[4,5,8,128]{3,2,1,0:T(8,128)S(1)}, f32[4,5,8,128]{3,2,1,0:T(8,128)S(1)}, u32[]{:S(2)}, u32[]{:S(2)}) %collective-permute-start.8) | collective-permute-done | bytes 81952 | tf_op jit(solution)/shard_map/ppermute | solution.py:451
  28.3 2.7 %shard_map.117 = (f32[6,64,128]{2,1,0:T(8,128)S(1)}, f32[4,16,128]{2,1,0:T(8,128)S(1)}, f32[32,8,128]{2,1,0:T(8,128)}) custom-call(f32[4,4,16,256]{3,2,1,0:T(8,128)S(1)} %get-tuple-element.8.own, f32[4,5,8,128]{3,2,1,0:T(8,128)S(1)} %collective-permute-done.7.north, f32[4,5,8,128]{3,2,1,0:T(8,128)S(1)} %collective-permute-done.8.south), custom_call_target="tpu_custom_call" | custom-call | tf_op jit(solution)/shard_map/pallas_call | solution.py:352
  30.9 3.9 %all-to-all-start = ((f32[32,8,128]{2,1,0:T(8,128)}), f32[32,8,128]{2,1,0:T(8,128)S(1)}, u32[]{:S(2)}, u32[]{:S(2)}) async-start(f32[32,8,128]{2,1,0:T(8,128)} %get-tuple-element.11), calls=%async_computation | async-start | bytes 262144 | tf_op jit(solution)/shard_map/all_to_all | solution.py:462
  34.9 4.0 %copy-done = f32[20,4,16,2048]{3,2,1,0:T(8,128)S(1)} copy-done((f32[20,4,16,2048]{3,2,1,0:T(8,128)S(1)}, f32[20,4,16,2048]{3,2,1,0:T(8,128)}, u32[]{:S(2)}) %copy-start) | copy-done | bytes 10485784
  38.8 1.1 %copy-done.1 = f32[20,4,2048]{2,1,0:T(4,128)S(1)} copy-done((f32[20,4,2048]{2,1,0:T(4,128)S(1)}, f32[20,4,2048]{2,1,0:T(4,128)}, u32[]{:S(2)}) %copy-start.1) | copy-done | bytes 655384
  39.9 1.1 %copy-done.2 = f32[20,4,2048]{2,1,0:T(4,128)S(1)} copy-done((f32[20,4,2048]{2,1,0:T(4,128)S(1)}, f32[20,4,2048]{2,1,0:T(4,128)}, u32[]{:S(2)}) %copy-start.2) | copy-done | bytes 655384
  41.0 0.8 %copy-done.5 = s32[4,2048]{1,0:T(4,128)S(1)} copy-done((s32[4,2048]{1,0:T(4,128)S(1)}, s32[4,2048]{1,0:T(4,128)}, u32[]{:S(2)}) %copy-start.5) | copy-done | bytes 32792
  41.8 0.8 %copy-done.6 = s32[4,2048]{1,0:T(4,128)S(1)} copy-done((s32[4,2048]{1,0:T(4,128)S(1)}, s32[4,2048]{1,0:T(4,128)}, u32[]{:S(2)}) %copy-start.6) | copy-done | bytes 32792
  42.5 4.1 %shard_map.113.rest_0_ = f32[20,4,16,2048]{3,2,1,0:T(8,128)} custom-call(f32[20,4,16,2048]{3,2,1,0:T(8,128)S(1)} %copy-done, f32[20,4,2048]{2,1,0:T(4,128)S(1)} %copy-done.1, f32[20,4,2048]{2,1,0:T(4,128)S(1)} %copy-done.2, s32[4,2048]{1,0:T(4,128)S(1)} %copy-done.5, s32[4,2048]{1,0:T(4,128)S(1)} %copy-done.6), custom_call_target="tpu_custom_call" | custom-call | flops 13107200 | bytes 11141120 | tf_op jit(solution)/shard_map/pallas_call | solution.py:105
  46.7 4.1 %shard_map.114 = f32[20,4,16,2048]{3,2,1,0:T(8,128)} custom-call(f32[20,4,16,2048]{3,2,1,0:T(8,128)S(1)} %copy-done, f32[20,4,2048]{2,1,0:T(4,128)S(1)} %copy-done.1, f32[20,4,2048]{2,1,0:T(4,128)S(1)} %copy-done.2, s32[4,2048]{1,0:T(4,128)S(1)} %copy-done.5, s32[4,2048]{1,0:T(4,128)S(1)} %copy-done.6, ...), custom_call_target="tpu_custom_call", output_to_operand_aliasing={{}: (5, {})} | custom-call | flops 13107200 | bytes 11141120 | tf_op jit(solution)/shard_map/pallas_call | solution.py:105
  50.8 1.8 %shard_map.118 = f32[4,16,128]{2,1,0:T(8,128)} custom-call(f32[32,8,128]{2,1,0:T(8,128)S(1)} %all-to-all-done.sums, f32[6,64,128]{2,1,0:T(8,128)S(1)} %get-tuple-element.12.vectors, f32[4,16,128]{2,1,0:T(8,128)S(1)} %get-tuple-element.13.guess), custom_call_target="tpu_custom_call" | custom-call | tf_op jit(solution)/shard_map/pallas_call | solution.py:409
  (25 shorter events, 2.3 us)
Async XLA Ops:
  0.6 1.0 %copy-start.3 = (bf16[20,4,2048]{2,1,0:T(4,128)(2,1)S(1)}, bf16[20,4,2048]{2,1,0:T(4,128)(2,1)}, u32[]{:S(2)}) copy-start(bf16[20,4,2048]{2,1,0:T(4,128)(2,1)} %buoyancy.1) | copy-start | bytes 983044
  1.6 0.8 %copy-start.4 = (s32[4,2048]{1,0:T(4,128)S(1)}, s32[4,2048]{1,0:T(4,128)}, u32[]{:S(2)}) copy-start(s32[4,2048]{1,0:T(4,128)} %wet.5) | copy-start | bytes 98308
  2.4 0.8 %copy-start.7 = (f32[4,2048]{1,0:T(4,128)S(1)}, f32[4,2048]{1,0:T(4,128)}, u32[]{:S(2)}) copy-start(f32[4,2048]{1,0:T(4,128)} %prior.1) | copy-start | bytes 98308
  3.1 0.8 %copy-start.8 = (s32[4,16,128]{2,1,0:T(8,128)S(1)}, s32[4,16,128]{2,1,0:T(8,128)}, u32[]{:S(2)}) copy-start(s32[4,16,128]{2,1,0:T(8,128)} %land.1) | copy-start | bytes 98308
  4.0 6.9 %collective-permute-start = (f32[4,4,16,128]{3,2,1,0:T(8,128)S(1)}, f32[4,4,16,128]{3,2,1,0:T(8,128)S(1)}, u32[]{:S(2)}, u32[]{:S(2)}) collective-permute-start(f32[4,4,16,128]{3,2,1,0:T(8,128)S(1)} %shard_map.115.refs_0_), channel_id=1, source_target_pairs={{0,2},{1,3},{2,0},{3,1},{4,6},{5,7},{6,4},{7,5},{8,10},{9,11},{10,... | collective-permute-start | bytes 393224 | tf_op jit(solution)/shard_map/ppermute | solution.py:420
  7.0 7.8 %collective-permute-start.1 = (f32[4,4,16,128]{3,2,1,0:T(8,128)S(1)}, f32[4,4,16,128]{3,2,1,0:T(8,128)S(1)}, u32[]{:S(2)}, u32[]{:S(2)}) collective-permute-start(f32[4,4,16,128]{3,2,1,0:T(8,128)S(1)} %shard_map.115.refs_0_), channel_id=1, source_target_pairs={{0,4},{1,5},{2,6},{3,7},{4,0},{5,1},{6,2},{7,3},{8,12},{9,13},{10,... | collective-permute-start | bytes 393224 | tf_op jit(solution)/shard_map/ppermute | solution.py:420
  8.6 6.3 %collective-permute-start.2 = (f32[4,4,16,128]{3,2,1,0:T(8,128)S(1)}, f32[4,4,16,128]{3,2,1,0:T(8,128)S(1)}, u32[]{:S(2)}, u32[]{:S(2)}) collective-permute-start(f32[4,4,16,128]{3,2,1,0:T(8,128)S(1)} %shard_map.115.refs_0_), channel_id=1, source_target_pairs={{0,6},{1,7},{2,4},{3,5},{4,2},{5,3},{6,0},{7,1},{8,14},{9,15},{10,... | collective-permute-start | bytes 393224 | tf_op jit(solution)/shard_map/ppermute | solution.py:420
  8.6 6.8 %collective-permute-start.3 = (f32[4,4,16,128]{3,2,1,0:T(8,128)S(1)}, f32[4,4,16,128]{3,2,1,0:T(8,128)S(1)}, u32[]{:S(2)}, u32[]{:S(2)}) collective-permute-start(f32[4,4,16,128]{3,2,1,0:T(8,128)S(1)} %shard_map.115.refs_0_), channel_id=1, source_target_pairs={{0,1},{1,0},{2,3},{3,2},{4,5},{5,4},{6,7},{7,6},{8,9},{9,8},{10,11... | collective-permute-start | bytes 393224 | tf_op jit(solution)/shard_map/ppermute | solution.py:420
  10.9 4.5 %collective-permute-start.4 = (f32[4,4,16,128]{3,2,1,0:T(8,128)S(1)}, f32[4,4,16,128]{3,2,1,0:T(8,128)S(1)}, u32[]{:S(2)}, u32[]{:S(2)}) collective-permute-start(f32[4,4,16,128]{3,2,1,0:T(8,128)S(1)} %collective-permute-done.refs_1_), channel_id=1, source_target_pairs={{0,1},{1,0},{2,3},{3,2},{4,5},{5,4},{6,7},{7,6},{8,9},{9,8},{10,11... | collective-permute-start | bytes 393224 | tf_op jit(solution)/shard_map/ppermute | solution.py:420
  14.8 1.3 %collective-permute-start.5 = (f32[4,4,16,128]{3,2,1,0:T(8,128)S(1)}, f32[4,4,16,128]{3,2,1,0:T(8,128)S(1)}, u32[]{:S(2)}, u32[]{:S(2)}) collective-permute-start(f32[4,4,16,128]{3,2,1,0:T(8,128)S(1)} %collective-permute-done.1.refs_2_), channel_id=1, source_target_pairs={{0,1},{1,0},{2,3},{3,2},{4,5},{5,4},{6,7},{7,6},{8,9},{9,8},{10,11... | collective-permute-start | bytes 393224 | tf_op jit(solution)/shard_map/ppermute | solution.py:420
  14.8 1.5 %collective-permute-start.6 = (f32[4,4,16,128]{3,2,1,0:T(8,128)S(1)}, f32[4,4,16,128]{3,2,1,0:T(8,128)S(1)}, u32[]{:S(2)}, u32[]{:S(2)}) collective-permute-start(f32[4,4,16,128]{3,2,1,0:T(8,128)S(1)} %collective-permute-done.2.refs_3_), channel_id=1, source_target_pairs={{0,1},{1,0},{2,3},{3,2},{4,5},{5,4},{6,7},{7,6},{8,9},{9,8},{10,11... | collective-permute-start | bytes 393224 | tf_op jit(solution)/shard_map/ppermute | solution.py:420
  16.3 0.7 %copy-start.9 = (s32[128]{0:T(128)S(1)}, s32[128]{0:T(128)}, u32[]{:S(2)}) copy-start(s32[128]{0:T(128)} %refs_8_.1) | copy-start | bytes 1540
  17.0 0.7 %copy-start.10 = (s32[128]{0:T(128)S(1)}, s32[128]{0:T(128)}, u32[]{:S(2)}) copy-start(s32[128]{0:T(128)} %refs_9_.1) | copy-start | bytes 1540
  18.5 5.7 %collective-permute-start.7 = (f32[4,5,8,128]{3,2,1,0:T(8,128)S(1)}, f32[4,5,8,128]{3,2,1,0:T(8,128)S(1)}, u32[]{:S(2)}, u32[]{:S(2)}) collective-permute-start(f32[4,5,8,128]{3,2,1,0:T(8,128)S(1)} %get-tuple-element.9), channel_id=1, source_target_pairs={{0,8},{8,16},{16,24},{1,9},{9,17},{17,25},{2,10},{10,18},{18,26},{... | collective-permute-start | bytes 245768 | tf_op jit(solution)/shard_map/ppermute | solution.py:450
  21.9 6.3 %collective-permute-start.8 = (f32[4,5,8,128]{3,2,1,0:T(8,128)S(1)}, f32[4,5,8,128]{3,2,1,0:T(8,128)S(1)}, u32[]{:S(2)}, u32[]{:S(2)}) collective-permute-start(f32[4,5,8,128]{3,2,1,0:T(8,128)S(1)} %get-tuple-element.10), channel_id=1, source_target_pairs={{8,0},{16,8},{24,16},{9,1},{17,9},{25,17},{10,2},{18,10},{26,18},{... | collective-permute-start | bytes 245768 | tf_op jit(solution)/shard_map/ppermute | solution.py:451
  30.9 19.9 %all-to-all-start = ((f32[32,8,128]{2,1,0:T(8,128)}), f32[32,8,128]{2,1,0:T(8,128)S(1)}, u32[]{:S(2)}, u32[]{:S(2)}) async-start(f32[32,8,128]{2,1,0:T(8,128)} %get-tuple-element.11), calls=%async_computation | async-start | bytes 262144 | tf_op jit(solution)/shard_map/all_to_all | solution.py:462
  34.9 4.0 %copy-start = (f32[20,4,16,2048]{3,2,1,0:T(8,128)S(1)}, f32[20,4,16,2048]{3,2,1,0:T(8,128)}, u32[]{:S(2)}) copy-start(f32[20,4,16,2048]{3,2,1,0:T(8,128)} %tracers.3) | copy-start | bytes 31457284
  38.8 1.1 %copy-start.1 = (f32[20,4,2048]{2,1,0:T(4,128)S(1)}, f32[20,4,2048]{2,1,0:T(4,128)}, u32[]{:S(2)}) copy-start(f32[20,4,2048]{2,1,0:T(4,128)} %speed.3) | copy-start | bytes 1966084
  39.9 1.1 %copy-start.2 = (f32[20,4,2048]{2,1,0:T(4,128)S(1)}, f32[20,4,2048]{2,1,0:T(4,128)}, u32[]{:S(2)}) copy-start(f32[20,4,2048]{2,1,0:T(4,128)} %mixing.3) | copy-start | bytes 1966084
  41.0 0.8 %copy-start.5 = (s32[4,2048]{1,0:T(4,128)S(1)}, s32[4,2048]{1,0:T(4,128)}, u32[]{:S(2)}) copy-start(s32[4,2048]{1,0:T(4,128)} %wet.5) | copy-start | bytes 98308
  41.8 0.8 %copy-start.6 = (s32[4,2048]{1,0:T(4,128)S(1)}, s32[4,2048]{1,0:T(4,128)}, u32[]{:S(2)}) copy-start(s32[4,2048]{1,0:T(4,128)} %patch.3) | copy-start | bytes 98308

commit v2 on v1

--- a/solution.py
+++ b/solution.py
@@ -16,31 +16,38 @@
 HALO = 8
 LANES = 128
 FIELDS = 4
-CHUNK = 256
+CHUNK = 512
+EARLY = 4
 F32 = jnp.float32
 VMEM = pl.BlockSpec(memory_space=pltpu.VMEM)
 SMEM = pl.BlockSpec(memory_space=pltpu.SMEM)
+HBM = pl.BlockSpec(memory_space=pltpu.HBM)
+
+
+def in_hbm(*arrays):
+    return [pltpu.with_memory_space_constraint(array, pltpu.HBM) for array in arrays]
 
 
 def params(mebibytes):
     return pltpu.CompilerParams(vmem_limit_bytes=mebibytes * 2**20)
 
 
-def columns_kernel(
-    tracers, speed, mixing, wet, patch, *rest
-):
-    out, carry_in, carry_own, carry_up, carry_low, carry_high = rest[-6:]
+def columns_step(tracers, speed, mixing, wet, patch, out, carry_in, carry_own, carry_up, carry_low, carry_high):
     levels, blocks, count, width = tracers.shape
-    wet_now = wet[...]
-    shape = wet_now.shape
-    zero = jnp.zeros(shape, F32)
+    tiles = width // LANES
+
+    def stacked(block):
+        return jnp.concatenate([block[:, t * LANES : (t + 1) * LANES] for t in range(tiles)], axis=0)
+
+    wet_now = stacked(wet[...])
+    zero = jnp.zeros(wet_now.shape, F32)
     mix_above, up_above, down_above, inverse = zero, zero, zero, zero
     for k in range(levels):
         is_wet = (k < wet_now).astype(F32)
         is_open = (k + 1 < wet_now).astype(F32)
-        flow = speed[k] * is_open
+        flow = stacked(speed[k]) * is_open
         up, down = jnp.maximum(flow, 0.0), jnp.minimum(flow, 0.0)
-        mix = mixing[k] * is_open
+        mix = stacked(mixing[k]) * is_open
         diagonal = 1.0 + mix + mix_above
         if k == 0:
             source = RESTORE * is_wet
@@ -57,58 +64,75 @@
             carry_in[k] = mix_above * inverse
             carry_high[k] = scaled_wet * down_above
         mix_above, up_above, down_above = mix, up, down
-    tracer_ids = lax.broadcasted_iota(jnp.int32, (count, width), 0)
-
-    def row(ref, k, b):
-        return jnp.broadcast_to(ref[k, b : b + 1, :], (count, width))
+    tracer_ids = lax.broadcasted_iota(jnp.int32, (count, LANES), 0)
 
     for b in range(blocks):
-        above = None
-        here = tracers[0, b]
-        value = None
-        for k in range(levels):
-            result = row(carry_own, k, b) * here
-            if k + 1 < levels:
-                below = tracers[k + 1, b]
-                result = result + row(carry_up, k, b) * below
-            if k == 0:
-                target = (patch[b : b + 1, :] == tracer_ids).astype(F32)
-                result = result + row(carry_in, k, b) * target
-            else:
-                result = result - row(carry_high, k, b) * above
-                result = result + row(carry_in, k, b) * value
-            value = result
-            if k + 1 < levels:
-                out[k, b] = value
-                above, here = here, below
-        out[levels - 1, b] = value
-        for k in range(levels - 2, -1, -1):
-            value = out[k, b] + row(carry_low, k, b) * value
-            out[k, b] = value
-
-
-def columns(tracers, speed, mixing, wet, patch, begin, end, previous):
-    levels, blocks, count, cells = tracers.shape
-    start = begin // CHUNK
-    steps = (end - begin) // CHUNK
+        for t in range(tiles):
+            lanes = slice(t * LANES, (t + 1) * LANES)
+            at = t * blocks + b
+
+            def row(ref, k):
+                return jnp.broadcast_to(ref[k, at : at + 1, :], (count, LANES))
+
+            above = value = None
+            here = tracers[0, b, :, lanes]
+            for k in range(levels):
+                result = row(carry_own, k) * here
+                if k + 1 < levels:
+                    below = tracers[k + 1, b, :, lanes]
+                    result = result + row(carry_up, k) * below
+                if k == 0:
+                    target = (patch[b : b + 1, lanes] == tracer_ids).astype(F32)
+                    result = result + row(carry_in, k) * target
+                else:
+                    result = result - row(carry_high, k) * above
+                    result = result + row(carry_in, k) * value
+                value = result
+                if k + 1 < levels:
+                    out[k, b, :, lanes] = value
+                    above, here = here, below
+            out[levels - 1, b, :, lanes] = value
+            for k in range(levels - 2, -1, -1):
+                value = out[k, b, :, lanes] + row(carry_low, k) * value
+                out[k, b, :, lanes] = value
+
+
+def columns_kernel(start, steps, operands, *refs):
+    inputs = refs[:5]
+    out, mark = refs[operands], refs[operands + 1]
+    scratch = refs[operands + 2 :]
+    levels, blocks, count, _ = out.shape
     wide = pl.BlockSpec((levels, blocks, count, CHUNK), lambda i: (0, 0, 0, i + start))
     flat = pl.BlockSpec((levels, blocks, CHUNK), lambda i: (0, 0, i + start))
     thin = pl.BlockSpec((blocks, CHUNK), lambda i: (0, i + start))
-    in_specs = [wide, flat, flat, thin, thin]
-    operands = [tracers, speed, mixing, wet, patch]
+
+    def body(*blocks_now):
+        columns_step(*blocks_now, *scratch)
+
+    pltpu.emit_pipeline(
+        body, grid=(steps,), in_specs=[wide, flat, flat, thin, thin], out_specs=[wide]
+    )(*inputs, out)
+    mark[...] = jnp.zeros(mark.shape, F32)
+
+
+def columns(tracers, speed, mixing, wet, patch, begin, end, previous, after):
+    levels, blocks, count, cells = tracers.shape
+    operands = in_hbm(tracers, speed, mixing, wet, patch) + [after]
     aliases = {}
     if previous is not None:
-        in_specs.append(pl.BlockSpec(memory_space=pl.ANY))
-        operands.append(previous)
-        aliases = {5: 0}
-    part = steps * CHUNK * blocks * levels
+        aliases = {len(operands): 0}
+        operands += in_hbm(previous)
+    part = (end - begin) * CHUNK * blocks * levels
+    tall = CHUNK // LANES * blocks
     return pl.pallas_call(
-        columns_kernel,
-        grid=(steps,),
-        in_specs=in_specs,
-        out_specs=wide,
-        out_shape=jax.ShapeDtypeStruct(tracers.shape, F32),
-        scratch_shapes=[pltpu.VMEM((levels, blocks, CHUNK), F32)] * 5,
+        functools.partial(columns_kernel, begin, end - begin, len(operands)),
+        in_specs=[HBM] * 5 + [pl.BlockSpec(memory_space=pl.ANY)] + [HBM] * len(aliases),
+        out_specs=[HBM, VMEM],
+        out_shape=[
+            jax.ShapeDtypeStruct(tracers.shape, F32),
+            jax.ShapeDtypeStruct((8, LANES), F32),
+        ],
+        scratch_shapes=[pltpu.VMEM((levels, tall, LANES), F32)] * 5,
         input_output_aliases=aliases,
         compiler_params=params(32),
         cost_estimate=pl.CostEstimate(
@@ -117,76 +141,107 @@
     )(*operands)
 
 
-def payload_kernel(buoyancy, wet, prior, land, out):
-    levels, blocks, cells = buoyancy.shape
+def payload_kernel(buoyancy, wet, prior, land, clinic, tropic, out, clinic_out, tropic_out, force, wet_in, prior_in, land_in, sems):
+    copies = [
+        pltpu.make_async_copy(source, target, sems.at[j])
+        for j, (source, target) in enumerate(
+            (
+                (buoyancy, force),
+                (wet, wet_in),
+                (prior, prior_in),
+                (land, land_in),
+                (clinic, clinic_out),
+                (tropic, tropic_out),
+            )
+        )
+    ]
+    for copy in copies:
+        copy.start()
+    for copy in copies:
+        copy.wait()
+    levels, blocks, cells = force.shape
     rows = cells // LANES
-    wet_now = wet[...]
+    wet_now = wet_in[...]
     total = jnp.zeros(wet_now.shape, F32)
     for k in range(levels):
-        total = total + (k < wet_now).astype(F32) * buoyancy[k].astype(F32)
+        total = total + (k < wet_now).astype(F32) * force[k].astype(F32)
     depth = wet_now.astype(F32)
-    first = prior[...]
+    first = prior_in[...]
     for r in range(rows):
         lanes = slice(r * LANES, (r + 1) * LANES)
         out[0, :, r, :] = total[:, lanes]
         out[1, :, r, :] = depth[:, lanes]
         out[2, :, r, :] = first[:, lanes]
-    out[3] = land[...].astype(F32)
-
-
-def payload_of(buoyancy, wet, prior, land):
+    out[3] = land_in[...].astype(F32)
+
+
+def payload_of(buoyancy, wet, prior, land, clinic, tropic):
     blocks, rows, lanes = land.shape
     return pl.pallas_call(
         payload_kernel,
-        in_specs=[VMEM] * 4,
-        out_specs=VMEM,
-        out_shape=jax.ShapeDtypeStruct((FIELDS, blocks, rows, lanes), F32),
+        in_specs=[HBM] * 6,
+        out_specs=[VMEM] * 3,
+        out_shape=[
+            jax.ShapeDtypeStruct((FIELDS, blocks, rows, lanes), F32),
+            jax.ShapeDtypeStruct(clinic.shape, clinic.dtype),
+            jax.ShapeDtypeStruct(tropic.shape, tropic.dtype),
+        ],
+        scratch_shapes=[
+            pltpu.VMEM(each.shape, each.dtype) for each in (buoyancy, wet, prior, land)
+        ]
+        + [pltpu.SemaphoreType.DMA((6,))],
         compiler_params=params(16),
-    )(buoyancy, wet, prior, land)
-
-
-def select_kernel(spread, *refs):
+    )(*in_hbm(buoyancy, wet, prior, land, clinic, tropic))
+
+
+def select_kernel(spread, band_rows, *refs):
     parts = refs[: len(spread)]
-    clinic, tropic, place, own, to_south, to_north, band = refs[len(spread) :]
-    blocks, rows = own.shape[1], own.shape[2]
+    clinic, tropic, _, own, to_pair, to_other, band = refs[len(spread) :]
+    blocks = own.shape[1]
     band_width = band.shape[1]
-    band_row, column, band_rows = place[0], place[1], place[2]
+    band_row, column = lax.axis_index("by"), lax.axis_index("bx")
     first_slot = band_row * band_width
-    for part, (hop, ref) in enumerate(zip(spread, parts)):
+    for hop, ref in zip(spread, parts):
         holder = (column ^ hop) * blocks
         for s in range(blocks):
             slot = first_slot + holder + s
             at = clinic[slot] - first_slot
             for f in range(FIELDS - 1):
-                band[f, at] = ref[f, s]
-            band[FIELDS - 1, tropic[slot] - first_slot] = ref[FIELDS - 1, s]
-
-    lane = lax.broadcasted_iota(jnp.int32, (rows, LANES), 1)
-
-    def sides(f, at, rows_from, rows_to):
+                for h in range(2):
+                    band[f, at, h] = ref[f, s, h * HALO : (h + 1) * HALO]
+            at = tropic[slot] - first_slot
+            for h in range(2):
+                band[FIELDS - 1, at, h] = ref[FIELDS - 1, s, h * HALO : (h + 1) * HALO]
+
+    lane = lax.broadcasted_iota(jnp.int32, (HALO, LANES), 1)
+
+    def sides(f, at, half):
         east = lax.rem(at + 1, band_width)
         west = lax.rem(at + band_width - 1, band_width)
-        pick = lane[rows_from:rows_to]
         return jnp.where(
-            pick < HALO,
-            band[f, east, rows_from:rows_to],
-            jnp.where(pick >= LANES - HALO, band[f, west, rows_from:rows_to], 0.0),
+            lane < HALO,
+            band[f, east, half],
+            jnp.where(lane >= LANES - HALO, band[f, west, half], 0.0),
         )
 
     for i in range(blocks):
         at = tropic[first_slot + column * blocks + i] - first_slot
         for f in range(FIELDS):
-            own[f, i, :, 0:LANES] = band[f, at]
-            own[f, i, :, LANES : 2 * LANES] = sides(f, at, 0, rows)
-
-    for out, move, rows_from in ((to_south, 1, rows - HALO), (to_north, -1, 0)):
+            for h in range(2):
+                rows = slice(h * HALO, (h + 1) * HALO)
+                own[f, i, rows, 0:LANES] = band[f, at, h]
+                own[f, i, rows, LANES : 2 * LANES] = sides(f, at, h)
+
+    odd = lax.rem(band_row, 2)
+    for out, move in ((to_pair, 1 - 2 * odd), (to_other, 2 * odd - 1)):
+        half = (move + 1) // 2
         other = lax.rem(band_row + move + band_rows, band_rows) * band_width
         packed = [None] * FIELDS
         for i in range(blocks):
             at = tropic[other + column * blocks + i] - other
             for f in range(FIELDS):
-                out[f, i] = band[f, at, rows_from : rows_from + HALO]
-                beside = sides(f, at, rows_from, rows_from + HALO)
+                out[f, i] = band[f, at, half]
+                beside = sides(f, at, half)
                 if i:
                     beside = pltpu.roll(beside, 2 * HALO * i, 1)
                 packed[f] = beside if i == 0 else packed[f] + beside
@@ -194,17 +249,18 @@
             out[f, blocks] = packed[f]
 
 
-def select(spread, parts, clinic, tropic, place, band_width):
+def select(spread, band_rows, parts, clinic, tropic, band_width, after):
     blocks, rows, lanes = parts[0].shape[1:]
+    assert 2 * HALO * blocks <= LANES
     edge = jax.ShapeDtypeStruct((FIELDS, blocks + 1, HALO, lanes), F32)
     return pl.pallas_call(
-        functools.partial(select_kernel, spread),
-        in_specs=[VMEM] * len(parts) + [SMEM] * 3,
+        functools.partial(select_kernel, spread, band_rows),
+        in_specs=[VMEM] * len(parts) + [SMEM] * 2 + [pl.BlockSpec(memory_space=pl.ANY)],
         out_specs=[VMEM] * 3,
         out_shape=[jax.ShapeDtypeStruct((FIELDS, blocks, rows, 2 * lanes), F32), edge, edge],
-        scratch_shapes=[pltpu.VMEM((FIELDS, band_width, rows, lanes), F32)],
+        scratch_shapes=[pltpu.VMEM((FIELDS, band_width, rows // HALO, HALO, lanes), F32)],
         compiler_params=params(16),
-    )(*parts, clinic, tropic, place)
+    )(*parts, clinic, tropic, after)
 
 
 def two_sum(a, b):
@@ -256,18 +312,23 @@
     return pair
 
 
-def basis_kernel(levels, own, north, south, vectors, guess, sums, images):
+def basis_kernel(levels, band_rows, own, from_pair, from_other, vectors, guess, sums, images):
     blocks, rows = own.shape[1], own.shape[2]
     tall = rows + 2 * HALO
     inner = slice(HALO, HALO + rows)
     lane = lax.broadcasted_iota(jnp.int32, (HALO, LANES), 1)
     beside = (lane < HALO) | (lane >= LANES - HALO)
 
-    def edge(ref, f, i):
-        packed = ref[f, blocks]
+    band_row = lax.axis_index("by")
+    odd = lax.rem(band_row, 2) == 1
+
+    def edge(from_odd, from_even, present, f, i):
+        packed = jnp.where(odd, from_odd[f, blocks], from_even[f, blocks])
         if i:
             packed = pltpu.roll(packed, LANES - 2 * HALO * i, 1)
-        return jnp.concatenate([ref[f, i], jnp.where(beside, packed, 0.0)], axis=1)
+        middle = jnp.where(odd, from_odd[f, i], from_even[f, i])
+        both = jnp.concatenate([middle, jnp.where(beside, packed, 0.0)], axis=1)
+        return jnp.where(present, both, 0.0)
 
     def east(v):
         return pltpu.roll(v, 2 * LANES - 1, 1)
@@ -283,7 +344,14 @@
 
     for i in range(blocks):
         forcing, depth, prior, ocean = (
-            jnp.concatenate([edge(north, f, i), own[f, i], edge(south, f, i)], axis=0)
+            jnp.concatenate(
+                [
+                    edge(from_pair, from_other, band_row > 0, f, i),
+                    own[f, i],
+                    edge(from_other, from_pair, band_row < band_rows - 1, f, i),
+                ],
+                axis=0,
+            )
             for f in range(FIELDS)
         )
         scale = FACE_SCALE / levels
@@ -344,32 +412,32 @@
         placed = high + low if placed is None else placed + high + low
     for step in (4, 2, 1):
         placed = placed + pltpu.roll(placed, step, 0)
-    sums[...] = jnp.broadcast_to(placed[None], sums.shape)
-
-
-def basis(levels, own, north, south, devices):
+    sums[...] = jnp.broadcast_to(placed[0:1][None], sums.shape)
+
+
+def basis(levels, own, from_pair, from_other, band_rows, devices):
     fields, blocks, rows, _ = own.shape
     return pl.pallas_call(
-        functools.partial(basis_kernel, levels),
+        functools.partial(basis_kernel, levels, band_rows),
         in_specs=[VMEM] * 3,
         out_specs=[VMEM] * 3,
         out_shape=[
             jax.ShapeDtypeStruct((ITERS, blocks * rows, LANES), F32),
             jax.ShapeDtypeStruct((blocks, rows, LANES), F32),
-            jax.ShapeDtypeStruct((devices, 8, LANES), F32),
+            jax.ShapeDtypeStruct((devices, 1, LANES), F32),
         ],
         scratch_shapes=[pltpu.VMEM((ITERS + 1, blocks * rows, LANES), F32)],
         compiler_params=params(16),
-    )(own, north, south)
+    )(own, from_pair, from_other)
 
 
 def finish_kernel(sums, vectors, guess, out):
     devices = sums.shape[0]
     blocks, rows = guess.shape[0], guess.shape[1]
-    pairs = [(sums[d], jnp.zeros((8, LANES), F32)) for d in range(devices)]
+    pairs = [(sums[d : d + 8], jnp.zeros((8, LANES), F32)) for d in range(0, devices, 8)]
     while len(pairs) > 1:
         pairs = [pair_add(pairs[j], pairs[j + 1]) for j in range(0, len(pairs), 2)]
-    total, error = pairs[0]
+    total, error = fold(pairs[0], 0, (4, 2, 1))
     low = error + pltpu.roll(total, 64, 1)
     row_id = lax.broadcasted_iota(jnp.int32, (8, LANES), 0)
     lane_id = lax.broadcasted_iota(jnp.int32, (8, LANES), 1)
@@ -420,6 +488,17 @@
     return lax.ppermute(array, axis, [(i, i ^ hop) for i in range(count)])
 
 
+def other_partners(band_rows, holders):
+    pairs = []
+    for row in range(band_rows):
+        other = ((row + 1) ^ 1) - 1
+        for column in range(holders):
+            inside = 0 <= other < band_rows
+            target = (other, column) if inside else (row, column ^ 1)
+            pairs.append((row * holders + column, target[0] * holders + target[1]))
+    return pairs
+
+
 def local(
     tracers,
     vertical_speed,
@@ -434,32 +513,31 @@
 ):
     levels, blocks, _, cells = tracers.shape
     band_rows, holders = lax.axis_size("by"), lax.axis_size("bx")
-    place = jnp.stack(
-        [lax.axis_index("by"), lax.axis_index("bx"), jnp.int32(band_rows)]
-    ).astype(jnp.int32)
-
-    payload = payload_of(buoyancy_force, wet_levels, prior_height, land_mask)
+    chunks = cells // CHUNK
+    early = chunks * EARLY // 8
+    column_inputs = (tracers, vertical_speed, diffusivity, wet_levels, surface_patch)
+
+    payload, clinic, tropic = payload_of(
+        buoyancy_force, wet_levels, prior_height, land_mask, baroclinic_map, barotropic_map
+    )
     spread = list(range(0, holders, 2))
     parts = [payload] + [swap(payload, "bx", hop) for hop in spread[1:]]
+    stepped, mark = columns(*column_inputs, 0, early, None, payload)
+    *parts, mark = lax.optimization_barrier((*parts, mark))
     parts = parts + [swap(part, "bx", 1) for part in parts]
     spread = spread + [hop + 1 for hop in spread]
 
-    own, to_south, to_north = select(
-        tuple(spread), parts, baroclinic_map, barotropic_map, place, holders * blocks
+    own, to_pair, to_other = select(
+        tuple(spread), band_rows, parts, clinic, tropic, holders * blocks, mark
     )
-    north = lax.ppermute(to_south, "by", [(i, i + 1) for i in range(band_rows - 1)])
-    south = lax.ppermute(to_north, "by", [(i + 1, i) for i in range(band_rows - 1)])
-
-    half = cells // 2
-    stepped = columns(
-        tracers, vertical_speed, diffusivity, wet_levels, surface_patch, 0, half, None
+    from_pair = swap(to_pair, "by", 1)
+    from_other = lax.ppermute(to_other, ("by", "bx"), other_partners(band_rows, holders))
+    vectors, guess, sums = basis(
+        levels, own, from_pair, from_other, band_rows, band_rows * holders
     )
-    stepped = columns(
-        tracers, vertical_speed, diffusivity, wet_levels, surface_patch, half, cells, stepped
-    )
-
-    vectors, guess, sums = basis(levels, own, north, south, band_rows * holders)
     gathered = lax.all_to_all(sums, ("by", "bx"), 0, 0, tiled=True)
+    stepped, _ = columns(*column_inputs, early, chunks, stepped, sums)
+    gathered = gathered.reshape(band_rows * holders, LANES)
     return stepped, finish(gathered, vectors, guess)
 
 

time: 53.3 us -> 37.5 us (0.70); the launches traced: 52.6 us -> 37.3 us
  local copies, waits for them, and re-layouts: 12.2 us -> 0 us
  waiting for transfers between devices: 12.2 us -> 6.46 us
  Pallas kernels: 13.7 us -> 17.3 us
  starting transfers between devices: 13.7 us -> 12.9 us
    unnamed x22 -> x0, local copies, waits for them, and re-layouts: 12.2 us -> none
    ppermute x2 -> x1, waiting for transfers between devices: 5.03 us -> 0.01 us  [local(): lax.ppermute(to_other, ('by', 'bx'), other_partners(band_rows, holders))]
    ppermute x2 -> x1, starting transfers between devices: 4.78 us -> 0.04 us  [local(): lax.ppermute(to_other, ('by', 'bx'), other_partners(band_rows, holders))]
    pallas_call x5, Pallas kernels: 11.9 us -> 15.6 us  [the longest x2 10.9 us: columns(): pl.pallas_call(functools.partial(columns_kernel, begin, end - begin, len(...]
    ppermute x7 -> x8, starting transfers between devices: 5.06 us -> 7.21 us  [swap(): return lax.ppermute(array, axis, [(i, i ^ hop) for i in range(count)])]
    ppermute x7 -> x8, waiting for transfers between devices: 7.17 us -> 5.15 us  [swap(): return lax.ppermute(array, axis, [(i, i ^ hop) for i in range(count)])]
    all_to_all x1, starting transfers between devices: 3.9 us -> 5.64 us  [local(): gathered = lax.all_to_all(sums, ('by', 'bx'), 0, 0, tiled=True)]
    all_to_all x1, waiting for transfers between devices: 0.01 us -> 1.31 us  [local(): gathered = lax.all_to_all(sums, ('by', 'bx'), 0, 0, tiled=True)]
  transfers between devices with their start and end apart: 10 -> 10, of which waited for: 6 -> 7; matrix products, arithmetic and copies ran while one was open for 0% -> 0% of each run, Pallas kernels for 16% -> 29%
where the time goes in v2:
time: 37.5 us; the launch traced here: 37.3 us
  Pallas kernels  17.3 us (46%)
  starting transfers between devices  12.9 us (34%)
  waiting for transfers between devices  6.46 us (17%)
  between operations  0.67 us (2%)
    pallas_call x2, Pallas kernels, columns(): pl.pallas_call(functools.partial(columns_kernel, begin, end - begin, len(...  10.9 us
    ppermute x8, starting transfers between devices, swap(): return lax.ppermute(array, axis, [(i, i ^ hop) for i in range(count)])  7.21 us
    all_to_all x1, starting transfers between devices, local(): gathered = lax.all_to_all(sums, ('by', 'bx'), 0, 0, tiled=True)  5.64 us
    ppermute x8, waiting for transfers between devices, swap(): return lax.ppermute(array, axis, [(i, i ^ hop) for i in range(count)])  5.15 us
    pallas_call x1, Pallas kernels, basis(): pl.pallas_call(functools.partial(basis_kernel, levels, band_rows), in_spe...  2.63 us
    pallas_call x1, Pallas kernels, finish(): pl.pallas_call(finish_kernel, in_specs=[VMEM] * 3, out_specs=VMEM, out_sh...  1.77 us
    all_to_all x1, waiting for transfers between devices, local(): gathered = lax.all_to_all(sums, ('by', 'bx'), 0, 0, tiled=True)  1.31 us
    pallas_call x1, Pallas kernels, payload_of(): pl.pallas_call(payload_kernel, in_specs=[HBM] * 6, out_specs=[VMEM] * 3,...  1.18 us
  transfers between devices with their start and end apart: 10, of which 7 were waited for; matrix products, arithmetic and copies ran while one was open for 0% of the time, Pallas kernels for 29%

profile of v2, /device:TPU:0, one launch (start us, length us, event | category | flops | bytes accessed | tf_op | source)
XLA Modules:
  0.0 37.3 jit_solution(15474218732037426381)
XLA Ops:
  0.6 1.2 %shard_map.113 = (f32[4,4,16,128]{3,2,1,0:T(8,128)S(1)}, s32[128]{0:T(128)S(1)}, s32[128]{0:T(128)S(1)}) custom-call(bf16[20,4,2048]{2,1,0:T(4,128)(2,1)} %buoyancy.1, s32[4,2048]{1,0:T(4,128)} %refs_3_.3, f32[4,2048]{1,0:T(4,128)} %prior.1, s32[4,16,128]{2,1,0:T(8,128)} %land.1, s32[128]{0:T(128)} %clinic.1, s32[128]{0:T(128)} %tropic.1), custom_call_target="tpu_custom_call" | custom-call | tf_op jit(solution)/shard_map/pallas_call | solution.py:180
  1.8 3.0 %collective-permute-start = (f32[4,4,16,128]{3,2,1,0:T(8,128)S(1)}, f32[4,4,16,128]{3,2,1,0:T(8,128)S(1)}, u32[]{:S(2)}, u32[]{:S(2)}) collective-permute-start(f32[4,4,16,128]{3,2,1,0:T(8,128)S(1)} %get-tuple-element.21.refs_5_.refs_0_), channel_id=1, source_target_pairs={{0,2},{1,3},{2,0},{3,1},{4,6},{5,7},{6,4},{7,5},{8,10},{9,11},{10,... | collective-permute-start | bytes 393224 | tf_op jit(solution)/shard_map/ppermute | solution.py:488
  4.8 1.5 %collective-permute-start.1 = (f32[4,4,16,128]{3,2,1,0:T(8,128)S(1)}, f32[4,4,16,128]{3,2,1,0:T(8,128)S(1)}, u32[]{:S(2)}, u32[]{:S(2)}) collective-permute-start(f32[4,4,16,128]{3,2,1,0:T(8,128)S(1)} %get-tuple-element.21.refs_5_.refs_0_), channel_id=1, source_target_pairs={{0,4},{1,5},{2,6},{3,7},{4,0},{5,1},{6,2},{7,3},{8,12},{9,13},{10,... | collective-permute-start | bytes 393224 | tf_op jit(solution)/shard_map/ppermute | solution.py:488
  6.3 0.0 collective-permute-start.2
  6.4 5.2 %shard_map.114 = (f32[20,4,16,2048]{3,2,1,0:T(8,128)}, f32[8,128]{1,0:T(8,128)S(1)}) custom-call(f32[20,4,16,2048]{3,2,1,0:T(8,128)} %refs_0_.3, f32[20,4,2048]{2,1,0:T(4,128)} %refs_1_.3, f32[20,4,2048]{2,1,0:T(4,128)} %refs_2_.3, s32[4,2048]{1,0:T(4,128)} %refs_3_.3, s32[4,2048]{1,0:T(4,128)} %refs_4_.3, ...), custom_call_target="tpu_custom_call" | custom-call | flops 13107200 | bytes 11141120 | tf_op jit(solution)/shard_map/pallas_call | solution.py:127
  11.5 0.0 collective-permute-done.refs_1_
  11.5 1.1 %collective-permute-done.1.refs_2_ = f32[4,4,16,128]{3,2,1,0:T(8,128)S(1)} collective-permute-done((f32[4,4,16,128]{3,2,1,0:T(8,128)S(1)}, f32[4,4,16,128]{3,2,1,0:T(8,128)S(1)}, u32[]{:S(2)}, u32[]{:S(2)}) %collective-permute-start.1) | collective-permute-done | bytes 131104 | tf_op jit(solution)/shard_map/ppermute | solution.py:488
  12.6 0.0 collective-permute-done.2.refs_3_
  12.6 0.5 %collective-permute-start.4 = (f32[4,4,16,128]{3,2,1,0:T(8,128)S(1)}, f32[4,4,16,128]{3,2,1,0:T(8,128)S(1)}, u32[]{:S(2)}, u32[]{:S(2)}) collective-permute-start(f32[4,4,16,128]{3,2,1,0:T(8,128)S(1)} %collective-permute-done.refs_1_), channel_id=1, source_target_pairs={{0,1},{1,0},{2,3},{3,2},{4,5},{5,4},{6,7},{7,6},{8,9},{9,8},{10,11... | collective-permute-start | bytes 393224 | tf_op jit(solution)/shard_map/ppermute | solution.py:488
  13.1 0.0 collective-permute-start.5
  13.1 0.5 %collective-permute-start.6 = (f32[4,4,16,128]{3,2,1,0:T(8,128)S(1)}, f32[4,4,16,128]{3,2,1,0:T(8,128)S(1)}, u32[]{:S(2)}, u32[]{:S(2)}) collective-permute-start(f32[4,4,16,128]{3,2,1,0:T(8,128)S(1)} %collective-permute-done.2.refs_3_), channel_id=1, source_target_pairs={{0,1},{1,0},{2,3},{3,2},{4,5},{5,4},{6,7},{7,6},{8,9},{9,8},{10,11... | collective-permute-start | bytes 393224 | tf_op jit(solution)/shard_map/ppermute | solution.py:488
  13.6 0.3 collective-permute-done.3.refs_4_
  14.0 0.2 collective-permute-done.4.refs_5_
  14.1 0.3 collective-permute-done.5.refs_6_
  14.5 0.2 collective-permute-done.6.refs_7_
  14.7 0.8 %shard_map.115 = (f32[4,4,16,256]{3,2,1,0:T(8,128)S(1)}, f32[4,5,8,128]{3,2,1,0:T(8,128)S(1)}, f32[4,5,8,128]{3,2,1,0:T(8,128)S(1)}) custom-call(f32[4,4,16,128]{3,2,1,0:T(8,128)S(1)} %get-tuple-element.21.refs_5_.refs_0_, f32[4,4,16,128]{3,2,1,0:T(8,128)S(1)} %collective-permute-done.refs_1_, f32[4,4,16,128]{3,2,1,0:T(8,128)S(1)} %collective-permute-done.1.refs_2_, ...), custom_call_target="tpu_custom_call" | custom-call | tf_op jit(solution)/shard_map/pallas_call | solution.py:256
  15.5 1.6 %collective-permute-start.7 = (f32[4,5,8,128]{3,2,1,0:T(8,128)S(1)}, f32[4,5,8,128]{3,2,1,0:T(8,128)S(1)}, u32[]{:S(2)}, u32[]{:S(2)}) collective-permute-start(f32[4,5,8,128]{3,2,1,0:T(8,128)S(1)} %get-tuple-element.29), channel_id=1, source_target_pairs={{0,8},{8,0},{16,24},{24,16},{1,9},{9,1},{17,25},{25,17},{2,10},{10... | collective-permute-start | bytes 245768 | tf_op jit(solution)/shard_map/ppermute | solution.py:488
  17.1 0.0 collective-permute-start.8
  17.2 3.1 %collective-permute-done.7.from_pair = f32[4,5,8,128]{3,2,1,0:T(8,128)S(1)} collective-permute-done((f32[4,5,8,128]{3,2,1,0:T(8,128)S(1)}, f32[4,5,8,128]{3,2,1,0:T(8,128)S(1)}, u32[]{:S(2)}, u32[]{:S(2)}) %collective-permute-start.7) | collective-permute-done | bytes 81952 | tf_op jit(solution)/shard_map/ppermute | solution.py:488
  20.2 2.6 %shard_map.116 = (f32[6,64,128]{2,1,0:T(8,128)S(1)}, f32[4,16,128]{2,1,0:T(8,128)S(1)}, f32[32,1,128]{2,1,0:T(1,128)}) custom-call(f32[4,4,16,256]{3,2,1,0:T(8,128)S(1)} %get-tuple-element.28.own, f32[4,5,8,128]{3,2,1,0:T(8,128)S(1)} %collective-permute-done.7.from_pair, f32[4,5,8,128]{3,2,1,0:T(8,128)S(1)} %collective-permute-done.8.from_other), custom_call_target="tpu_custom_call" | custom-call | tf_op jit(solution)/shard_map/pallas_call | solution.py:420
  22.9 5.6 %all-to-all-start = ((f32[32,1,128]{2,1,0:T(1,128)}), f32[32,1,128]{2,1,0:T(1,128)S(1)}, u32[]{:S(2)}, u32[]{:S(2)}) async-start(f32[32,1,128]{2,1,0:T(1,128)} %get-tuple-element.31.refs_5_), calls=%async_computation | async-start | bytes 32768 | tf_op jit(solution)/shard_map/all_to_all | solution.py:538
  28.5 5.8 %shard_map.117 = (f32[20,4,16,2048]{3,2,1,0:T(8,128)}, f32[8,128]{1,0:T(8,128)}) custom-call(f32[20,4,16,2048]{3,2,1,0:T(8,128)} %refs_0_.3, f32[20,4,2048]{2,1,0:T(4,128)} %refs_1_.3, f32[20,4,2048]{2,1,0:T(4,128)} %refs_2_.3, s32[4,2048]{1,0:T(4,128)} %refs_3_.3, s32[4,2048]{1,0:T(4,128)} %refs_4_.3, ...), custom_call_target="tpu_custom_call", output_to_operand_aliasing={{0}: (6, {})} | custom-call | flops 13107200 | bytes 11141120 | tf_op jit(solution)/shard_map/pallas_call | solution.py:127
  34.3 1.3 %all-to-all-done = f32[32,1,128]{2,1,0:T(1,128)S(1)} async-done(((f32[32,1,128]{2,1,0:T(1,128)}), f32[32,1,128]{2,1,0:T(1,128)S(1)}, u32[]{:S(2)}, u32[]{:S(2)}) %all-to-all-start) | async-done | bytes 16416 | tf_op jit(solution)/shard_map/all_to_all | solution.py:538
  35.6 1.8 %shard_map.118 = f32[4,16,128]{2,1,0:T(8,128)} custom-call(f32[32,128]{1,0:T(8,128)S(1)} %bitcast.1, f32[6,64,128]{2,1,0:T(8,128)S(1)} %get-tuple-element.34.vectors, f32[4,16,128]{2,1,0:T(8,128)S(1)} %get-tuple-element.35.guess), custom_call_target="tpu_custom_call" | custom-call | tf_op jit(solution)/shard_map/pallas_call | solution.py:477
  (2 shorter events, 0.0 us)
Async XLA Ops:
  1.8 9.7 %collective-permute-start = (f32[4,4,16,128]{3,2,1,0:T(8,128)S(1)}, f32[4,4,16,128]{3,2,1,0:T(8,128)S(1)}, u32[]{:S(2)}, u32[]{:S(2)}) collective-permute-start(f32[4,4,16,128]{3,2,1,0:T(8,128)S(1)} %get-tuple-element.21.refs_5_.refs_0_), channel_id=1, source_target_pairs={{0,2},{1,3},{2,0},{3,1},{4,6},{5,7},{6,4},{7,5},{8,10},{9,11},{10,... | collective-permute-start | bytes 393224 | tf_op jit(solution)/shard_map/ppermute | solution.py:488
  4.8 7.8 %collective-permute-start.1 = (f32[4,4,16,128]{3,2,1,0:T(8,128)S(1)}, f32[4,4,16,128]{3,2,1,0:T(8,128)S(1)}, u32[]{:S(2)}, u32[]{:S(2)}) collective-permute-start(f32[4,4,16,128]{3,2,1,0:T(8,128)S(1)} %get-tuple-element.21.refs_5_.refs_0_), channel_id=1, source_target_pairs={{0,4},{1,5},{2,6},{3,7},{4,0},{5,1},{6,2},{7,3},{8,12},{9,13},{10,... | collective-permute-start | bytes 393224 | tf_op jit(solution)/shard_map/ppermute | solution.py:488
  6.3 6.3 %collective-permute-start.2 = (f32[4,4,16,128]{3,2,1,0:T(8,128)S(1)}, f32[4,4,16,128]{3,2,1,0:T(8,128)S(1)}, u32[]{:S(2)}, u32[]{:S(2)}) collective-permute-start(f32[4,4,16,128]{3,2,1,0:T(8,128)S(1)} %get-tuple-element.21.refs_5_.refs_0_), channel_id=1, source_target_pairs={{0,6},{1,7},{2,4},{3,5},{4,2},{5,3},{6,0},{7,1},{8,14},{9,15},{10,... | collective-permute-start | bytes 393224 | tf_op jit(solution)/shard_map/ppermute | solution.py:488
  12.6 1.3 %collective-permute-start.3 = (f32[4,4,16,128]{3,2,1,0:T(8,128)S(1)}, f32[4,4,16,128]{3,2,1,0:T(8,128)S(1)}, u32[]{:S(2)}, u32[]{:S(2)}) collective-permute-start(f32[4,4,16,128]{3,2,1,0:T(8,128)S(1)} %get-tuple-element.21.refs_5_.refs_0_), channel_id=1, source_target_pairs={{0,1},{1,0},{2,3},{3,2},{4,5},{5,4},{6,7},{7,6},{8,9},{9,8},{10,11... | collective-permute-start | bytes 393224 | tf_op jit(solution)/shard_map/ppermute | solution.py:488
  12.6 1.5 %collective-permute-start.4 = (f32[4,4,16,128]{3,2,1,0:T(8,128)S(1)}, f32[4,4,16,128]{3,2,1,0:T(8,128)S(1)}, u32[]{:S(2)}, u32[]{:S(2)}) collective-permute-start(f32[4,4,16,128]{3,2,1,0:T(8,128)S(1)} %collective-permute-done.refs_1_), channel_id=1, source_target_pairs={{0,1},{1,0},{2,3},{3,2},{4,5},{5,4},{6,7},{7,6},{8,9},{9,8},{10,11... | collective-permute-start | bytes 393224 | tf_op jit(solution)/shard_map/ppermute | solution.py:488
  13.1 1.3 %collective-permute-start.5 = (f32[4,4,16,128]{3,2,1,0:T(8,128)S(1)}, f32[4,4,16,128]{3,2,1,0:T(8,128)S(1)}, u32[]{:S(2)}, u32[]{:S(2)}) collective-permute-start(f32[4,4,16,128]{3,2,1,0:T(8,128)S(1)} %collective-permute-done.1.refs_2_), channel_id=1, source_target_pairs={{0,1},{1,0},{2,3},{3,2},{4,5},{5,4},{6,7},{7,6},{8,9},{9,8},{10,11... | collective-permute-start | bytes 393224 | tf_op jit(solution)/shard_map/ppermute | solution.py:488
  13.1 1.5 %collective-permute-start.6 = (f32[4,4,16,128]{3,2,1,0:T(8,128)S(1)}, f32[4,4,16,128]{3,2,1,0:T(8,128)S(1)}, u32[]{:S(2)}, u32[]{:S(2)}) collective-permute-start(f32[4,4,16,128]{3,2,1,0:T(8,128)S(1)} %collective-permute-done.2.refs_3_), channel_id=1, source_target_pairs={{0,1},{1,0},{2,3},{3,2},{4,5},{5,4},{6,7},{7,6},{8,9},{9,8},{10,11... | collective-permute-start | bytes 393224 | tf_op jit(solution)/shard_map/ppermute | solution.py:488
  15.5 4.7 %collective-permute-start.7 = (f32[4,5,8,128]{3,2,1,0:T(8,128)S(1)}, f32[4,5,8,128]{3,2,1,0:T(8,128)S(1)}, u32[]{:S(2)}, u32[]{:S(2)}) collective-permute-start(f32[4,5,8,128]{3,2,1,0:T(8,128)S(1)} %get-tuple-element.29), channel_id=1, source_target_pairs={{0,8},{8,0},{16,24},{24,16},{1,9},{9,1},{17,25},{25,17},{2,10},{10... | collective-permute-start | bytes 245768 | tf_op jit(solution)/shard_map/ppermute | solution.py:488
  17.1 3.1 %collective-permute-start.8 = (f32[4,5,8,128]{3,2,1,0:T(8,128)S(1)}, f32[4,5,8,128]{3,2,1,0:T(8,128)S(1)}, u32[]{:S(2)}, u32[]{:S(2)}) collective-permute-start(f32[4,5,8,128]{3,2,1,0:T(8,128)S(1)} %get-tuple-element.30), channel_id=1, source_target_pairs={{0,1},{1,0},{2,3},{3,2},{4,5},{5,4},{6,7},{7,6},{8,16},{9,17},{10,... | collective-permute-start | bytes 245768 | tf_op jit(solution)/shard_map/ppermute | solution.py:534
  22.9 12.7 %all-to-all-start = ((f32[32,1,128]{2,1,0:T(1,128)}), f32[32,1,128]{2,1,0:T(1,128)S(1)}, u32[]{:S(2)}, u32[]{:S(2)}) async-start(f32[32,1,128]{2,1,0:T(1,128)} %get-tuple-element.31.refs_5_), calls=%async_computation | async-start | bytes 32768 | tf_op jit(solution)/shard_map/all_to_all | solution.py:538

commit v3 on v2

--- a/solution.py
+++ b/solution.py
@@ -16,8 +16,9 @@
 HALO = 8
 LANES = 128
 FIELDS = 4
+ENTRIES = [(a, b) for a in range(ITERS) for b in range(a, ITERS + 1)]
 CHUNK = 512
-EARLY = 4
+EARLY = 9
 F32 = jnp.float32
 VMEM = pl.BlockSpec(memory_space=pltpu.VMEM)
 SMEM = pl.BlockSpec(memory_space=pltpu.SMEM)
@@ -32,13 +33,15 @@
     return pltpu.CompilerParams(vmem_limit_bytes=mebibytes * 2**20)
 
 
-def columns_step(tracers, speed, mixing, wet, patch, out, carry_in, carry_own, carry_up, carry_low, carry_high):
-    levels, blocks, count, width = tracers.shape
-    tiles = width // LANES
+def fold_columns(speed, mixing, wet, patch, regions, factors):
+    enter, keep, raise_, lower, sink = factors
+    levels = speed.shape[0]
+    tiles = speed.shape[2] // LANES
 
     def stacked(block):
         return jnp.concatenate([block[:, t * LANES : (t + 1) * LANES] for t in range(tiles)], axis=0)
 
+    regions[...] = stacked(patch[...])
     wet_now = stacked(wet[...])
     zero = jnp.zeros(wet_now.shape, F32)
     mix_above, up_above, down_above, inverse = zero, zero, zero, zero
@@ -54,91 +57,157 @@
             diagonal = diagonal + source
         inverse = 1.0 / (diagonal - mix_above * (mix_above * inverse))
         scaled_wet = is_wet * inverse
-        carry_own[k] = scaled_wet * (1.0 + down - up_above)
-        carry_up[k] = scaled_wet * up
-        carry_low[k] = mix * inverse
-        if k == 0:
-            carry_in[k] = source * inverse
-            carry_high[k] = zero
-        else:
-            carry_in[k] = mix_above * inverse
-            carry_high[k] = scaled_wet * down_above
+        keep[k] = scaled_wet * (1.0 + down - up_above)
+        raise_[k] = scaled_wet * up
+        lower[k] = mix * inverse
+        enter[k] = (source if k == 0 else mix_above) * inverse
+        sink[k] = scaled_wet * down_above
         mix_above, up_above, down_above = mix, up, down
-    tracer_ids = lax.broadcasted_iota(jnp.int32, (count, LANES), 0)
-
-    for b in range(blocks):
-        for t in range(tiles):
-            lanes = slice(t * LANES, (t + 1) * LANES)
-            at = t * blocks + b
-
-            def row(ref, k):
-                return jnp.broadcast_to(ref[k, at : at + 1, :], (count, LANES))
-
-            above = value = None
-            here = tracers[0, b, :, lanes]
-            for k in range(levels):
-                result = row(carry_own, k) * here
-                if k + 1 < levels:
-                    below = tracers[k + 1, b, :, lanes]
-                    result = result + row(carry_up, k) * below
-                if k == 0:
-                    target = (patch[b : b + 1, lanes] == tracer_ids).astype(F32)
-                    result = result + row(carry_in, k) * target
-                else:
-                    result = result - row(carry_high, k) * above
-                    result = result + row(carry_in, k) * value
-                value = result
-                if k + 1 < levels:
-                    out[k, b, :, lanes] = value
-                    above, here = here, below
-            out[levels - 1, b, :, lanes] = value
-            for k in range(levels - 2, -1, -1):
-                value = out[k, b, :, lanes] + row(carry_low, k) * value
-                out[k, b, :, lanes] = value
-
-
-def columns_kernel(start, steps, operands, *refs):
-    inputs = refs[:5]
-    out, mark = refs[operands], refs[operands + 1]
-    scratch = refs[operands + 2 :]
-    levels, blocks, count, _ = out.shape
-    wide = pl.BlockSpec((levels, blocks, count, CHUNK), lambda i: (0, 0, 0, i + start))
-    flat = pl.BlockSpec((levels, blocks, CHUNK), lambda i: (0, 0, i + start))
-    thin = pl.BlockSpec((blocks, CHUNK), lambda i: (0, i + start))
-
-    def body(*blocks_now):
-        columns_step(*blocks_now, *scratch)
-
-    pltpu.emit_pipeline(
-        body, grid=(steps,), in_specs=[wide, flat, flat, thin, thin], out_specs=[wide]
-    )(*inputs, out)
+
+
+def sweep(begin, tracers, out, regions, factors, held, in_sems, out_sems):
+    enter, keep, raise_, lower, sink = factors
+    steps, levels, count, width = held.shape
+    blocks = tracers.shape[1]
+    tiles = width // LANES
+
+    def place(ref, j):
+        slot = lax.rem(j + begin, blocks)
+        at = pl.multiple_of((j + begin) // blocks * width, width)
+        return ref.at[:, slot, :, pl.ds(at, width)]
+
+    def load(j):
+        return pltpu.make_async_copy(place(tracers, j), held.at[j], in_sems.at[j])
+
+    def store(j):
+        return pltpu.make_async_copy(held.at[j], place(out, j), out_sems.at[j])
+
+    tracer_ids = lax.broadcasted_iota(jnp.int32, (count, width), 0)
+
+    def solve(j, carry):
+        load(j).wait()
+        slot = lax.rem(j + begin, blocks)
+        first = (j + begin) // blocks * tiles
+
+        def rows(take):
+            return jnp.concatenate(
+                [
+                    jnp.broadcast_to(take(pl.ds((first + t) * blocks + slot, 1)), (count, LANES))
+                    for t in range(tiles)
+                ],
+                axis=1,
+            )
+
+        def row(ref, k):
+            return rows(lambda at: ref[k, at, :])
+
+        above = value = None
+        here = held[j, 0]
+        for k in range(levels):
+            result = row(keep, k) * here
+            if k + 1 < levels:
+                below = held[j, k + 1]
+                result = result + row(raise_, k) * below
+            if k == 0:
+                target = (rows(lambda at: regions[at, :]) == tracer_ids).astype(F32)
+                result = result + row(enter, k) * target
+            else:
+                result = result - row(sink, k) * above
+                result = result + row(enter, k) * value
+            value = result
+            held[j, k] = value
+            if k + 1 < levels:
+                above, here = here, below
+        for k in range(levels - 2, -1, -1):
+            value = held[j, k] + row(lower, k) * value
+            held[j, k] = value
+        store(j).start()
+        return carry
+
+    def run(prepare):
+        for j in range(steps):
+            load(j).start()
+        prepare()
+        lax.fori_loop(0, steps, solve, 0)
+        for j in range(steps):
+            store(j).wait()
+
+    return run
+
+
+def first_columns_kernel(tracers, speed, mixing, wet, patch, after, out, mark, regions, *rest):
+    factors, (held, speed_in, mixing_in, wet_in, patch_in, sems, in_sems, out_sems) = rest[:5], rest[5:]
+    copies = [
+        pltpu.make_async_copy(source, target, sems.at[j])
+        for j, (source, target) in enumerate(
+            ((speed, speed_in), (mixing, mixing_in), (wet, wet_in), (patch, patch_in))
+        )
+    ]
+    for copy in copies:
+        copy.start()
+
+    def prepare():
+        for copy in copies:
+            copy.wait()
+        fold_columns(speed_in, mixing_in, wet_in, patch_in, regions, factors)
+
     mark[...] = jnp.zeros(mark.shape, F32)
-
-
-def columns(tracers, speed, mixing, wet, patch, begin, end, previous, after):
+    sweep(0, tracers, out, regions, factors, held, in_sems, out_sems)(prepare)
+
+
+def first_columns(tracers, speed, mixing, wet, patch, steps, after):
     levels, blocks, count, cells = tracers.shape
-    operands = in_hbm(tracers, speed, mixing, wet, patch) + [after]
-    aliases = {}
-    if previous is not None:
-        aliases = {len(operands): 0}
-        operands += in_hbm(previous)
-    part = (end - begin) * CHUNK * blocks * levels
-    tall = CHUNK // LANES * blocks
+    rows = cells // LANES * blocks
+    factor = jax.ShapeDtypeStruct((levels, rows, LANES), F32)
     return pl.pallas_call(
-        functools.partial(columns_kernel, begin, end - begin, len(operands)),
-        in_specs=[HBM] * 5 + [pl.BlockSpec(memory_space=pl.ANY)] + [HBM] * len(aliases),
+        first_columns_kernel,
+        in_specs=[HBM] * 5 + [pl.BlockSpec(memory_space=pl.ANY)],
+        out_specs=[HBM] + [VMEM] * 7,
+        out_shape=[
+            jax.ShapeDtypeStruct(tracers.shape, F32),
+            jax.ShapeDtypeStruct((8, LANES), F32),
+            jax.ShapeDtypeStruct((rows, LANES), jnp.int32),
+        ]
+        + [factor] * 5,
+        scratch_shapes=[pltpu.VMEM((steps, levels, count, CHUNK), F32)]
+        + [pltpu.VMEM(each.shape, each.dtype) for each in (speed, mixing, wet, patch)]
+        + [pltpu.SemaphoreType.DMA((n,)) for n in (4, steps, steps)],
+        compiler_params=params(40),
+        cost_estimate=column_cost(tracers, steps),
+    )(*in_hbm(tracers, speed, mixing, wet, patch), after)
+
+
+def rest_columns_kernel(begin, tracers, regions, *rest):
+    factors, (_, _, out, mark, held, in_sems, out_sems) = rest[:5], rest[5:]
+    mark[...] = jnp.zeros(mark.shape, F32)
+    sweep(begin, tracers, out, regions, factors, held, in_sems, out_sems)(lambda: None)
+
+
+def rest_columns(tracers, begin, previous, regions, factors, after):
+    levels, blocks, count, cells = tracers.shape
+    steps = cells // CHUNK * blocks - begin
+    return pl.pallas_call(
+        functools.partial(rest_columns_kernel, begin),
+        in_specs=[HBM] + [VMEM] * 6 + [HBM, pl.BlockSpec(memory_space=pl.ANY)],
         out_specs=[HBM, VMEM],
         out_shape=[
             jax.ShapeDtypeStruct(tracers.shape, F32),
             jax.ShapeDtypeStruct((8, LANES), F32),
         ],
-        scratch_shapes=[pltpu.VMEM((levels, tall, LANES), F32)] * 5,
-        input_output_aliases=aliases,
-        compiler_params=params(32),
-        cost_estimate=pl.CostEstimate(
-            flops=part * count * 10, bytes_accessed=part * (count * 8 + 8), transcendentals=0
-        ),
-    )(*operands)
+        scratch_shapes=[pltpu.VMEM((steps, levels, count, CHUNK), F32)]
+        + [pltpu.SemaphoreType.DMA((steps,))] * 2,
+        input_output_aliases={7: 0},
+        compiler_params=params(24),
+        cost_estimate=column_cost(tracers, steps),
+    )(*in_hbm(tracers), regions, *factors, *in_hbm(previous), after)
+
+
+def column_cost(tracers, steps):
+    levels, _, count, _ = tracers.shape
+    part = steps * CHUNK * levels
+    return pl.CostEstimate(
+        flops=part * count * 10, bytes_accessed=part * (count * 8 + 8), transcendentals=0
+    )
 
 
 def payload_kernel(buoyancy, wet, prior, land, clinic, tropic, out, clinic_out, tropic_out, force, wet_in, prior_in, land_in, sems):
@@ -290,29 +359,21 @@
     return value, error
 
 
-def pair_mul(a, b):
-    value, error = product(a[0], b[0])
-    error = error + (a[0] * b[1] + a[1] * b[0])
-    total = value + error
-    return total, error - (total - value)
-
-
-def pair_inverse(a):
-    guess = 1.0 / a[0]
-    value, error = product(guess, a[0])
-    rest = (1.0 - value) - error - guess * a[1]
-    low = guess * rest
-    total = guess + low
-    return total, low - (total - guess)
-
-
 def fold(pair, axis, steps):
     for step in steps:
         pair = pair_add(pair, tuple(pltpu.roll(part, step, axis) for part in pair))
     return pair
 
 
-def basis_kernel(levels, band_rows, own, from_pair, from_other, vectors, guess, sums, images):
+def lane_sum(pair):
+    high, low = pair
+    grid = 384.0 * jnp.max(jnp.abs(high), axis=1, keepdims=True)
+    lead = (high + grid) - grid
+    rest = jnp.sum((high - lead) + low, axis=1, keepdims=True)
+    return two_sum(jnp.sum(lead, axis=1, keepdims=True), rest)
+
+
+def basis_kernel(levels, band_rows, own, from_pair, from_other, _, vectors, guess, sums, images):
     blocks, rows = own.shape[1], own.shape[2]
     tall = rows + 2 * HALO
     inner = slice(HALO, HALO + rows)
@@ -356,18 +417,15 @@
         )
         scale = FACE_SCALE / levels
         east_face = scale * jnp.minimum(depth, east(depth)) * ocean * east(ocean)
-        west_face = west(east_face)
         south_face = scale * jnp.minimum(depth, below(depth)) * ocean * below(ocean)
-        north_face = above(south_face)
         centre = SURFACE * ocean + (1.0 - ocean)
-        diagonal = centre + east_face + west_face + south_face + north_face
+        diagonal = centre + east_face + west(east_face) + south_face + above(south_face)
         inverse = 1.0 / diagonal
 
         def operate(v):
-            result = centre * v + east_face * (v - east(v))
-            result = result + west_face * (v - west(v))
-            result = result + south_face * (v - below(v))
-            return result + north_face * (v - above(v))
+            along = east_face * (v - east(v))
+            across = south_face * (v - below(v))
+            return centre * v + along - west(along) + across - above(across)
 
         first = ocean * prior
         residual = ocean * forcing - operate(first)
@@ -385,14 +443,10 @@
 
     row_id = lax.broadcasted_iota(jnp.int32, (8, LANES), 0)
     lane_id = lax.broadcasted_iota(jnp.int32, (8, LANES), 1)
-    entries = [(a, b) for a in range(ITERS) for b in range(a, ITERS + 1)]
-    spots = [(8 * a + b, 8 * b + a if b < ITERS else -1) for a, b in entries]
     placed = None
-    for begin in range(0, len(entries), 8):
+    for begin in range(0, len(ENTRIES), 8):
         packed = (jnp.zeros((8, LANES), F32),) * 2
-        spot = jnp.full((8, LANES), -1, jnp.int32)
-        twin = jnp.full((8, LANES), -1, jnp.int32)
-        for offset, (a, b) in enumerate(entries[begin : begin + 8]):
+        for offset, (a, b) in enumerate(ENTRIES[begin : begin + 8]):
             total = error = None
             for r in range(0, blocks * rows, 8):
                 value, rest = product(vectors[a, r : r + 8], images[b, r : r + 8])
@@ -402,24 +456,21 @@
                     total, extra = two_sum(total, value)
                     error = error + (rest + extra)
             pair = fold((total, error), 0, (4, 2, 1))
-            mine = row_id == offset
-            packed = tuple(jnp.where(mine, new, old) for new, old in zip(pair, packed))
-            spot = jnp.where(mine, spots[begin + offset][0], spot)
-            twin = jnp.where(mine, spots[begin + offset][1], twin)
-        packed = fold(packed, 1, (64, 32, 16, 8, 4, 2, 1))
-        high = jnp.where((lane_id == spot) | (lane_id == twin), packed[0], 0.0)
-        low = jnp.where((lane_id == spot + 64) | ((lane_id == twin + 64) & (twin >= 0)), packed[1], 0.0)
+            packed = tuple(jnp.where(row_id == offset, new, old) for new, old in zip(pair, packed))
+        high, low = lane_sum(packed)
+        high = jnp.where(lane_id == row_id + begin, high, 0.0)
+        low = jnp.where(lane_id == row_id + (begin + LANES // 2), low, 0.0)
         placed = high + low if placed is None else placed + high + low
     for step in (4, 2, 1):
         placed = placed + pltpu.roll(placed, step, 0)
     sums[...] = jnp.broadcast_to(placed[0:1][None], sums.shape)
 
 
-def basis(levels, own, from_pair, from_other, band_rows, devices):
+def basis(levels, own, from_pair, from_other, after, band_rows, devices):
     fields, blocks, rows, _ = own.shape
     return pl.pallas_call(
         functools.partial(basis_kernel, levels, band_rows),
-        in_specs=[VMEM] * 3,
+        in_specs=[VMEM] * 3 + [pl.BlockSpec(memory_space=pl.ANY)],
         out_specs=[VMEM] * 3,
         out_shape=[
             jax.ShapeDtypeStruct((ITERS, blocks * rows, LANES), F32),
@@ -428,7 +479,7 @@
         ],
         scratch_shapes=[pltpu.VMEM((ITERS + 1, blocks * rows, LANES), F32)],
         compiler_params=params(16),
-    )(own, from_pair, from_other)
+    )(own, from_pair, from_other, after)
 
 
 def finish_kernel(sums, vectors, guess, out):
@@ -439,38 +490,40 @@
         pairs = [pair_add(pairs[j], pairs[j + 1]) for j in range(0, len(pairs), 2)]
     total, error = fold(pairs[0], 0, (4, 2, 1))
     low = error + pltpu.roll(total, 64, 1)
-    row_id = lax.broadcasted_iota(jnp.int32, (8, LANES), 0)
-    lane_id = lax.broadcasted_iota(jnp.int32, (8, LANES), 1)
-    keep = (row_id < ITERS) & (lane_id < ITERS + 1)
-
-    def rows_of(vector):
-        moved = vector
-        for i in range(1, ITERS):
-            moved = jnp.where(row_id == i, pltpu.roll(vector, LANES - 8 * i, 1), moved)
-        return jnp.where(keep, moved, 0.0)
-
-    matrix = (rows_of(total), rows_of(low))
-    energy = matrix[0]
+    entry = {
+        pair: tuple(jnp.broadcast_to(part[:, n : n + 1], (8, LANES)) for part in (total, low))
+        for n, pair in enumerate(ENTRIES)
+    }
+    energy = [entry[k, k][0] for k in range(ITERS)]
+    inverse, below = [], {}
     for k in range(ITERS):
-        column = tuple(jnp.broadcast_to(part[:, k : k + 1], (8, LANES)) for part in matrix)
-        pivot_row = tuple(jnp.broadcast_to(part[k : k + 1, :], (8, LANES)) for part in matrix)
-        pivot = tuple(jnp.broadcast_to(part[k : k + 1, :], (8, LANES)) for part in column)
-        full = jnp.broadcast_to(energy[k : k + 1, k : k + 1], (8, LANES))
-        good = pivot[0] > PIVOT_FLOOR * full
-        safe = (jnp.where(good, pivot[0], 1.0), jnp.where(good, pivot[1], 0.0))
-        inverse = tuple(jnp.where(good, part, 0.0) for part in pair_inverse(safe))
-        scaled = pair_mul(pivot_row, inverse)
-        change = pair_mul(column, scaled)
-        moved = pair_add(matrix, (-change[0], -change[1]))
-        matrix = tuple(
-            jnp.where(row_id == k, new, jnp.where(keep, old, 0.0)) for new, old in zip(scaled, moved)
-        )
-    weights = matrix[0]
-    result = guess[...]
-    for k in range(ITERS):
-        weight = jnp.broadcast_to(weights[k : k + 1, ITERS : ITERS + 1], (rows, LANES))
-        result = result + weight[None] * vectors[k].reshape(blocks, rows, LANES)
-    out[...] = result
+        pivot = entry[k, k]
+        good = pivot[0] > PIVOT_FLOOR * energy[k]
+        inverse.append(jnp.where(good, 1.0 / jnp.where(good, pivot[0], 1.0), 0.0))
+        for i in range(k + 1, ITERS):
+            side = entry[k, i]
+            lead = side[0] * inverse[k]
+            value, error = product(lead, pivot[0])
+            rest = ((side[0] - value) - error) + (side[1] - lead * pivot[1])
+            below[i, k] = (lead, rest * inverse[k])
+        for i in range(k + 1, ITERS):
+            lead, rest = below[i, k]
+            for j in range(i, ITERS + 1):
+                across = entry[k, j]
+                value, error = product(lead, across[0])
+                error = error + (lead * across[1] + rest * across[0])
+                entry[i, j] = pair_add(entry[i, j], (-value, -error))
+    weights = [entry[k, ITERS][0] * inverse[k] for k in range(ITERS)]
+    for k in range(ITERS - 2, -1, -1):
+        for i in range(ITERS - 1, k, -1):
+            weights[k] = weights[k] - below[i, k][0] * weights[i]
+    for b in range(blocks):
+        for r in range(0, rows, 8):
+            at = b * rows + r
+            result = guess[b, r : r + 8]
+            for k in range(ITERS):
+                result = result + weights[k] * vectors[k, at : at + 8]
+            out[b, r : r + 8] = result
 
 
 def finish(sums, vectors, guess):
@@ -513,16 +566,16 @@
 ):
     levels, blocks, _, cells = tracers.shape
     band_rows, holders = lax.axis_size("by"), lax.axis_size("bx")
-    chunks = cells // CHUNK
-    early = chunks * EARLY // 8
-    column_inputs = (tracers, vertical_speed, diffusivity, wet_levels, surface_patch)
+    early = cells // CHUNK * blocks * EARLY // 16
 
     payload, clinic, tropic = payload_of(
         buoyancy_force, wet_levels, prior_height, land_mask, baroclinic_map, barotropic_map
     )
     spread = list(range(0, holders, 2))
     parts = [payload] + [swap(payload, "bx", hop) for hop in spread[1:]]
-    stepped, mark = columns(*column_inputs, 0, early, None, payload)
+    stepped, mark, regions, *factors = first_columns(
+        tracers, vertical_speed, diffusivity, wet_levels, surface_patch, early, payload
+    )
     *parts, mark = lax.optimization_barrier((*parts, mark))
     parts = parts + [swap(part, "bx", 1) for part in parts]
     spread = spread + [hop + 1 for hop in spread]
@@ -532,11 +585,12 @@
     )
     from_pair = swap(to_pair, "by", 1)
     from_other = lax.ppermute(to_other, ("by", "bx"), other_partners(band_rows, holders))
+    stepped, late = rest_columns(tracers, early, stepped, regions, factors, to_other)
+    from_pair, from_other, late = lax.optimization_barrier((from_pair, from_other, late))
     vectors, guess, sums = basis(
-        levels, own, from_pair, from_other, band_rows, band_rows * holders
+        levels, own, from_pair, from_other, late, band_rows, band_rows * holders
     )
     gathered = lax.all_to_all(sums, ("by", "bx"), 0, 0, tiled=True)
-    stepped, _ = columns(*column_inputs, early, chunks, stepped, sums)
     gathered = gathered.reshape(band_rows * holders, LANES)
     return stepped, finish(gathered, vectors, guess)
 

time: 37.5 us -> 35.5 us (0.947)
  blocking collectives: 0 us -> 12 us
  starting transfers between devices: 12.9 us -> 7.31 us
  waiting for transfers between devices: 6.46 us -> 2.01 us
  Pallas kernels: 17.3 us -> 13.3 us
    all_to_all x0 -> x1, blocking collectives: none -> 12 us  [local(): gathered = lax.all_to_all(sums, ('by', 'bx'), 0, 0, tiled=True)]
    all_to_all x1 -> x0, starting transfers between devices: 5.64 us -> none  [local(): gathered = lax.all_to_all(sums, ('by', 'bx'), 0, 0, tiled=True)]
    ppermute x8, waiting for transfers between devices: 5.15 us -> 2.01 us  [swap(): return lax.ppermute(array, axis, [(i, i ^ hop) for i in range(count)])]
    pallas_call x2, Pallas kernels: 10.9 us -> 8.61 us  [the longest x1 4.91 us: first_columns(): pl.pallas_call(first_columns_kernel, in_specs=[HBM] * 5 + [pl.BlockSpec(m...]
    all_to_all x1 -> x0, waiting for transfers between devices: 1.31 us -> none  [local(): gathered = lax.all_to_all(sums, ('by', 'bx'), 0, 0, tiled=True)]
    pallas_call x1, Pallas kernels: 2.63 us -> 1.64 us  [basis(): pl.pallas_call(functools.partial(basis_kernel, levels, band_rows), in_spe...]
    pallas_call x1, Pallas kernels: 1.77 us -> 1.05 us  [finish(): pl.pallas_call(finish_kernel, in_specs=[VMEM] * 3, out_specs=VMEM, out_sh...]
  transfers between devices with their start and end apart: 10 -> 9, of which waited for: 7 -> 6; matrix products, arithmetic and copies ran while one was open for 0% -> 0% of each run, Pallas kernels for 29% -> 24%
where the time goes in v3:
time: 35.5 us; the launch traced here: 35.3 us
  Pallas kernels  13.3 us (37%)
  blocking collectives  12 us (34%)
  starting transfers between devices  7.31 us (21%)
  waiting for transfers between devices  2.01 us (6%)
  between operations  0.7 us (2%)
    all_to_all x1, blocking collectives, local(): gathered = lax.all_to_all(sums, ('by', 'bx'), 0, 0, tiled=True)  12 us
    ppermute x8, starting transfers between devices, swap(): return lax.ppermute(array, axis, [(i, i ^ hop) for i in range(count)])  7.26 us
    pallas_call x1, Pallas kernels, first_columns(): pl.pallas_call(first_columns_kernel, in_specs=[HBM] * 5 + [pl.BlockSpec(m...  4.91 us
    pallas_call x1, Pallas kernels, rest_columns(): pl.pallas_call(functools.partial(rest_columns_kernel, begin), in_specs=[H...  3.7 us
    ppermute x8, waiting for transfers between devices, swap(): return lax.ppermute(array, axis, [(i, i ^ hop) for i in range(count)])  2.01 us
    pallas_call x1, Pallas kernels, basis(): pl.pallas_call(functools.partial(basis_kernel, levels, band_rows), in_spe...  1.64 us
    pallas_call x1, Pallas kernels, payload_of(): pl.pallas_call(payload_kernel, in_specs=[HBM] * 6, out_specs=[VMEM] * 3,...  1.18 us
    pallas_call x1, Pallas kernels, finish(): pl.pallas_call(finish_kernel, in_specs=[VMEM] * 3, out_specs=VMEM, out_sh...  1.05 us
  transfers between devices with their start and end apart: 9, of which 6 were waited for; matrix products, arithmetic and copies ran while one was open for 0% of the time, Pallas kernels for 24%

profile of v3, /device:TPU:0, one launch (start us, length us, event | category | flops | bytes accessed | tf_op | source)
XLA Modules:
  0.0 35.3 jit_solution(12425140012024624134)
XLA Ops:
  0.6 1.2 %shard_map.113 = (f32[4,4,16,128]{3,2,1,0:T(8,128)S(1)}, s32[128]{0:T(128)S(1)}, s32[128]{0:T(128)S(1)}) custom-call(bf16[20,4,2048]{2,1,0:T(4,128)(2,1)} %buoyancy.1, s32[4,2048]{1,0:T(4,128)} %wet.3, f32[4,2048]{1,0:T(4,128)} %prior.1, s32[4,16,128]{2,1,0:T(8,128)} %land.1, s32[128]{0:T(128)} %clinic.1, s32[128]{0:T(128)} %tropic.1), custom_call_target="tpu_custom_call" | custom-call | tf_op jit(solution)/shard_map/pallas_call | solution.py:249
  1.8 4.0 %collective-permute-start.2 = (f32[4,4,16,128]{3,2,1,0:T(8,128)S(1)}, f32[4,4,16,128]{3,2,1,0:T(8,128)S(1)}, u32[]{:S(2)}, u32[]{:S(2)}) collective-permute-start(f32[4,4,16,128]{3,2,1,0:T(8,128)S(1)} %get-tuple-element.38.after.refs_0_), channel_id=1, source_target_pairs={{0,6},{1,7},{2,4},{3,5},{4,2},{5,3},{6,0},{7,1},{8,14},{9,15},{10,... | collective-permute-start | bytes 393224 | tf_op jit(solution)/shard_map/ppermute | solution.py:541
  5.8 0.5 %collective-permute-start.1 = (f32[4,4,16,128]{3,2,1,0:T(8,128)S(1)}, f32[4,4,16,128]{3,2,1,0:T(8,128)S(1)}, u32[]{:S(2)}, u32[]{:S(2)}) collective-permute-start(f32[4,4,16,128]{3,2,1,0:T(8,128)S(1)} %get-tuple-element.38.after.refs_0_), channel_id=1, source_target_pairs={{0,4},{1,5},{2,6},{3,7},{4,0},{5,1},{6,2},{7,3},{8,12},{9,13},{10,... | collective-permute-start | bytes 393224 | tf_op jit(solution)/shard_map/ppermute | solution.py:541
  6.3 0.1 collective-permute-start
  6.4 4.9 %shard_map.114 = (f32[20,4,16,2048]{3,2,1,0:T(8,128)}, f32[8,128]{1,0:T(8,128)S(1)}, s32[64,128]{1,0:T(8,128)S(1)}, f32[20,64,128]{2,1,0:T(8,128)S(1)}, f32[20,6...) custom-call(f32[20,4,16,2048]{3,2,1,0:T(8,128)} %tracers.3, ...), custom_call_target="tpu_custom_call" | custom-call | flops 14745600 | bytes 12533760 | tf_op jit(solution)/shard_map/pallas_call | solution.py:162
  11.3 0.0 collective-permute-done.2.refs_3_
  11.4 0.7 %collective-permute-done.1.refs_2_ = f32[4,4,16,128]{3,2,1,0:T(8,128)S(1)} collective-permute-done((f32[4,4,16,128]{3,2,1,0:T(8,128)S(1)}, f32[4,4,16,128]{3,2,1,0:T(8,128)S(1)}, u32[]{:S(2)}, u32[]{:S(2)}) %collective-permute-start.1) | collective-permute-done | bytes 131104 | tf_op jit(solution)/shard_map/ppermute | solution.py:541
  12.1 0.2 collective-permute-done.refs_1_
  12.3 0.0 collective-permute-start.3
  12.3 0.5 %collective-permute-start.4 = (f32[4,4,16,128]{3,2,1,0:T(8,128)S(1)}, f32[4,4,16,128]{3,2,1,0:T(8,128)S(1)}, u32[]{:S(2)}, u32[]{:S(2)}) collective-permute-start(f32[4,4,16,128]{3,2,1,0:T(8,128)S(1)} %collective-permute-done.refs_1_), channel_id=1, source_target_pairs={{0,1},{1,0},{2,3},{3,2},{4,5},{5,4},{6,7},{7,6},{8,9},{9,8},{10,11... | collective-permute-start | bytes 393224 | tf_op jit(solution)/shard_map/ppermute | solution.py:541
  12.8 0.0 collective-permute-start.5
  12.8 0.5 %collective-permute-start.6 = (f32[4,4,16,128]{3,2,1,0:T(8,128)S(1)}, f32[4,4,16,128]{3,2,1,0:T(8,128)S(1)}, u32[]{:S(2)}, u32[]{:S(2)}) collective-permute-start(f32[4,4,16,128]{3,2,1,0:T(8,128)S(1)} %collective-permute-done.2.refs_3_), channel_id=1, source_target_pairs={{0,1},{1,0},{2,3},{3,2},{4,5},{5,4},{6,7},{7,6},{8,9},{9,8},{10,11... | collective-permute-start | bytes 393224 | tf_op jit(solution)/shard_map/ppermute | solution.py:541
  13.4 0.3 collective-permute-done.3.refs_4_
  13.7 0.2 collective-permute-done.4.refs_5_
  13.9 0.3 collective-permute-done.5.refs_6_
  14.2 0.2 collective-permute-done.6.refs_7_
  14.4 0.8 %shard_map.115 = (f32[4,4,16,256]{3,2,1,0:T(8,128)S(1)}, f32[4,5,8,128]{3,2,1,0:T(8,128)S(1)}, f32[4,5,8,128]{3,2,1,0:T(8,128)S(1)}) custom-call(f32[4,4,16,128]{3,2,1,0:T(8,128)S(1)} %get-tuple-element.38.after.refs_0_, f32[4,4,16,128]{3,2,1,0:T(8,128)S(1)} %collective-permute-done.refs_1_, f32[4,4,16,128]{3,2,1,0:T(8,128)S(1)} %collective-permute-done.1.refs_2_, ...), custom_call_target="tpu_custom_call" | custom-call | tf_op jit(solution)/shard_map/pallas_call | solution.py:325
  15.2 1.6 %collective-permute-start.7 = (f32[4,5,8,128]{3,2,1,0:T(8,128)S(1)}, f32[4,5,8,128]{3,2,1,0:T(8,128)S(1)}, u32[]{:S(2)}, u32[]{:S(2)}) collective-permute-start(f32[4,5,8,128]{3,2,1,0:T(8,128)S(1)} %get-tuple-element.48), channel_id=1, source_target_pairs={{0,8},{8,0},{16,24},{24,16},{1,9},{9,1},{17,25},{25,17},{2,10},{10... | collective-permute-start | bytes 245768 | tf_op jit(solution)/shard_map/ppermute | solution.py:541
  16.9 0.0 collective-permute-start.8
  16.9 3.7 %shard_map.116 = (f32[20,4,16,2048]{3,2,1,0:T(8,128)}, f32[8,128]{1,0:T(8,128)S(1)}) custom-call(f32[20,4,16,2048]{3,2,1,0:T(8,128)} %tracers.3, s32[64,128]{1,0:T(8,128)S(1)} %get-tuple-element.30.regions, f32[20,64,128]{2,1,0:T(8,128)S(1)} %get-tuple-element.31.rest_0_, ...), custom_call_target="tpu_custom_call", output_to_operand_aliasing={{0}: (7, {})} | custom-call | flops 11468800 | bytes 9748480 | tf_op jit(solution)/shard_map/pallas_call | solution.py:189
  20.6 0.0 collective-permute-done.7.from_pair
  20.6 1.6 %shard_map.117 = (f32[6,64,128]{2,1,0:T(8,128)S(1)}, f32[4,16,128]{2,1,0:T(8,128)S(1)}, f32[32,1,128]{2,1,0:T(1,128)S(1)}) custom-call(f32[4,4,16,256]{3,2,1,0:T(8,128)S(1)} %get-tuple-element.47.own, f32[4,5,8,128]{3,2,1,0:T(8,128)S(1)} %collective-permute-done.7.from_pair, f32[4,5,8,128]{3,2,1,0:T(8,128)S(1)} %collective-permute-done.8.from_other, ...), custom_call_target="tpu_custom_call" | custom-call | tf_op jit(solution)/shard_map/pallas_call | solution.py:471
  22.3 12.0 %all_to_all.5 = f32[32,1,128]{2,1,0:T(1,128)S(1)} all-to-all(f32[32,1,128]{2,1,0:T(1,128)S(1)} %get-tuple-element.53), channel_id=1, replica_groups=mesh['by'=4,'bx'=8] {'by','bx'}, dimensions={0} | all-to-all | bytes 32768 | tf_op jit(solution)/shard_map/all_to_all | solution.py:593
  34.2 1.1 %shard_map.118 = f32[4,16,128]{2,1,0:T(8,128)} custom-call(f32[32,128]{1,0:T(8,128)S(1)} %bitcast.1, f32[6,64,128]{2,1,0:T(8,128)S(1)} %get-tuple-element.54.vectors, f32[4,16,128]{2,1,0:T(8,128)S(1)} %get-tuple-element.55.guess), custom_call_target="tpu_custom_call" | custom-call | tf_op jit(solution)/shard_map/pallas_call | solution.py:530
  (1 shorter events, 0.0 us)
Async XLA Ops:
  1.8 9.5 %collective-permute-start.2 = (f32[4,4,16,128]{3,2,1,0:T(8,128)S(1)}, f32[4,4,16,128]{3,2,1,0:T(8,128)S(1)}, u32[]{:S(2)}, u32[]{:S(2)}) collective-permute-start(f32[4,4,16,128]{3,2,1,0:T(8,128)S(1)} %get-tuple-element.38.after.refs_0_), channel_id=1, source_target_pairs={{0,6},{1,7},{2,4},{3,5},{4,2},{5,3},{6,0},{7,1},{8,14},{9,15},{10,... | collective-permute-start | bytes 393224 | tf_op jit(solution)/shard_map/ppermute | solution.py:541
  5.8 6.3 %collective-permute-start.1 = (f32[4,4,16,128]{3,2,1,0:T(8,128)S(1)}, f32[4,4,16,128]{3,2,1,0:T(8,128)S(1)}, u32[]{:S(2)}, u32[]{:S(2)}) collective-permute-start(f32[4,4,16,128]{3,2,1,0:T(8,128)S(1)} %get-tuple-element.38.after.refs_0_), channel_id=1, source_target_pairs={{0,4},{1,5},{2,6},{3,7},{4,0},{5,1},{6,2},{7,3},{8,12},{9,13},{10,... | collective-permute-start | bytes 393224 | tf_op jit(solution)/shard_map/ppermute | solution.py:541
  6.3 6.0 %collective-permute-start = (f32[4,4,16,128]{3,2,1,0:T(8,128)S(1)}, f32[4,4,16,128]{3,2,1,0:T(8,128)S(1)}, u32[]{:S(2)}, u32[]{:S(2)}) collective-permute-start(f32[4,4,16,128]{3,2,1,0:T(8,128)S(1)} %get-tuple-element.38.after.refs_0_), channel_id=1, source_target_pairs={{0,2},{1,3},{2,0},{3,1},{4,6},{5,7},{6,4},{7,5},{8,10},{9,11},{10,... | collective-permute-start | bytes 393224 | tf_op jit(solution)/shard_map/ppermute | solution.py:541
  12.3 1.3 %collective-permute-start.3 = (f32[4,4,16,128]{3,2,1,0:T(8,128)S(1)}, f32[4,4,16,128]{3,2,1,0:T(8,128)S(1)}, u32[]{:S(2)}, u32[]{:S(2)}) collective-permute-start(f32[4,4,16,128]{3,2,1,0:T(8,128)S(1)} %get-tuple-element.38.after.refs_0_), channel_id=1, source_target_pairs={{0,1},{1,0},{2,3},{3,2},{4,5},{5,4},{6,7},{7,6},{8,9},{9,8},{10,11... | collective-permute-start | bytes 393224 | tf_op jit(solution)/shard_map/ppermute | solution.py:541
  12.3 1.5 %collective-permute-start.4 = (f32[4,4,16,128]{3,2,1,0:T(8,128)S(1)}, f32[4,4,16,128]{3,2,1,0:T(8,128)S(1)}, u32[]{:S(2)}, u32[]{:S(2)}) collective-permute-start(f32[4,4,16,128]{3,2,1,0:T(8,128)S(1)} %collective-permute-done.refs_1_), channel_id=1, source_target_pairs={{0,1},{1,0},{2,3},{3,2},{4,5},{5,4},{6,7},{7,6},{8,9},{9,8},{10,11... | collective-permute-start | bytes 393224 | tf_op jit(solution)/shard_map/ppermute | solution.py:541
  12.8 1.3 %collective-permute-start.5 = (f32[4,4,16,128]{3,2,1,0:T(8,128)S(1)}, f32[4,4,16,128]{3,2,1,0:T(8,128)S(1)}, u32[]{:S(2)}, u32[]{:S(2)}) collective-permute-start(f32[4,4,16,128]{3,2,1,0:T(8,128)S(1)} %collective-permute-done.1.refs_2_), channel_id=1, source_target_pairs={{0,1},{1,0},{2,3},{3,2},{4,5},{5,4},{6,7},{7,6},{8,9},{9,8},{10,11... | collective-permute-start | bytes 393224 | tf_op jit(solution)/shard_map/ppermute | solution.py:541
  12.8 1.5 %collective-permute-start.6 = (f32[4,4,16,128]{3,2,1,0:T(8,128)S(1)}, f32[4,4,16,128]{3,2,1,0:T(8,128)S(1)}, u32[]{:S(2)}, u32[]{:S(2)}) collective-permute-start(f32[4,4,16,128]{3,2,1,0:T(8,128)S(1)} %collective-permute-done.2.refs_3_), channel_id=1, source_target_pairs={{0,1},{1,0},{2,3},{3,2},{4,5},{5,4},{6,7},{7,6},{8,9},{9,8},{10,11... | collective-permute-start | bytes 393224 | tf_op jit(solution)/shard_map/ppermute | solution.py:541
  15.2 5.4 %collective-permute-start.7 = (f32[4,5,8,128]{3,2,1,0:T(8,128)S(1)}, f32[4,5,8,128]{3,2,1,0:T(8,128)S(1)}, u32[]{:S(2)}, u32[]{:S(2)}) collective-permute-start(f32[4,5,8,128]{3,2,1,0:T(8,128)S(1)} %get-tuple-element.48), channel_id=1, source_target_pairs={{0,8},{8,0},{16,24},{24,16},{1,9},{9,1},{17,25},{25,17},{2,10},{10... | collective-permute-start | bytes 245768 | tf_op jit(solution)/shard_map/ppermute | solution.py:541
  16.9 3.8 %collective-permute-start.8 = (f32[4,5,8,128]{3,2,1,0:T(8,128)S(1)}, f32[4,5,8,128]{3,2,1,0:T(8,128)S(1)}, u32[]{:S(2)}, u32[]{:S(2)}) collective-permute-start(f32[4,5,8,128]{3,2,1,0:T(8,128)S(1)} %get-tuple-element.45.rest_6_), channel_id=1, source_target_pairs={{0,1},{1,0},{2,3},{3,2},{4,5},{5,4},{6,7},{7,6},{8,16},{9,17},{10,... | collective-permute-start | bytes 245768 | tf_op jit(solution)/shard_map/ppermute | solution.py:587

commit v4 on v3

--- a/solution.py
+++ b/solution.py
@@ -11,7 +11,6 @@
 RESTORE = 0.5
 SURFACE = 0.1
 FACE_SCALE = 2.0
-SHIFTS = (0.0, 2.0, 1.0, 0.4, 1.6)
 PIVOT_FLOOR = 1e-11
 HALO = 8
 LANES = 128
@@ -439,7 +438,11 @@
             images[k, place] = image[inner, 0:LANES]
             if k + 1 < ITERS:
                 following = image * inverse
-                v = following - SHIFTS[k] * v if SHIFTS[k] else following
+                if k == 1:
+                    following = v - following
+                elif k > 1:
+                    following = 2.0 * (v - following) - before
+                before, v = v, following
 
     row_id = lax.broadcasted_iota(jnp.int32, (8, LANES), 0)
     lane_id = lax.broadcasted_iota(jnp.int32, (8, LANES), 1)
@@ -576,8 +579,9 @@
     stepped, mark, regions, *factors = first_columns(
         tracers, vertical_speed, diffusivity, wet_levels, surface_patch, early, payload
     )
-    *parts, mark = lax.optimization_barrier((*parts, mark))
-    parts = parts + [swap(part, "bx", 1) for part in parts]
+    beside = swap(payload, "bx", 1)
+    beside, *parts, mark = lax.optimization_barrier((beside, *parts, mark))
+    parts = parts + [beside] + [swap(part, "bx", 1) for part in parts[1:]]
     spread = spread + [hop + 1 for hop in spread]
 
     own, to_pair, to_other = select(

time: 35.5 us -> 35.5 us (level)
  starting transfers between devices: 7.31 us -> 6.76 us
    ppermute x8, starting transfers between devices: 7.26 us -> 6.76 us  [swap(): return lax.ppermute(array, axis, [(i, i ^ hop) for i in range(count)])]
  transfers between devices with their start and end apart: 9 -> 9, of which waited for: 6 -> 5; matrix products, arithmetic and copies ran while one was open for 0% -> 0% of each run, Pallas kernels for 24% -> 24%
where the time goes in v4:
time: 35.5 us; the launch traced here: 35.3 us
  Pallas kernels  13.3 us (37%)
  blocking collectives  12.2 us (34%)
  starting transfers between devices  6.76 us (19%)
  waiting for transfers between devices  2.33 us (7%)
  between operations  0.7 us (2%)
    all_to_all x1, blocking collectives, local(): gathered = lax.all_to_all(sums, ('by', 'bx'), 0, 0, tiled=True)  12.2 us
    ppermute x8, starting transfers between devices, swap(): return lax.ppermute(array, axis, [(i, i ^ hop) for i in range(count)])  6.76 us
    pallas_call x1, Pallas kernels, first_columns(): pl.pallas_call(first_columns_kernel, in_specs=[HBM] * 5 + [pl.BlockSpec(m...  4.91 us
    pallas_call x1, Pallas kernels, rest_columns(): pl.pallas_call(functools.partial(rest_columns_kernel, begin), in_specs=[H...  3.7 us
    ppermute x8, waiting for transfers between devices, swap(): return lax.ppermute(array, axis, [(i, i ^ hop) for i in range(count)])  2.33 us
    pallas_call x1, Pallas kernels, basis(): pl.pallas_call(functools.partial(basis_kernel, levels, band_rows), in_spe...  1.66 us
    pallas_call x1, Pallas kernels, payload_of(): pl.pallas_call(payload_kernel, in_specs=[HBM] * 6, out_specs=[VMEM] * 3,...  1.18 us
    pallas_call x1, Pallas kernels, finish(): pl.pallas_call(finish_kernel, in_specs=[VMEM] * 3, out_specs=VMEM, out_sh...  1.05 us
  transfers between devices with their start and end apart: 9, of which 5 were waited for; matrix products, arithmetic and copies ran while one was open for 0% of the time, Pallas kernels for 24%

profile of v4, /device:TPU:0, one launch (start us, length us, event | category | flops | bytes accessed | tf_op | source)
XLA Modules:
  0.0 35.3 jit_solution(4337324111850516912)
XLA Ops:
  0.6 1.2 %shard_map.113 = (f32[4,4,16,128]{3,2,1,0:T(8,128)S(1)}, s32[128]{0:T(128)S(1)}, s32[128]{0:T(128)S(1)}) custom-call(bf16[20,4,2048]{2,1,0:T(4,128)(2,1)} %buoyancy.1, s32[4,2048]{1,0:T(4,128)} %wet.3, f32[4,2048]{1,0:T(4,128)} %prior.1, s32[4,16,128]{2,1,0:T(8,128)} %land.1, s32[128]{0:T(128)} %clinic.1, s32[128]{0:T(128)} %tropic.1), custom_call_target="tpu_custom_call" | custom-call | tf_op jit(solution)/shard_map/pallas_call | solution.py:248
  1.8 4.0 %collective-permute-start.3 = (f32[4,4,16,128]{3,2,1,0:T(8,128)S(1)}, f32[4,4,16,128]{3,2,1,0:T(8,128)S(1)}, u32[]{:S(2)}, u32[]{:S(2)}) collective-permute-start(f32[4,4,16,128]{3,2,1,0:T(8,128)S(1)} %get-tuple-element.39.after.refs_0_), channel_id=1, source_target_pairs={{0,6},{1,7},{2,4},{3,5},{4,2},{5,3},{6,0},{7,1},{8,14},{9,15},{10,... | collective-permute-start | bytes 393224 | tf_op jit(solution)/shard_map/ppermute | solution.py:544
  5.8 0.5 %collective-permute-start.2 = (f32[4,4,16,128]{3,2,1,0:T(8,128)S(1)}, f32[4,4,16,128]{3,2,1,0:T(8,128)S(1)}, u32[]{:S(2)}, u32[]{:S(2)}) collective-permute-start(f32[4,4,16,128]{3,2,1,0:T(8,128)S(1)} %get-tuple-element.39.after.refs_0_), channel_id=1, source_target_pairs={{0,4},{1,5},{2,6},{3,7},{4,0},{5,1},{6,2},{7,3},{8,12},{9,13},{10,... | collective-permute-start | bytes 393224 | tf_op jit(solution)/shard_map/ppermute | solution.py:544
  6.3 0.1 collective-permute-start.1
  6.4 0.0 collective-permute-start
  6.4 4.9 %shard_map.114 = (f32[20,4,16,2048]{3,2,1,0:T(8,128)}, f32[8,128]{1,0:T(8,128)S(1)}, s32[64,128]{1,0:T(8,128)S(1)}, f32[20,64,128]{2,1,0:T(8,128)S(1)}, f32[20,6...) custom-call(f32[20,4,16,2048]{3,2,1,0:T(8,128)} %tracers.3, ...), custom_call_target="tpu_custom_call" | custom-call | flops 14745600 | bytes 12533760 | tf_op jit(solution)/shard_map/pallas_call | solution.py:161
  11.3 0.0 collective-permute-done.3.refs_3_
  11.4 0.7 %collective-permute-done.2.refs_2_ = f32[4,4,16,128]{3,2,1,0:T(8,128)S(1)} collective-permute-done((f32[4,4,16,128]{3,2,1,0:T(8,128)S(1)}, f32[4,4,16,128]{3,2,1,0:T(8,128)S(1)}, u32[]{:S(2)}, u32[]{:S(2)}) %collective-permute-start.2) | collective-permute-done | bytes 131104 | tf_op jit(solution)/shard_map/ppermute | solution.py:544
  12.1 0.2 collective-permute-done.1.refs_1_
  12.3 0.0 collective-permute-done.refs_4_
  12.3 0.0 collective-permute-start.4
  12.3 0.5 %collective-permute-start.5 = (f32[4,4,16,128]{3,2,1,0:T(8,128)S(1)}, f32[4,4,16,128]{3,2,1,0:T(8,128)S(1)}, u32[]{:S(2)}, u32[]{:S(2)}) collective-permute-start(f32[4,4,16,128]{3,2,1,0:T(8,128)S(1)} %collective-permute-done.2.refs_2_), channel_id=1, source_target_pairs={{0,1},{1,0},{2,3},{3,2},{4,5},{5,4},{6,7},{7,6},{8,9},{9,8},{10,11... | collective-permute-start | bytes 393224 | tf_op jit(solution)/shard_map/ppermute | solution.py:544
  12.9 0.0 collective-permute-start.6
  12.9 0.8 %collective-permute-done.4.refs_5_ = f32[4,4,16,128]{3,2,1,0:T(8,128)S(1)} collective-permute-done((f32[4,4,16,128]{3,2,1,0:T(8,128)S(1)}, f32[4,4,16,128]{3,2,1,0:T(8,128)S(1)}, u32[]{:S(2)}, u32[]{:S(2)}) %collective-permute-start.4) | collective-permute-done | bytes 131104 | tf_op jit(solution)/shard_map/ppermute | solution.py:544
  13.7 0.2 collective-permute-done.5.refs_6_
  13.9 0.3 collective-permute-done.6.refs_7_
  14.2 0.8 %shard_map.115 = (f32[4,4,16,256]{3,2,1,0:T(8,128)S(1)}, f32[4,5,8,128]{3,2,1,0:T(8,128)S(1)}, f32[4,5,8,128]{3,2,1,0:T(8,128)S(1)}) custom-call(f32[4,4,16,128]{3,2,1,0:T(8,128)S(1)} %get-tuple-element.39.after.refs_0_, f32[4,4,16,128]{3,2,1,0:T(8,128)S(1)} %collective-permute-done.1.refs_1_, f32[4,4,16,128]{3,2,1,0:T(8,128)S(1)} %collective-permute-done.2.refs_2_, ...), custom_call_target="tpu_custom_call" | custom-call | tf_op jit(solution)/shard_map/pallas_call | solution.py:324
  15.0 1.6 %collective-permute-start.7 = (f32[4,5,8,128]{3,2,1,0:T(8,128)S(1)}, f32[4,5,8,128]{3,2,1,0:T(8,128)S(1)}, u32[]{:S(2)}, u32[]{:S(2)}) collective-permute-start(f32[4,5,8,128]{3,2,1,0:T(8,128)S(1)} %get-tuple-element.50), channel_id=1, source_target_pairs={{0,8},{8,0},{16,24},{24,16},{1,9},{9,1},{17,25},{25,17},{2,10},{10... | collective-permute-start | bytes 245768 | tf_op jit(solution)/shard_map/ppermute | solution.py:544
  16.7 0.0 collective-permute-start.8
  16.7 3.7 %shard_map.116 = (f32[20,4,16,2048]{3,2,1,0:T(8,128)}, f32[8,128]{1,0:T(8,128)S(1)}) custom-call(f32[20,4,16,2048]{3,2,1,0:T(8,128)} %tracers.3, s32[64,128]{1,0:T(8,128)S(1)} %get-tuple-element.31.regions, f32[20,64,128]{2,1,0:T(8,128)S(1)} %get-tuple-element.32.rest_0_, ...), custom_call_target="tpu_custom_call", output_to_operand_aliasing={{0}: (7, {})} | custom-call | flops 11468800 | bytes 9748480 | tf_op jit(solution)/shard_map/pallas_call | solution.py:188
  20.4 0.0 collective-permute-done.7.from_pair
  20.4 1.7 %shard_map.117 = (f32[6,64,128]{2,1,0:T(8,128)S(1)}, f32[4,16,128]{2,1,0:T(8,128)S(1)}, f32[32,1,128]{2,1,0:T(1,128)S(1)}) custom-call(f32[4,4,16,256]{3,2,1,0:T(8,128)S(1)} %get-tuple-element.49.own, f32[4,5,8,128]{3,2,1,0:T(8,128)S(1)} %collective-permute-done.7.from_pair, f32[4,5,8,128]{3,2,1,0:T(8,128)S(1)} %collective-permute-done.8.from_other, ...), custom_call_target="tpu_custom_call" | custom-call | tf_op jit(solution)/shard_map/pallas_call | solution.py:474
  22.1 12.2 %all_to_all.5 = f32[32,1,128]{2,1,0:T(1,128)S(1)} all-to-all(f32[32,1,128]{2,1,0:T(1,128)S(1)} %get-tuple-element.55), channel_id=1, replica_groups=mesh['by'=4,'bx'=8] {'by','bx'}, dimensions={0} | all-to-all | bytes 32768 | tf_op jit(solution)/shard_map/all_to_all | solution.py:597
  34.3 1.1 %shard_map.118 = f32[4,16,128]{2,1,0:T(8,128)} custom-call(f32[32,128]{1,0:T(8,128)S(1)} %bitcast.1, f32[6,64,128]{2,1,0:T(8,128)S(1)} %get-tuple-element.56.vectors, f32[4,16,128]{2,1,0:T(8,128)S(1)} %get-tuple-element.57.guess), custom_call_target="tpu_custom_call" | custom-call | tf_op jit(solution)/shard_map/pallas_call | solution.py:533
  (1 shorter events, 0.0 us)
Async XLA Ops:
  1.8 9.5 %collective-permute-start.3 = (f32[4,4,16,128]{3,2,1,0:T(8,128)S(1)}, f32[4,4,16,128]{3,2,1,0:T(8,128)S(1)}, u32[]{:S(2)}, u32[]{:S(2)}) collective-permute-start(f32[4,4,16,128]{3,2,1,0:T(8,128)S(1)} %get-tuple-element.39.after.refs_0_), channel_id=1, source_target_pairs={{0,6},{1,7},{2,4},{3,5},{4,2},{5,3},{6,0},{7,1},{8,14},{9,15},{10,... | collective-permute-start | bytes 393224 | tf_op jit(solution)/shard_map/ppermute | solution.py:544
  5.8 6.3 %collective-permute-start.2 = (f32[4,4,16,128]{3,2,1,0:T(8,128)S(1)}, f32[4,4,16,128]{3,2,1,0:T(8,128)S(1)}, u32[]{:S(2)}, u32[]{:S(2)}) collective-permute-start(f32[4,4,16,128]{3,2,1,0:T(8,128)S(1)} %get-tuple-element.39.after.refs_0_), channel_id=1, source_target_pairs={{0,4},{1,5},{2,6},{3,7},{4,0},{5,1},{6,2},{7,3},{8,12},{9,13},{10,... | collective-permute-start | bytes 393224 | tf_op jit(solution)/shard_map/ppermute | solution.py:544
  6.3 6.0 %collective-permute-start.1 = (f32[4,4,16,128]{3,2,1,0:T(8,128)S(1)}, f32[4,4,16,128]{3,2,1,0:T(8,128)S(1)}, u32[]{:S(2)}, u32[]{:S(2)}) collective-permute-start(f32[4,4,16,128]{3,2,1,0:T(8,128)S(1)} %get-tuple-element.39.after.refs_0_), channel_id=1, source_target_pairs={{0,2},{1,3},{2,0},{3,1},{4,6},{5,7},{6,4},{7,5},{8,10},{9,11},{10,... | collective-permute-start | bytes 393224 | tf_op jit(solution)/shard_map/ppermute | solution.py:544
  6.4 5.9 %collective-permute-start = (f32[4,4,16,128]{3,2,1,0:T(8,128)S(1)}, f32[4,4,16,128]{3,2,1,0:T(8,128)S(1)}, u32[]{:S(2)}, u32[]{:S(2)}) collective-permute-start(f32[4,4,16,128]{3,2,1,0:T(8,128)S(1)} %get-tuple-element.39.after.refs_0_), channel_id=1, source_target_pairs={{0,1},{1,0},{2,3},{3,2},{4,5},{5,4},{6,7},{7,6},{8,9},{9,8},{10,11... | collective-permute-start | bytes 393224 | tf_op jit(solution)/shard_map/ppermute | solution.py:544
  12.3 1.3 %collective-permute-start.4 = (f32[4,4,16,128]{3,2,1,0:T(8,128)S(1)}, f32[4,4,16,128]{3,2,1,0:T(8,128)S(1)}, u32[]{:S(2)}, u32[]{:S(2)}) collective-permute-start(f32[4,4,16,128]{3,2,1,0:T(8,128)S(1)} %collective-permute-done.1.refs_1_), channel_id=1, source_target_pairs={{0,1},{1,0},{2,3},{3,2},{4,5},{5,4},{6,7},{7,6},{8,9},{9,8},{10,11... | collective-permute-start | bytes 393224 | tf_op jit(solution)/shard_map/ppermute | solution.py:544
  12.3 1.5 %collective-permute-start.5 = (f32[4,4,16,128]{3,2,1,0:T(8,128)S(1)}, f32[4,4,16,128]{3,2,1,0:T(8,128)S(1)}, u32[]{:S(2)}, u32[]{:S(2)}) collective-permute-start(f32[4,4,16,128]{3,2,1,0:T(8,128)S(1)} %collective-permute-done.2.refs_2_), channel_id=1, source_target_pairs={{0,1},{1,0},{2,3},{3,2},{4,5},{5,4},{6,7},{7,6},{8,9},{9,8},{10,11... | collective-permute-start | bytes 393224 | tf_op jit(solution)/shard_map/ppermute | solution.py:544
  12.9 1.3 %collective-permute-start.6 = (f32[4,4,16,128]{3,2,1,0:T(8,128)S(1)}, f32[4,4,16,128]{3,2,1,0:T(8,128)S(1)}, u32[]{:S(2)}, u32[]{:S(2)}) collective-permute-start(f32[4,4,16,128]{3,2,1,0:T(8,128)S(1)} %collective-permute-done.3.refs_3_), channel_id=1, source_target_pairs={{0,1},{1,0},{2,3},{3,2},{4,5},{5,4},{6,7},{7,6},{8,9},{9,8},{10,11... | collective-permute-start | bytes 393224 | tf_op jit(solution)/shard_map/ppermute | solution.py:544
  15.0 5.4 %collective-permute-start.7 = (f32[4,5,8,128]{3,2,1,0:T(8,128)S(1)}, f32[4,5,8,128]{3,2,1,0:T(8,128)S(1)}, u32[]{:S(2)}, u32[]{:S(2)}) collective-permute-start(f32[4,5,8,128]{3,2,1,0:T(8,128)S(1)} %get-tuple-element.50), channel_id=1, source_target_pairs={{0,8},{8,0},{16,24},{24,16},{1,9},{9,1},{17,25},{25,17},{2,10},{10... | collective-permute-start | bytes 245768 | tf_op jit(solution)/shard_map/ppermute | solution.py:544
  16.7 3.7 %collective-permute-start.8 = (f32[4,5,8,128]{3,2,1,0:T(8,128)S(1)}, f32[4,5,8,128]{3,2,1,0:T(8,128)S(1)}, u32[]{:S(2)}, u32[]{:S(2)}) collective-permute-start(f32[4,5,8,128]{3,2,1,0:T(8,128)S(1)} %get-tuple-element.47.rest_6_), channel_id=1, source_target_pairs={{0,1},{1,0},{2,3},{3,2},{4,5},{5,4},{6,7},{7,6},{8,16},{9,17},{10,... | collective-permute-start | bytes 245768 | tf_op jit(solution)/shard_map/ppermute | solution.py:591

commit v5 on v4

--- a/solution.py
+++ b/solution.py
@@ -17,7 +17,7 @@
 FIELDS = 4
 ENTRIES = [(a, b) for a in range(ITERS) for b in range(a, ITERS + 1)]
 CHUNK = 512
-EARLY = 9
+EARLY = 7
 F32 = jnp.float32
 VMEM = pl.BlockSpec(memory_space=pltpu.VMEM)
 SMEM = pl.BlockSpec(memory_space=pltpu.SMEM)
@@ -64,10 +64,10 @@
         mix_above, up_above, down_above = mix, up, down
 
 
-def sweep(begin, tracers, out, regions, factors, held, in_sems, out_sems):
+def sweep(begin, tracers, out, regions, factors, held, in_sems, out_sems, ready=None):
     enter, keep, raise_, lower, sink = factors
     steps, levels, count, width = held.shape
-    blocks = tracers.shape[1]
+    blocks = out.shape[1]
     tiles = width // LANES
 
     def place(ref, j):
@@ -84,7 +84,8 @@
     tracer_ids = lax.broadcasted_iota(jnp.int32, (count, width), 0)
 
     def solve(j, carry):
-        load(j).wait()
+        if ready is None:
+            load(j).wait()
         slot = lax.rem(j + begin, blocks)
         first = (j + begin) // blocks * tiles
 
@@ -101,11 +102,17 @@
             return rows(lambda at: ref[k, at, :])
 
         above = value = None
-        here = held[j, 0]
+        def given(k):
+            if ready is None:
+                return held[j, k]
+            at = pl.multiple_of((j + begin) // blocks * width, width)
+            return ready[k, slot, :, pl.ds(at, width)]
+
+        here = given(0)
         for k in range(levels):
             result = row(keep, k) * here
             if k + 1 < levels:
-                below = held[j, k + 1]
+                below = given(k + 1)
                 result = result + row(raise_, k) * below
             if k == 0:
                 target = (rows(lambda at: regions[at, :]) == tracer_ids).astype(F32)
@@ -124,7 +131,7 @@
         return carry
 
     def run(prepare):
-        for j in range(steps):
+        for j in range(steps if ready is None else 0):
             load(j).start()
         prepare()
         lax.fori_loop(0, steps, solve, 0)
@@ -179,7 +186,7 @@
 def rest_columns_kernel(begin, tracers, regions, *rest):
     factors, (_, _, out, mark, held, in_sems, out_sems) = rest[:5], rest[5:]
     mark[...] = jnp.zeros(mark.shape, F32)
-    sweep(begin, tracers, out, regions, factors, held, in_sems, out_sems)(lambda: None)
+    sweep(begin, None, out, regions, factors, held, in_sems, out_sems, tracers)(lambda: None)
 
 
 def rest_columns(tracers, begin, previous, regions, factors, after):
@@ -187,10 +194,10 @@
     steps = cells // CHUNK * blocks - begin
     return pl.pallas_call(
         functools.partial(rest_columns_kernel, begin),
-        in_specs=[HBM] + [VMEM] * 6 + [HBM, pl.BlockSpec(memory_space=pl.ANY)],
+        in_specs=[VMEM] * 7 + [HBM, pl.BlockSpec(memory_space=pl.ANY)],
         out_specs=[HBM, VMEM],
         out_shape=[
-            jax.ShapeDtypeStruct(tracers.shape, F32),
+            jax.ShapeDtypeStruct(previous.shape, F32),
             jax.ShapeDtypeStruct((8, LANES), F32),
         ],
         scratch_shapes=[pltpu.VMEM((steps, levels, count, CHUNK), F32)]
@@ -198,7 +205,7 @@
         input_output_aliases={7: 0},
         compiler_params=params(24),
         cost_estimate=column_cost(tracers, steps),
-    )(*in_hbm(tracers), regions, *factors, *in_hbm(previous), after)
+    )(tracers, regions, *factors, *in_hbm(previous), after)
 
 
 def column_cost(tracers, steps):
@@ -225,22 +232,26 @@
     ]
     for copy in copies:
         copy.start()
-    for copy in copies:
+    for copy in copies[1:4]:
         copy.wait()
     levels, blocks, cells = force.shape
     rows = cells // LANES
     wet_now = wet_in[...]
-    total = jnp.zeros(wet_now.shape, F32)
-    for k in range(levels):
-        total = total + (k < wet_now).astype(F32) * force[k].astype(F32)
     depth = wet_now.astype(F32)
     first = prior_in[...]
     for r in range(rows):
         lanes = slice(r * LANES, (r + 1) * LANES)
-        out[0, :, r, :] = total[:, lanes]
         out[1, :, r, :] = depth[:, lanes]
         out[2, :, r, :] = first[:, lanes]
     out[3] = land_in[...].astype(F32)
+    copies[0].wait()
+    total = jnp.zeros(wet_now.shape, F32)
+    for k in range(levels):
+        total = total + (k < wet_now).astype(F32) * force[k].astype(F32)
+    for r in range(rows):
+        out[0, :, r, :] = total[:, r * LANES : (r + 1) * LANES]
+    for copy in copies[4:]:
+        copy.wait()
 
 
 def payload_of(buoyancy, wet, prior, land, clinic, tropic):
@@ -351,9 +362,13 @@
 
 
 def product(a, b):
+    return split_product(a, split(a), b, split(b))
+
+
+def split_product(a, a_parts, b, b_parts):
     value = a * b
-    a_high, a_low = split(a)
-    b_high, b_low = split(b)
+    a_high, a_low = a_parts
+    b_high, b_low = b_parts
     error = ((a_high * b_high - value) + a_high * b_low + a_low * b_high) + a_low * b_low
     return value, error
 
@@ -372,7 +387,7 @@
     return two_sum(jnp.sum(lead, axis=1, keepdims=True), rest)
 
 
-def basis_kernel(levels, band_rows, own, from_pair, from_other, _, vectors, guess, sums, images):
+def basis_kernel(levels, band_rows, own, from_pair, from_other, _, vectors, guess, sums, images, vector_parts, image_parts):
     blocks, rows = own.shape[1], own.shape[2]
     tall = rows + 2 * HALO
     inner = slice(HALO, HALO + rows)
@@ -402,6 +417,7 @@
     def above(v):
         return pltpu.roll(v, 1, 0)
 
+    fields = []
     for i in range(blocks):
         forcing, depth, prior, ocean = (
             jnp.concatenate(
@@ -421,18 +437,20 @@
         diagonal = centre + east_face + west(east_face) + south_face + above(south_face)
         inverse = 1.0 / diagonal
 
-        def operate(v):
+        def operate(v, centre=centre, east_face=east_face, south_face=south_face):
             along = east_face * (v - east(v))
             across = south_face * (v - below(v))
             return centre * v + along - west(along) + across - above(across)
 
         first = ocean * prior
         residual = ocean * forcing - operate(first)
-        v = residual * inverse
         guess[i] = first[inner, 0:LANES]
-        place = slice(i * rows, (i + 1) * rows)
-        images[ITERS, place] = residual[inner, 0:LANES]
-        for k in range(ITERS):
+        images[ITERS, slice(i * rows, (i + 1) * rows)] = residual[inner, 0:LANES]
+        fields.append((operate, inverse, residual * inverse, None))
+
+    for k in range(ITERS):
+        for i, (operate, inverse, v, before) in enumerate(fields):
+            place = slice(i * rows, (i + 1) * rows)
             image = operate(v)
             vectors[k, place] = v[inner, 0:LANES]
             images[k, place] = image[inner, 0:LANES]
@@ -442,17 +460,27 @@
                     following = v - following
                 elif k > 1:
                     following = 2.0 * (v - following) - before
-                before, v = v, following
+                fields[i] = (operate, inverse, following, v)
 
     row_id = lax.broadcasted_iota(jnp.int32, (8, LANES), 0)
     lane_id = lax.broadcasted_iota(jnp.int32, (8, LANES), 1)
+    for source, parts in ((vectors, vector_parts), (images, image_parts)):
+        for a in range(source.shape[0]):
+            for r in range(0, blocks * rows, 8):
+                parts[0, a, r : r + 8], parts[1, a, r : r + 8] = split(source[a, r : r + 8])
     placed = None
     for begin in range(0, len(ENTRIES), 8):
         packed = (jnp.zeros((8, LANES), F32),) * 2
         for offset, (a, b) in enumerate(ENTRIES[begin : begin + 8]):
             total = error = None
             for r in range(0, blocks * rows, 8):
-                value, rest = product(vectors[a, r : r + 8], images[b, r : r + 8])
+                at = slice(r, r + 8)
+                value, rest = split_product(
+                    vectors[a, at],
+                    (vector_parts[0, a, at], vector_parts[1, a, at]),
+                    images[b, at],
+                    (image_parts[0, b, at], image_parts[1, b, at]),
+                )
                 if total is None:
                     total, error = value, rest
                 else:
@@ -480,7 +508,11 @@
             jax.ShapeDtypeStruct((blocks, rows, LANES), F32),
             jax.ShapeDtypeStruct((devices, 1, LANES), F32),
         ],
-        scratch_shapes=[pltpu.VMEM((ITERS + 1, blocks * rows, LANES), F32)],
+        scratch_shapes=[
+            pltpu.VMEM((ITERS + 1, blocks * rows, LANES), F32),
+            pltpu.VMEM((2, ITERS, blocks * rows, LANES), F32),
+            pltpu.VMEM((2, ITERS + 1, blocks * rows, LANES), F32),
+        ],
         compiler_params=params(16),
     )(own, from_pair, from_other, after)
 

time: 35.5 us -> 35.2 us (level)
  Pallas kernels: 13.3 us -> 12.3 us
  waiting for transfers between devices: 2.33 us -> 2.84 us
    pallas_call x1, Pallas kernels: 3.7 us -> 3.05 us  [rest_columns(): pl.pallas_call(functools.partial(rest_columns_kernel, begin), in_specs=[V...]
    ppermute x8, waiting for transfers between devices: 2.33 us -> 2.84 us  [swap(): return lax.ppermute(array, axis, [(i, i ^ hop) for i in range(count)])]
    pallas_call x1, Pallas kernels: 4.91 us -> 4.4 us  [first_columns(): pl.pallas_call(first_columns_kernel, in_specs=[HBM] * 5 + [pl.BlockSpec(m...]
  transfers between devices with their start and end apart: 9 -> 9, of which waited for: 5 -> 5; matrix products, arithmetic and copies ran while one was open for 0% -> 0% of each run, Pallas kernels for 24% -> 21%
where the time goes in v5:
time: 35.2 us; the launch traced here: 35 us
  blocking collectives  12.4 us (35%)
  Pallas kernels  12.3 us (35%)
  starting transfers between devices  6.76 us (19%)
  waiting for transfers between devices  2.84 us (8%)
  between operations  0.71 us (2%)
    all_to_all x1, blocking collectives, local(): gathered = lax.all_to_all(sums, ('by', 'bx'), 0, 0, tiled=True)  12.4 us
    ppermute x8, starting transfers between devices, swap(): return lax.ppermute(array, axis, [(i, i ^ hop) for i in range(count)])  6.76 us
    pallas_call x1, Pallas kernels, first_columns(): pl.pallas_call(first_columns_kernel, in_specs=[HBM] * 5 + [pl.BlockSpec(m...  4.4 us
    pallas_call x1, Pallas kernels, rest_columns(): pl.pallas_call(functools.partial(rest_columns_kernel, begin), in_specs=[V...  3.05 us
    ppermute x8, waiting for transfers between devices, swap(): return lax.ppermute(array, axis, [(i, i ^ hop) for i in range(count)])  2.84 us
    pallas_call x1, Pallas kernels, basis(): pl.pallas_call(functools.partial(basis_kernel, levels, band_rows), in_spe...  1.64 us
    pallas_call x1, Pallas kernels, payload_of(): pl.pallas_call(payload_kernel, in_specs=[HBM] * 6, out_specs=[VMEM] * 3,...  1.31 us
    pallas_call x1, Pallas kernels, finish(): pl.pallas_call(finish_kernel, in_specs=[VMEM] * 3, out_specs=VMEM, out_sh...  1.05 us
  transfers between devices with their start and end apart: 9, of which 5 were waited for; matrix products, arithmetic and copies ran while one was open for 0% of the time, Pallas kernels for 21%

profile of v5, /device:TPU:0, one launch (start us, length us, event | category | flops | bytes accessed | tf_op | source)
XLA Modules:
  0.0 35.0 jit_solution(766289999311365714)
XLA Ops:
  0.6 0.0 copy-start
  0.6 1.3 %shard_map.113 = (f32[4,4,16,128]{3,2,1,0:T(8,128)S(1)}, s32[128]{0:T(128)S(1)}, s32[128]{0:T(128)S(1)}) custom-call(bf16[20,4,2048]{2,1,0:T(4,128)(2,1)} %buoyancy.1, s32[4,2048]{1,0:T(4,128)} %wet.3, f32[4,2048]{1,0:T(4,128)} %prior.1, s32[4,16,128]{2,1,0:T(8,128)} %land.1, s32[128]{0:T(128)} %clinic.1, s32[128]{0:T(128)} %tropic.1), custom_call_target="tpu_custom_call" | custom-call | tf_op jit(solution)/shard_map/pallas_call | solution.py:259
  2.0 4.0 %collective-permute-start.3 = (f32[4,4,16,128]{3,2,1,0:T(8,128)S(1)}, f32[4,4,16,128]{3,2,1,0:T(8,128)S(1)}, u32[]{:S(2)}, u32[]{:S(2)}) collective-permute-start(f32[4,4,16,128]{3,2,1,0:T(8,128)S(1)} %get-tuple-element.39.after.refs_0_), channel_id=1, source_target_pairs={{0,6},{1,7},{2,4},{3,5},{4,2},{5,3},{6,0},{7,1},{8,14},{9,15},{10,... | collective-permute-start | bytes 393224 | tf_op jit(solution)/shard_map/ppermute | solution.py:576
  5.9 0.5 %collective-permute-start.2 = (f32[4,4,16,128]{3,2,1,0:T(8,128)S(1)}, f32[4,4,16,128]{3,2,1,0:T(8,128)S(1)}, u32[]{:S(2)}, u32[]{:S(2)}) collective-permute-start(f32[4,4,16,128]{3,2,1,0:T(8,128)S(1)} %get-tuple-element.39.after.refs_0_), channel_id=1, source_target_pairs={{0,4},{1,5},{2,6},{3,7},{4,0},{5,1},{6,2},{7,3},{8,12},{9,13},{10,... | collective-permute-start | bytes 393224 | tf_op jit(solution)/shard_map/ppermute | solution.py:576
  6.4 0.1 collective-permute-start.1
  6.6 0.0 collective-permute-start
  6.6 4.4 %shard_map.114 = (f32[20,4,16,2048]{3,2,1,0:T(8,128)}, f32[8,128]{1,0:T(8,128)S(1)}, s32[64,128]{1,0:T(8,128)S(1)}, f32[20,64,128]{2,1,0:T(8,128)S(1)}, f32[20,6...) custom-call(f32[20,4,16,2048]{3,2,1,0:T(8,128)} %tracers.3, ...), custom_call_target="tpu_custom_call" | custom-call | flops 11468800 | bytes 9748480 | tf_op jit(solution)/shard_map/pallas_call | solution.py:168
  11.0 0.0 collective-permute-done.3.refs_3_
  11.0 1.2 %collective-permute-done.2.refs_2_ = f32[4,4,16,128]{3,2,1,0:T(8,128)S(1)} collective-permute-done((f32[4,4,16,128]{3,2,1,0:T(8,128)S(1)}, f32[4,4,16,128]{3,2,1,0:T(8,128)S(1)}, u32[]{:S(2)}, u32[]{:S(2)}) %collective-permute-start.2) | collective-permute-done | bytes 131104 | tf_op jit(solution)/shard_map/ppermute | solution.py:576
  12.2 0.2 collective-permute-done.1.refs_1_
  12.5 0.0 collective-permute-done.refs_4_
  12.5 0.0 collective-permute-start.4
  12.5 0.5 %collective-permute-start.5 = (f32[4,4,16,128]{3,2,1,0:T(8,128)S(1)}, f32[4,4,16,128]{3,2,1,0:T(8,128)S(1)}, u32[]{:S(2)}, u32[]{:S(2)}) collective-permute-start(f32[4,4,16,128]{3,2,1,0:T(8,128)S(1)} %collective-permute-done.2.refs_2_), channel_id=1, source_target_pairs={{0,1},{1,0},{2,3},{3,2},{4,5},{5,4},{6,7},{7,6},{8,9},{9,8},{10,11... | collective-permute-start | bytes 393224 | tf_op jit(solution)/shard_map/ppermute | solution.py:576
  13.0 0.0 collective-permute-start.6
  13.0 0.8 %collective-permute-done.4.refs_5_ = f32[4,4,16,128]{3,2,1,0:T(8,128)S(1)} collective-permute-done((f32[4,4,16,128]{3,2,1,0:T(8,128)S(1)}, f32[4,4,16,128]{3,2,1,0:T(8,128)S(1)}, u32[]{:S(2)}, u32[]{:S(2)}) %collective-permute-start.4) | collective-permute-done | bytes 131104 | tf_op jit(solution)/shard_map/ppermute | solution.py:576
  13.8 0.2 collective-permute-done.5.refs_6_
  14.0 0.3 collective-permute-done.6.refs_7_
  14.3 0.8 %shard_map.115 = (f32[4,4,16,256]{3,2,1,0:T(8,128)S(1)}, f32[4,5,8,128]{3,2,1,0:T(8,128)S(1)}, f32[4,5,8,128]{3,2,1,0:T(8,128)S(1)}) custom-call(f32[4,4,16,128]{3,2,1,0:T(8,128)S(1)} %get-tuple-element.39.after.refs_0_, f32[4,4,16,128]{3,2,1,0:T(8,128)S(1)} %collective-permute-done.1.refs_1_, f32[4,4,16,128]{3,2,1,0:T(8,128)S(1)} %collective-permute-done.2.refs_2_, ...), custom_call_target="tpu_custom_call" | custom-call | tf_op jit(solution)/shard_map/pallas_call | solution.py:335
  15.2 1.6 %collective-permute-start.7 = (f32[4,5,8,128]{3,2,1,0:T(8,128)S(1)}, f32[4,5,8,128]{3,2,1,0:T(8,128)S(1)}, u32[]{:S(2)}, u32[]{:S(2)}) collective-permute-start(f32[4,5,8,128]{3,2,1,0:T(8,128)S(1)} %get-tuple-element.50), channel_id=1, source_target_pairs={{0,8},{8,0},{16,24},{24,16},{1,9},{9,1},{17,25},{25,17},{2,10},{10... | collective-permute-start | bytes 245768 | tf_op jit(solution)/shard_map/ppermute | solution.py:576
  16.8 3.0 %shard_map.116 = (f32[20,4,16,2048]{3,2,1,0:T(8,128)}, f32[8,128]{1,0:T(8,128)S(1)}) custom-call(f32[20,4,16,2048]{3,2,1,0:T(8,128)S(1)} %copy-done, s32[64,128]{1,0:T(8,128)S(1)} %get-tuple-element.31.regions, f32[20,64,128]{2,1,0:T(8,128)S(1)} %get-tuple-element.32.rest_0_, ...), custom_call_target="tpu_custom_call", output_to_operand_aliasing={{0}: (7, {})} | custom-call | flops 14745600 | bytes 12533760 | tf_op jit(solution)/shard_map/pallas_call | solution.py:195
  19.9 0.0 collective-permute-done.7.from_pair
  19.9 1.6 %shard_map.117 = (f32[6,64,128]{2,1,0:T(8,128)S(1)}, f32[4,16,128]{2,1,0:T(8,128)S(1)}, f32[32,1,128]{2,1,0:T(1,128)S(1)}) custom-call(f32[4,4,16,256]{3,2,1,0:T(8,128)S(1)} %get-tuple-element.49.own, f32[4,5,8,128]{3,2,1,0:T(8,128)S(1)} %collective-permute-done.7.from_pair, f32[4,5,8,128]{3,2,1,0:T(8,128)S(1)} %collective-permute-done.8.from_other, ...), custom_call_target="tpu_custom_call" | custom-call | tf_op jit(solution)/shard_map/pallas_call | solution.py:502
  21.5 12.4 %all_to_all.5 = f32[32,1,128]{2,1,0:T(1,128)S(1)} all-to-all(f32[32,1,128]{2,1,0:T(1,128)S(1)} %get-tuple-element.55), channel_id=1, replica_groups=mesh['by'=4,'bx'=8] {'by','bx'}, dimensions={0} | all-to-all | bytes 32768 | tf_op jit(solution)/shard_map/all_to_all | solution.py:629
  33.9 1.1 %shard_map.118 = f32[4,16,128]{2,1,0:T(8,128)} custom-call(f32[32,128]{1,0:T(8,128)S(1)} %bitcast.1, f32[6,64,128]{2,1,0:T(8,128)S(1)} %get-tuple-element.56.vectors, f32[4,16,128]{2,1,0:T(8,128)S(1)} %get-tuple-element.57.guess), custom_call_target="tpu_custom_call" | custom-call | tf_op jit(solution)/shard_map/pallas_call | solution.py:565
  (3 shorter events, 0.0 us)
Async XLA Ops:
  0.6 16.2 %copy-start = (f32[20,4,16,2048]{3,2,1,0:T(8,128)S(1)}, f32[20,4,16,2048]{3,2,1,0:T(8,128)}, u32[]{:S(2)}) copy-start(f32[20,4,16,2048]{3,2,1,0:T(8,128)} %tracers.3) | copy-start | bytes 31457284
  2.0 9.0 %collective-permute-start.3 = (f32[4,4,16,128]{3,2,1,0:T(8,128)S(1)}, f32[4,4,16,128]{3,2,1,0:T(8,128)S(1)}, u32[]{:S(2)}, u32[]{:S(2)}) collective-permute-start(f32[4,4,16,128]{3,2,1,0:T(8,128)S(1)} %get-tuple-element.39.after.refs_0_), channel_id=1, source_target_pairs={{0,6},{1,7},{2,4},{3,5},{4,2},{5,3},{6,0},{7,1},{8,14},{9,15},{10,... | collective-permute-start | bytes 393224 | tf_op jit(solution)/shard_map/ppermute | solution.py:576
  5.9 6.3 %collective-permute-start.2 = (f32[4,4,16,128]{3,2,1,0:T(8,128)S(1)}, f32[4,4,16,128]{3,2,1,0:T(8,128)S(1)}, u32[]{:S(2)}, u32[]{:S(2)}) collective-permute-start(f32[4,4,16,128]{3,2,1,0:T(8,128)S(1)} %get-tuple-element.39.after.refs_0_), channel_id=1, source_target_pairs={{0,4},{1,5},{2,6},{3,7},{4,0},{5,1},{6,2},{7,3},{8,12},{9,13},{10,... | collective-permute-start | bytes 393224 | tf_op jit(solution)/shard_map/ppermute | solution.py:576
  6.4 6.0 %collective-permute-start.1 = (f32[4,4,16,128]{3,2,1,0:T(8,128)S(1)}, f32[4,4,16,128]{3,2,1,0:T(8,128)S(1)}, u32[]{:S(2)}, u32[]{:S(2)}) collective-permute-start(f32[4,4,16,128]{3,2,1,0:T(8,128)S(1)} %get-tuple-element.39.after.refs_0_), channel_id=1, source_target_pairs={{0,2},{1,3},{2,0},{3,1},{4,6},{5,7},{6,4},{7,5},{8,10},{9,11},{10,... | collective-permute-start | bytes 393224 | tf_op jit(solution)/shard_map/ppermute | solution.py:576
  6.6 5.9 %collective-permute-start = (f32[4,4,16,128]{3,2,1,0:T(8,128)S(1)}, f32[4,4,16,128]{3,2,1,0:T(8,128)S(1)}, u32[]{:S(2)}, u32[]{:S(2)}) collective-permute-start(f32[4,4,16,128]{3,2,1,0:T(8,128)S(1)} %get-tuple-element.39.after.refs_0_), channel_id=1, source_target_pairs={{0,1},{1,0},{2,3},{3,2},{4,5},{5,4},{6,7},{7,6},{8,9},{9,8},{10,11... | collective-permute-start | bytes 393224 | tf_op jit(solution)/shard_map/ppermute | solution.py:576
  12.5 1.3 %collective-permute-start.4 = (f32[4,4,16,128]{3,2,1,0:T(8,128)S(1)}, f32[4,4,16,128]{3,2,1,0:T(8,128)S(1)}, u32[]{:S(2)}, u32[]{:S(2)}) collective-permute-start(f32[4,4,16,128]{3,2,1,0:T(8,128)S(1)} %collective-permute-done.1.refs_1_), channel_id=1, source_target_pairs={{0,1},{1,0},{2,3},{3,2},{4,5},{5,4},{6,7},{7,6},{8,9},{9,8},{10,11... | collective-permute-start | bytes 393224 | tf_op jit(solution)/shard_map/ppermute | solution.py:576
  12.5 1.5 %collective-permute-start.5 = (f32[4,4,16,128]{3,2,1,0:T(8,128)S(1)}, f32[4,4,16,128]{3,2,1,0:T(8,128)S(1)}, u32[]{:S(2)}, u32[]{:S(2)}) collective-permute-start(f32[4,4,16,128]{3,2,1,0:T(8,128)S(1)} %collective-permute-done.2.refs_2_), channel_id=1, source_target_pairs={{0,1},{1,0},{2,3},{3,2},{4,5},{5,4},{6,7},{7,6},{8,9},{9,8},{10,11... | collective-permute-start | bytes 393224 | tf_op jit(solution)/shard_map/ppermute | solution.py:576
  13.0 1.3 %collective-permute-start.6 = (f32[4,4,16,128]{3,2,1,0:T(8,128)S(1)}, f32[4,4,16,128]{3,2,1,0:T(8,128)S(1)}, u32[]{:S(2)}, u32[]{:S(2)}) collective-permute-start(f32[4,4,16,128]{3,2,1,0:T(8,128)S(1)} %collective-permute-done.3.refs_3_), channel_id=1, source_target_pairs={{0,1},{1,0},{2,3},{3,2},{4,5},{5,4},{6,7},{7,6},{8,9},{9,8},{10,11... | collective-permute-start | bytes 393224 | tf_op jit(solution)/shard_map/ppermute | solution.py:576
  15.2 4.7 %collective-permute-start.7 = (f32[4,5,8,128]{3,2,1,0:T(8,128)S(1)}, f32[4,5,8,128]{3,2,1,0:T(8,128)S(1)}, u32[]{:S(2)}, u32[]{:S(2)}) collective-permute-start(f32[4,5,8,128]{3,2,1,0:T(8,128)S(1)} %get-tuple-element.50), channel_id=1, source_target_pairs={{0,8},{8,0},{16,24},{24,16},{1,9},{9,1},{17,25},{25,17},{2,10},{10... | collective-permute-start | bytes 245768 | tf_op jit(solution)/shard_map/ppermute | solution.py:576
  16.8 3.1 %collective-permute-start.8 = (f32[4,5,8,128]{3,2,1,0:T(8,128)S(1)}, f32[4,5,8,128]{3,2,1,0:T(8,128)S(1)}, u32[]{:S(2)}, u32[]{:S(2)}) collective-permute-start(f32[4,5,8,128]{3,2,1,0:T(8,128)S(1)} %get-tuple-element.47.rest_6_), channel_id=1, source_target_pairs={{0,1},{1,0},{2,3},{3,2},{4,5},{5,4},{6,7},{7,6},{8,16},{9,17},{10,... | collective-permute-start | bytes 245768 | tf_op jit(solution)/shard_map/ppermute | solution.py:623

commit v6 on v5

--- a/solution.py
+++ b/solution.py
@@ -517,10 +517,14 @@
     )(own, from_pair, from_other, after)
 
 
-def finish_kernel(sums, vectors, guess, out):
-    devices = sums.shape[0]
+def finish_kernel(mine, theirs, vectors, guess, out):
+    devices = mine.shape[0]
     blocks, rows = guess.shape[0], guess.shape[1]
-    pairs = [(sums[d : d + 8], jnp.zeros((8, LANES), F32)) for d in range(0, devices, 8)]
+    pairs = [
+        (rows[d : d + 8], jnp.zeros((8, LANES), F32))
+        for rows in (mine, theirs)
+        for d in range(0, devices, 8)
+    ]
     while len(pairs) > 1:
         pairs = [pair_add(pairs[j], pairs[j + 1]) for j in range(0, len(pairs), 2)]
     total, error = fold(pairs[0], 0, (4, 2, 1))
@@ -561,14 +565,14 @@
             out[b, r : r + 8] = result
 
 
-def finish(sums, vectors, guess):
+def finish(mine, theirs, vectors, guess):
     return pl.pallas_call(
         finish_kernel,
-        in_specs=[VMEM] * 3,
+        in_specs=[VMEM] * 4,
         out_specs=VMEM,
         out_shape=jax.ShapeDtypeStruct(guess.shape, F32),
         compiler_params=params(16),
-    )(sums, vectors, guess)
+    )(mine, theirs, vectors, guess)
 
 
 def swap(array, axis, hop):
@@ -624,11 +628,20 @@
     stepped, late = rest_columns(tracers, early, stepped, regions, factors, to_other)
     from_pair, from_other, late = lax.optimization_barrier((from_pair, from_other, late))
     vectors, guess, sums = basis(
-        levels, own, from_pair, from_other, late, band_rows, band_rows * holders
+        levels, own, from_pair, from_other, late, band_rows, band_rows * holders // 2
     )
-    gathered = lax.all_to_all(sums, ("by", "bx"), 0, 0, tiled=True)
-    gathered = gathered.reshape(band_rows * holders, LANES)
-    return stepped, finish(gathered, vectors, guess)
+    peers = band_rows * holders // 2
+    gathered = lax.all_to_all(
+        sums,
+        ("by", "bx"),
+        0,
+        0,
+        tiled=True,
+        axis_index_groups=[list(range(side, 2 * peers, 2))[::-1] for side in range(2)],
+    )
+    beside = swap(gathered, "bx", 1).reshape(peers, LANES)
+    gathered = gathered.reshape(peers, LANES)
+    return stepped, finish(gathered, beside, vectors, guess)
 
 
 def solution(mesh):

time: 35.2 us -> 34.8 us (0.989)
  blocking collectives: 12.4 us -> 10.8 us
  waiting for transfers between devices: 2.84 us -> 4.01 us
    all_to_all x1, blocking collectives: 12.4 us -> 10.8 us  [local(): lax.all_to_all(sums, ('by', 'bx'), 0, 0, tiled=True, axis_index_groups=[l...]
    ppermute x8 -> x9, waiting for transfers between devices: 2.84 us -> 4.01 us  [swap(): return lax.ppermute(array, axis, [(i, i ^ hop) for i in range(count)])]
    ppermute x8 -> x9, starting transfers between devices: 6.76 us -> 6.76 us  [swap(): return lax.ppermute(array, axis, [(i, i ^ hop) for i in range(count)])]
  transfers between devices with their start and end apart: 9 -> 10, of which waited for: 5 -> 6; matrix products, arithmetic and copies ran while one was open for 0% -> 0% of each run, Pallas kernels for 21% -> 22%
where the time goes in v6:
time: 34.8 us; the launch traced here: 34.6 us
  Pallas kernels  12.3 us (35%)
  blocking collectives  10.8 us (31%)
  starting transfers between devices  6.77 us (19%)
  waiting for transfers between devices  4.01 us (12%)
  between operations  0.71 us (2%)
    all_to_all x1, blocking collectives, local(): lax.all_to_all(sums, ('by', 'bx'), 0, 0, tiled=True, axis_index_groups=[l...  10.8 us
    ppermute x9, starting transfers between devices, swap(): return lax.ppermute(array, axis, [(i, i ^ hop) for i in range(count)])  6.76 us
    pallas_call x1, Pallas kernels, first_columns(): pl.pallas_call(first_columns_kernel, in_specs=[HBM] * 5 + [pl.BlockSpec(m...  4.4 us
    ppermute x9, waiting for transfers between devices, swap(): return lax.ppermute(array, axis, [(i, i ^ hop) for i in range(count)])  4.01 us
    pallas_call x1, Pallas kernels, rest_columns(): pl.pallas_call(functools.partial(rest_columns_kernel, begin), in_specs=[V...  3.05 us
    pallas_call x1, Pallas kernels, basis(): pl.pallas_call(functools.partial(basis_kernel, levels, band_rows), in_spe...  1.63 us
    pallas_call x1, Pallas kernels, payload_of(): pl.pallas_call(payload_kernel, in_specs=[HBM] * 6, out_specs=[VMEM] * 3,...  1.31 us
    pallas_call x1, Pallas kernels, finish(): pl.pallas_call(finish_kernel, in_specs=[VMEM] * 4, out_specs=VMEM, out_sh...  1.05 us
  transfers between devices with their start and end apart: 10, of which 6 were waited for; matrix products, arithmetic and copies ran while one was open for 0% of the time, Pallas kernels for 22%

profile of v6, /device:TPU:0, one launch (start us, length us, event | category | flops | bytes accessed | tf_op | source)
XLA Modules:
  0.0 34.6 jit_solution(6012128409909185621)
XLA Ops:
  0.6 0.0 copy-start
  0.6 1.3 %shard_map.113 = (f32[4,4,16,128]{3,2,1,0:T(8,128)S(1)}, s32[128]{0:T(128)S(1)}, s32[128]{0:T(128)S(1)}) custom-call(bf16[20,4,2048]{2,1,0:T(4,128)(2,1)} %buoyancy.1, s32[4,2048]{1,0:T(4,128)} %wet.3, f32[4,2048]{1,0:T(4,128)} %prior.1, s32[4,16,128]{2,1,0:T(8,128)} %land.1, s32[128]{0:T(128)} %clinic.1, s32[128]{0:T(128)} %tropic.1), custom_call_target="tpu_custom_call" | custom-call | tf_op jit(solution)/shard_map/pallas_call | solution.py:259
  2.0 4.0 %collective-permute-start.3 = (f32[4,4,16,128]{3,2,1,0:T(8,128)S(1)}, f32[4,4,16,128]{3,2,1,0:T(8,128)S(1)}, u32[]{:S(2)}, u32[]{:S(2)}) collective-permute-start(f32[4,4,16,128]{3,2,1,0:T(8,128)S(1)} %get-tuple-element.39.after.refs_0_), channel_id=1, source_target_pairs={{0,6},{1,7},{2,4},{3,5},{4,2},{5,3},{6,0},{7,1},{8,14},{9,15},{10,... | collective-permute-start | bytes 393224 | tf_op jit(solution)/shard_map/ppermute | solution.py:580
  5.9 0.5 %collective-permute-start.2 = (f32[4,4,16,128]{3,2,1,0:T(8,128)S(1)}, f32[4,4,16,128]{3,2,1,0:T(8,128)S(1)}, u32[]{:S(2)}, u32[]{:S(2)}) collective-permute-start(f32[4,4,16,128]{3,2,1,0:T(8,128)S(1)} %get-tuple-element.39.after.refs_0_), channel_id=1, source_target_pairs={{0,4},{1,5},{2,6},{3,7},{4,0},{5,1},{6,2},{7,3},{8,12},{9,13},{10,... | collective-permute-start | bytes 393224 | tf_op jit(solution)/shard_map/ppermute | solution.py:580
  6.4 0.1 collective-permute-start.1
  6.6 0.0 collective-permute-start
  6.6 4.4 %shard_map.114 = (f32[20,4,16,2048]{3,2,1,0:T(8,128)}, f32[8,128]{1,0:T(8,128)S(1)}, s32[64,128]{1,0:T(8,128)S(1)}, f32[20,64,128]{2,1,0:T(8,128)S(1)}, f32[20,6...) custom-call(f32[20,4,16,2048]{3,2,1,0:T(8,128)} %tracers.3, ...), custom_call_target="tpu_custom_call" | custom-call | flops 11468800 | bytes 9748480 | tf_op jit(solution)/shard_map/pallas_call | solution.py:168
  11.0 0.0 collective-permute-done.3.refs_3_
  11.0 1.2 %collective-permute-done.2.refs_2_ = f32[4,4,16,128]{3,2,1,0:T(8,128)S(1)} collective-permute-done((f32[4,4,16,128]{3,2,1,0:T(8,128)S(1)}, f32[4,4,16,128]{3,2,1,0:T(8,128)S(1)}, u32[]{:S(2)}, u32[]{:S(2)}) %collective-permute-start.2) | collective-permute-done | bytes 131104 | tf_op jit(solution)/shard_map/ppermute | solution.py:580
  12.2 0.2 collective-permute-done.1.refs_1_
  12.5 0.0 collective-permute-done.refs_4_
  12.5 0.5 %collective-permute-start.5 = (f32[4,4,16,128]{3,2,1,0:T(8,128)S(1)}, f32[4,4,16,128]{3,2,1,0:T(8,128)S(1)}, u32[]{:S(2)}, u32[]{:S(2)}) collective-permute-start(f32[4,4,16,128]{3,2,1,0:T(8,128)S(1)} %collective-permute-done.2.refs_2_), channel_id=1, source_target_pairs={{0,1},{1,0},{2,3},{3,2},{4,5},{5,4},{6,7},{7,6},{8,9},{9,8},{10,11... | collective-permute-start | bytes 393224 | tf_op jit(solution)/shard_map/ppermute | solution.py:580
  13.0 0.0 collective-permute-start.6
  13.0 0.8 %collective-permute-done.4.refs_5_ = f32[4,4,16,128]{3,2,1,0:T(8,128)S(1)} collective-permute-done((f32[4,4,16,128]{3,2,1,0:T(8,128)S(1)}, f32[4,4,16,128]{3,2,1,0:T(8,128)S(1)}, u32[]{:S(2)}, u32[]{:S(2)}) %collective-permute-start.4) | collective-permute-done | bytes 131104 | tf_op jit(solution)/shard_map/ppermute | solution.py:580
  13.8 0.2 collective-permute-done.5.refs_6_
  14.0 0.3 collective-permute-done.6.refs_7_
  14.3 0.8 %shard_map.115 = (f32[4,4,16,256]{3,2,1,0:T(8,128)S(1)}, f32[4,5,8,128]{3,2,1,0:T(8,128)S(1)}, f32[4,5,8,128]{3,2,1,0:T(8,128)S(1)}) custom-call(f32[4,4,16,128]{3,2,1,0:T(8,128)S(1)} %get-tuple-element.39.after.refs_0_, f32[4,4,16,128]{3,2,1,0:T(8,128)S(1)} %collective-permute-done.1.refs_1_, f32[4,4,16,128]{3,2,1,0:T(8,128)S(1)} %collective-permute-done.2.refs_2_, ...), custom_call_target="tpu_custom_call" | custom-call | tf_op jit(solution)/shard_map/pallas_call | solution.py:335
  15.2 1.6 %collective-permute-start.7 = (f32[4,5,8,128]{3,2,1,0:T(8,128)S(1)}, f32[4,5,8,128]{3,2,1,0:T(8,128)S(1)}, u32[]{:S(2)}, u32[]{:S(2)}) collective-permute-start(f32[4,5,8,128]{3,2,1,0:T(8,128)S(1)} %get-tuple-element.50), channel_id=1, source_target_pairs={{0,8},{8,0},{16,24},{24,16},{1,9},{9,1},{17,25},{25,17},{2,10},{10... | collective-permute-start | bytes 245768 | tf_op jit(solution)/shard_map/ppermute | solution.py:580
  16.8 3.0 %shard_map.116 = (f32[20,4,16,2048]{3,2,1,0:T(8,128)}, f32[8,128]{1,0:T(8,128)S(1)}) custom-call(f32[20,4,16,2048]{3,2,1,0:T(8,128)S(1)} %copy-done, s32[64,128]{1,0:T(8,128)S(1)} %get-tuple-element.31.regions, f32[20,64,128]{2,1,0:T(8,128)S(1)} %get-tuple-element.32.rest_0_, ...), custom_call_target="tpu_custom_call", output_to_operand_aliasing={{0}: (7, {})} | custom-call | flops 14745600 | bytes 12533760 | tf_op jit(solution)/shard_map/pallas_call | solution.py:195
  19.9 0.0 collective-permute-done.7.from_pair
  19.9 1.6 %shard_map.117 = (f32[6,64,128]{2,1,0:T(8,128)S(1)}, f32[4,16,128]{2,1,0:T(8,128)S(1)}, f32[16,1,128]{2,1,0:T(1,128)S(1)}) custom-call(f32[4,4,16,256]{3,2,1,0:T(8,128)S(1)} %get-tuple-element.49.own, f32[4,5,8,128]{3,2,1,0:T(8,128)S(1)} %collective-permute-done.7.from_pair, f32[4,5,8,128]{3,2,1,0:T(8,128)S(1)} %collective-permute-done.8.from_other, ...), custom_call_target="tpu_custom_call" | custom-call | tf_op jit(solution)/shard_map/pallas_call | solution.py:502
  21.5 10.8 %all_to_all.5 = f32[16,1,128]{2,1,0:T(1,128)S(1)} all-to-all(f32[16,1,128]{2,1,0:T(1,128)S(1)} %get-tuple-element.55), channel_id=1, replica_groups={{30,28,26,24,22,20,18,16,14,12,10,8,6,4,2,0},{31,29,27,25,23,21,19,17,1..., dimensions={0} | all-to-all | bytes 16384 | tf_op jit(solution)/shard_map/all_to_all | solution.py:634
  32.4 1.2 %collective-permute-done.9 = f32[16,1,128]{2,0,1:T(8,128)S(1)} collective-permute-done((f32[16,1,128]{2,0,1:T(8,128)S(1)}, f32[16,1,128]{2,0,1:T(8,128)S(1)}, u32[]{:S(2)}, u32[]{:S(2)}) %collective-permute-start.9) | collective-permute-done | bytes 8224 | tf_op jit(solution)/shard_map/ppermute | solution.py:580
  33.5 1.1 %shard_map.118 = f32[4,16,128]{2,1,0:T(8,128)} custom-call(f32[16,128]{1,0:T(8,128)S(1)} %bitcast.4, f32[16,128]{1,0:T(8,128)S(1)} %bitcast.5, f32[6,64,128]{2,1,0:T(8,128)S(1)} %get-tuple-element.56.vectors, f32[4,16,128]{2,1,0:T(8,128)S(1)} %get-tuple-element.57.guess), custom_call_target="tpu_custom_call" | custom-call | tf_op jit(solution)/shard_map/pallas_call | solution.py:569
  (5 shorter events, 0.0 us)
Async XLA Ops:
  0.6 16.2 %copy-start = (f32[20,4,16,2048]{3,2,1,0:T(8,128)S(1)}, f32[20,4,16,2048]{3,2,1,0:T(8,128)}, u32[]{:S(2)}) copy-start(f32[20,4,16,2048]{3,2,1,0:T(8,128)} %tracers.3) | copy-start | bytes 31457284
  2.0 9.0 %collective-permute-start.3 = (f32[4,4,16,128]{3,2,1,0:T(8,128)S(1)}, f32[4,4,16,128]{3,2,1,0:T(8,128)S(1)}, u32[]{:S(2)}, u32[]{:S(2)}) collective-permute-start(f32[4,4,16,128]{3,2,1,0:T(8,128)S(1)} %get-tuple-element.39.after.refs_0_), channel_id=1, source_target_pairs={{0,6},{1,7},{2,4},{3,5},{4,2},{5,3},{6,0},{7,1},{8,14},{9,15},{10,... | collective-permute-start | bytes 393224 | tf_op jit(solution)/shard_map/ppermute | solution.py:580
  5.9 6.3 %collective-permute-start.2 = (f32[4,4,16,128]{3,2,1,0:T(8,128)S(1)}, f32[4,4,16,128]{3,2,1,0:T(8,128)S(1)}, u32[]{:S(2)}, u32[]{:S(2)}) collective-permute-start(f32[4,4,16,128]{3,2,1,0:T(8,128)S(1)} %get-tuple-element.39.after.refs_0_), channel_id=1, source_target_pairs={{0,4},{1,5},{2,6},{3,7},{4,0},{5,1},{6,2},{7,3},{8,12},{9,13},{10,... | collective-permute-start | bytes 393224 | tf_op jit(solution)/shard_map/ppermute | solution.py:580
  6.4 6.0 %collective-permute-start.1 = (f32[4,4,16,128]{3,2,1,0:T(8,128)S(1)}, f32[4,4,16,128]{3,2,1,0:T(8,128)S(1)}, u32[]{:S(2)}, u32[]{:S(2)}) collective-permute-start(f32[4,4,16,128]{3,2,1,0:T(8,128)S(1)} %get-tuple-element.39.after.refs_0_), channel_id=1, source_target_pairs={{0,2},{1,3},{2,0},{3,1},{4,6},{5,7},{6,4},{7,5},{8,10},{9,11},{10,... | collective-permute-start | bytes 393224 | tf_op jit(solution)/shard_map/ppermute | solution.py:580
  6.6 5.9 %collective-permute-start = (f32[4,4,16,128]{3,2,1,0:T(8,128)S(1)}, f32[4,4,16,128]{3,2,1,0:T(8,128)S(1)}, u32[]{:S(2)}, u32[]{:S(2)}) collective-permute-start(f32[4,4,16,128]{3,2,1,0:T(8,128)S(1)} %get-tuple-element.39.after.refs_0_), channel_id=1, source_target_pairs={{0,1},{1,0},{2,3},{3,2},{4,5},{5,4},{6,7},{7,6},{8,9},{9,8},{10,11... | collective-permute-start | bytes 393224 | tf_op jit(solution)/shard_map/ppermute | solution.py:580
  12.5 1.3 %collective-permute-start.4 = (f32[4,4,16,128]{3,2,1,0:T(8,128)S(1)}, f32[4,4,16,128]{3,2,1,0:T(8,128)S(1)}, u32[]{:S(2)}, u32[]{:S(2)}) collective-permute-start(f32[4,4,16,128]{3,2,1,0:T(8,128)S(1)} %collective-permute-done.1.refs_1_), channel_id=1, source_target_pairs={{0,1},{1,0},{2,3},{3,2},{4,5},{5,4},{6,7},{7,6},{8,9},{9,8},{10,11... | collective-permute-start | bytes 393224 | tf_op jit(solution)/shard_map/ppermute | solution.py:580
  12.5 1.5 %collective-permute-start.5 = (f32[4,4,16,128]{3,2,1,0:T(8,128)S(1)}, f32[4,4,16,128]{3,2,1,0:T(8,128)S(1)}, u32[]{:S(2)}, u32[]{:S(2)}) collective-permute-start(f32[4,4,16,128]{3,2,1,0:T(8,128)S(1)} %collective-permute-done.2.refs_2_), channel_id=1, source_target_pairs={{0,1},{1,0},{2,3},{3,2},{4,5},{5,4},{6,7},{7,6},{8,9},{9,8},{10,11... | collective-permute-start | bytes 393224 | tf_op jit(solution)/shard_map/ppermute | solution.py:580
  13.0 1.3 %collective-permute-start.6 = (f32[4,4,16,128]{3,2,1,0:T(8,128)S(1)}, f32[4,4,16,128]{3,2,1,0:T(8,128)S(1)}, u32[]{:S(2)}, u32[]{:S(2)}) collective-permute-start(f32[4,4,16,128]{3,2,1,0:T(8,128)S(1)} %collective-permute-done.3.refs_3_), channel_id=1, source_target_pairs={{0,1},{1,0},{2,3},{3,2},{4,5},{5,4},{6,7},{7,6},{8,9},{9,8},{10,11... | collective-permute-start | bytes 393224 | tf_op jit(solution)/shard_map/ppermute | solution.py:580
  15.2 4.7 %collective-permute-start.7 = (f32[4,5,8,128]{3,2,1,0:T(8,128)S(1)}, f32[4,5,8,128]{3,2,1,0:T(8,128)S(1)}, u32[]{:S(2)}, u32[]{:S(2)}) collective-permute-start(f32[4,5,8,128]{3,2,1,0:T(8,128)S(1)} %get-tuple-element.50), channel_id=1, source_target_pairs={{0,8},{8,0},{16,24},{24,16},{1,9},{9,1},{17,25},{25,17},{2,10},{10... | collective-permute-start | bytes 245768 | tf_op jit(solution)/shard_map/ppermute | solution.py:580
  16.8 3.1 %collective-permute-start.8 = (f32[4,5,8,128]{3,2,1,0:T(8,128)S(1)}, f32[4,5,8,128]{3,2,1,0:T(8,128)S(1)}, u32[]{:S(2)}, u32[]{:S(2)}) collective-permute-start(f32[4,5,8,128]{3,2,1,0:T(8,128)S(1)} %get-tuple-element.47.rest_6_), channel_id=1, source_target_pairs={{0,1},{1,0},{2,3},{3,2},{4,5},{5,4},{6,7},{7,6},{8,16},{9,17},{10,... | collective-permute-start | bytes 245768 | tf_op jit(solution)/shard_map/ppermute | solution.py:627
  32.4 1.2 %collective-permute-start.9 = (f32[16,1,128]{2,0,1:T(8,128)S(1)}, f32[16,1,128]{2,0,1:T(8,128)S(1)}, u32[]{:S(2)}, u32[]{:S(2)}) collective-permute-start(f32[16,1,128]{2,0,1:T(8,128)S(1)} %bitcast.3), channel_id=1, source_target_pairs={{0,1},{1,0},{2,3},{3,2},{4,5},{5,4},{6,7},{7,6},{8,9},{9,8},{10,11... | collective-permute-start | bytes 24584 | tf_op jit(solution)/shard_map/ppermute | solution.py:580

commit v7 on v6

--- a/solution.py
+++ b/solution.py
@@ -17,7 +17,7 @@
 FIELDS = 4
 ENTRIES = [(a, b) for a in range(ITERS) for b in range(a, ITERS + 1)]
 CHUNK = 512
-EARLY = 7
+EARLY = 5
 F32 = jnp.float32
 VMEM = pl.BlockSpec(memory_space=pltpu.VMEM)
 SMEM = pl.BlockSpec(memory_space=pltpu.SMEM)
@@ -616,7 +616,7 @@
         tracers, vertical_speed, diffusivity, wet_levels, surface_patch, early, payload
     )
     beside = swap(payload, "bx", 1)
-    beside, *parts, mark = lax.optimization_barrier((beside, *parts, mark))
+    beside, *parts[2:], mark = lax.optimization_barrier((beside, *parts[2:], mark))
     parts = parts + [beside] + [swap(part, "bx", 1) for part in parts[1:]]
     spread = spread + [hop + 1 for hop in spread]
 
@@ -637,7 +637,7 @@
         0,
         0,
         tiled=True,
-        axis_index_groups=[list(range(side, 2 * peers, 2))[::-1] for side in range(2)],
+        axis_index_groups=[[(d ^ 22) for d in range(side, 2 * peers, 2)] for side in range(2)],
     )
     beside = swap(gathered, "bx", 1).reshape(peers, LANES)
     gathered = gathered.reshape(peers, LANES)

time: 34.8 us -> 35.2 us (1.011)
    pallas_call x1, Pallas kernels: 4.4 us -> 3.9 us  [first_columns(): pl.pallas_call(first_columns_kernel, in_specs=[HBM] * 5 + [pl.BlockSpec(m...]
    pallas_call x1, Pallas kernels: 3.05 us -> 3.55 us  [rest_columns(): pl.pallas_call(functools.partial(rest_columns_kernel, begin), in_specs=[V...]
  transfers between devices with their start and end apart: 10 -> 10, of which waited for: 6 -> 5; matrix products, arithmetic and copies ran while one was open for 0% -> 0% of each run, Pallas kernels for 22% -> 21%
where the time goes in v7:
time: 35.2 us; the launch traced here: 35 us
  Pallas kernels  12.3 us (35%)
  blocking collectives  10.8 us (31%)
  starting transfers between devices  6.97 us (20%)
  waiting for transfers between devices  4.26 us (12%)
  between operations  0.71 us (2%)
    all_to_all x1, blocking collectives, local(): lax.all_to_all(sums, ('by', 'bx'), 0, 0, tiled=True, axis_index_groups=[[...  10.8 us
    ppermute x9, starting transfers between devices, swap(): return lax.ppermute(array, axis, [(i, i ^ hop) for i in range(count)])  6.97 us
    ppermute x9, waiting for transfers between devices, swap(): return lax.ppermute(array, axis, [(i, i ^ hop) for i in range(count)])  4.26 us
    pallas_call x1, Pallas kernels, first_columns(): pl.pallas_call(first_columns_kernel, in_specs=[HBM] * 5 + [pl.BlockSpec(m...  3.9 us
    pallas_call x1, Pallas kernels, rest_columns(): pl.pallas_call(functools.partial(rest_columns_kernel, begin), in_specs=[V...  3.55 us
    pallas_call x1, Pallas kernels, basis(): pl.pallas_call(functools.partial(basis_kernel, levels, band_rows), in_spe...  1.63 us
    pallas_call x1, Pallas kernels, payload_of(): pl.pallas_call(payload_kernel, in_specs=[HBM] * 6, out_specs=[VMEM] * 3,...  1.31 us
    pallas_call x1, Pallas kernels, finish(): pl.pallas_call(finish_kernel, in_specs=[VMEM] * 4, out_specs=VMEM, out_sh...  1.05 us
  transfers between devices with their start and end apart: 10, of which 5 were waited for; matrix products, arithmetic and copies ran while one was open for 0% of the time, Pallas kernels for 21%

profile of v7, /device:TPU:0, one launch (start us, length us, event | category | flops | bytes accessed | tf_op | source)
XLA Modules:
  0.0 35.0 jit_solution(6338775556833419990)
XLA Ops:
  0.6 0.0 copy-start
  0.6 1.3 %shard_map.113 = (f32[4,4,16,128]{3,2,1,0:T(8,128)S(1)}, s32[128]{0:T(128)S(1)}, s32[128]{0:T(128)S(1)}) custom-call(bf16[20,4,2048]{2,1,0:T(4,128)(2,1)} %buoyancy.1, s32[4,2048]{1,0:T(4,128)} %wet.3, f32[4,2048]{1,0:T(4,128)} %prior.1, s32[4,16,128]{2,1,0:T(8,128)} %land.1, s32[128]{0:T(128)} %clinic.1, s32[128]{0:T(128)} %tropic.1), custom_call_target="tpu_custom_call" | custom-call | tf_op jit(solution)/shard_map/pallas_call | solution.py:259
  2.0 4.0 %collective-permute-start.3 = (f32[4,4,16,128]{3,2,1,0:T(8,128)S(1)}, f32[4,4,16,128]{3,2,1,0:T(8,128)S(1)}, u32[]{:S(2)}, u32[]{:S(2)}) collective-permute-start(f32[4,4,16,128]{3,2,1,0:T(8,128)S(1)} %get-tuple-element.28.after.refs_0_), channel_id=1, source_target_pairs={{0,6},{1,7},{2,4},{3,5},{4,2},{5,3},{6,0},{7,1},{8,14},{9,15},{10,... | collective-permute-start | bytes 393224 | tf_op jit(solution)/shard_map/ppermute | solution.py:580
  5.9 0.5 %collective-permute-start.2 = (f32[4,4,16,128]{3,2,1,0:T(8,128)S(1)}, f32[4,4,16,128]{3,2,1,0:T(8,128)S(1)}, u32[]{:S(2)}, u32[]{:S(2)}) collective-permute-start(f32[4,4,16,128]{3,2,1,0:T(8,128)S(1)} %get-tuple-element.28.after.refs_0_), channel_id=1, source_target_pairs={{0,4},{1,5},{2,6},{3,7},{4,0},{5,1},{6,2},{7,3},{8,12},{9,13},{10,... | collective-permute-start | bytes 393224 | tf_op jit(solution)/shard_map/ppermute | solution.py:580
  6.4 0.1 collective-permute-start
  6.6 3.9 %shard_map.114 = (f32[20,4,16,2048]{3,2,1,0:T(8,128)}, f32[8,128]{1,0:T(8,128)S(1)}, s32[64,128]{1,0:T(8,128)S(1)}, f32[20,64,128]{2,1,0:T(8,128)S(1)}, f32[20,6...) custom-call(f32[20,4,16,2048]{3,2,1,0:T(8,128)} %tracers.3, ...), custom_call_target="tpu_custom_call" | custom-call | flops 8192000 | bytes 6963200 | tf_op jit(solution)/shard_map/pallas_call | solution.py:168
  10.5 1.7 %collective-permute-done.2.refs_2_ = f32[4,4,16,128]{3,2,1,0:T(8,128)S(1)} collective-permute-done((f32[4,4,16,128]{3,2,1,0:T(8,128)S(1)}, f32[4,4,16,128]{3,2,1,0:T(8,128)S(1)}, u32[]{:S(2)}, u32[]{:S(2)}) %collective-permute-start.2) | collective-permute-done | bytes 131104 | tf_op jit(solution)/shard_map/ppermute | solution.py:580
  12.2 0.0 collective-permute-done.1.refs_4_
  12.2 0.0 collective-permute-start.5
  12.2 0.3 collective-permute-done.refs_1_
  12.5 0.2 collective-permute-start.4
  12.7 0.3 collective-permute-start.6
  13.0 0.8 %collective-permute-done.4.refs_5_ = f32[4,4,16,128]{3,2,1,0:T(8,128)S(1)} collective-permute-done((f32[4,4,16,128]{3,2,1,0:T(8,128)S(1)}, f32[4,4,16,128]{3,2,1,0:T(8,128)S(1)}, u32[]{:S(2)}, u32[]{:S(2)}) %collective-permute-start.4) | collective-permute-done | bytes 131104 | tf_op jit(solution)/shard_map/ppermute | solution.py:580
  13.9 0.0 collective-permute-done.5.refs_6_
  13.9 0.2 collective-permute-done.6.refs_7_
  14.1 0.8 %shard_map.115 = (f32[4,4,16,256]{3,2,1,0:T(8,128)S(1)}, f32[4,5,8,128]{3,2,1,0:T(8,128)S(1)}, f32[4,5,8,128]{3,2,1,0:T(8,128)S(1)}) custom-call(f32[4,4,16,128]{3,2,1,0:T(8,128)S(1)} %get-tuple-element.28.after.refs_0_, f32[4,4,16,128]{3,2,1,0:T(8,128)S(1)} %collective-permute-done.refs_1_, f32[4,4,16,128]{3,2,1,0:T(8,128)S(1)} %collective-permute-done.2.refs_2_, ...), custom_call_target="tpu_custom_call" | custom-call | tf_op jit(solution)/shard_map/pallas_call | solution.py:335
  14.9 1.8 %collective-permute-start.7 = (f32[4,5,8,128]{3,2,1,0:T(8,128)S(1)}, f32[4,5,8,128]{3,2,1,0:T(8,128)S(1)}, u32[]{:S(2)}, u32[]{:S(2)}) collective-permute-start(f32[4,5,8,128]{3,2,1,0:T(8,128)S(1)} %get-tuple-element.46), channel_id=1, source_target_pairs={{0,8},{8,0},{16,24},{24,16},{1,9},{9,1},{17,25},{25,17},{2,10},{10... | collective-permute-start | bytes 245768 | tf_op jit(solution)/shard_map/ppermute | solution.py:580
  16.8 0.0 collective-permute-start.8
  16.8 3.6 %shard_map.116 = (f32[20,4,16,2048]{3,2,1,0:T(8,128)}, f32[8,128]{1,0:T(8,128)S(1)}) custom-call(f32[20,4,16,2048]{3,2,1,0:T(8,128)S(1)} %copy-done, s32[64,128]{1,0:T(8,128)S(1)} %get-tuple-element.29.regions, f32[20,64,128]{2,1,0:T(8,128)S(1)} %get-tuple-element.30.rest_0_, ...), custom_call_target="tpu_custom_call", output_to_operand_aliasing={{0}: (7, {})} | custom-call | flops 18022400 | bytes 15319040 | tf_op jit(solution)/shard_map/pallas_call | solution.py:195
  20.3 0.0 collective-permute-done.8.from_other
  20.3 1.6 %shard_map.117 = (f32[6,64,128]{2,1,0:T(8,128)S(1)}, f32[4,16,128]{2,1,0:T(8,128)S(1)}, f32[16,1,128]{2,1,0:T(1,128)S(1)}) custom-call(f32[4,4,16,256]{3,2,1,0:T(8,128)S(1)} %get-tuple-element.45.own, f32[4,5,8,128]{3,2,1,0:T(8,128)S(1)} %collective-permute-done.7.from_pair, f32[4,5,8,128]{3,2,1,0:T(8,128)S(1)} %collective-permute-done.8.from_other, ...), custom_call_target="tpu_custom_call" | custom-call | tf_op jit(solution)/shard_map/pallas_call | solution.py:502
  22.0 10.8 %all_to_all.5 = f32[16,1,128]{2,1,0:T(1,128)S(1)} all-to-all(f32[16,1,128]{2,1,0:T(1,128)S(1)} %get-tuple-element.51), channel_id=1, replica_groups={{22,20,18,16,30,28,26,24,6,4,2,0,14,12,10,8},{23,21,19,17,31,29,27,25,7..., dimensions={0} | all-to-all | bytes 16384 | tf_op jit(solution)/shard_map/all_to_all | solution.py:634
  32.8 1.2 %collective-permute-done.9 = f32[16,1,128]{2,0,1:T(8,128)S(1)} collective-permute-done((f32[16,1,128]{2,0,1:T(8,128)S(1)}, f32[16,1,128]{2,0,1:T(8,128)S(1)}, u32[]{:S(2)}, u32[]{:S(2)}) %collective-permute-start.9) | collective-permute-done | bytes 8224 | tf_op jit(solution)/shard_map/ppermute | solution.py:580
  33.9 1.1 %shard_map.118 = f32[4,16,128]{2,1,0:T(8,128)} custom-call(f32[16,128]{1,0:T(8,128)S(1)} %bitcast.4, f32[16,128]{1,0:T(8,128)S(1)} %bitcast.5, f32[6,64,128]{2,1,0:T(8,128)S(1)} %get-tuple-element.52.vectors, f32[4,16,128]{2,1,0:T(8,128)S(1)} %get-tuple-element.53.guess), custom_call_target="tpu_custom_call" | custom-call | tf_op jit(solution)/shard_map/pallas_call | solution.py:569
  (5 shorter events, 0.0 us)
Async XLA Ops:
  0.6 16.1 %copy-start = (f32[20,4,16,2048]{3,2,1,0:T(8,128)S(1)}, f32[20,4,16,2048]{3,2,1,0:T(8,128)}, u32[]{:S(2)}) copy-start(f32[20,4,16,2048]{3,2,1,0:T(8,128)} %tracers.3) | copy-start | bytes 31457284
  2.0 8.5 %collective-permute-start.3 = (f32[4,4,16,128]{3,2,1,0:T(8,128)S(1)}, f32[4,4,16,128]{3,2,1,0:T(8,128)S(1)}, u32[]{:S(2)}, u32[]{:S(2)}) collective-permute-start(f32[4,4,16,128]{3,2,1,0:T(8,128)S(1)} %get-tuple-element.28.after.refs_0_), channel_id=1, source_target_pairs={{0,6},{1,7},{2,4},{3,5},{4,2},{5,3},{6,0},{7,1},{8,14},{9,15},{10,... | collective-permute-start | bytes 393224 | tf_op jit(solution)/shard_map/ppermute | solution.py:580
  5.9 6.3 %collective-permute-start.2 = (f32[4,4,16,128]{3,2,1,0:T(8,128)S(1)}, f32[4,4,16,128]{3,2,1,0:T(8,128)S(1)}, u32[]{:S(2)}, u32[]{:S(2)}) collective-permute-start(f32[4,4,16,128]{3,2,1,0:T(8,128)S(1)} %get-tuple-element.28.after.refs_0_), channel_id=1, source_target_pairs={{0,4},{1,5},{2,6},{3,7},{4,0},{5,1},{6,2},{7,3},{8,12},{9,13},{10,... | collective-permute-start | bytes 393224 | tf_op jit(solution)/shard_map/ppermute | solution.py:580
  6.4 5.8 %collective-permute-start.1 = (f32[4,4,16,128]{3,2,1,0:T(8,128)S(1)}, f32[4,4,16,128]{3,2,1,0:T(8,128)S(1)}, u32[]{:S(2)}, u32[]{:S(2)}) collective-permute-start(f32[4,4,16,128]{3,2,1,0:T(8,128)S(1)} %get-tuple-element.28.after.refs_0_), channel_id=1, source_target_pairs={{0,1},{1,0},{2,3},{3,2},{4,5},{5,4},{6,7},{7,6},{8,9},{9,8},{10,11... | collective-permute-start | bytes 393224 | tf_op jit(solution)/shard_map/ppermute | solution.py:580
  6.4 6.1 %collective-permute-start = (f32[4,4,16,128]{3,2,1,0:T(8,128)S(1)}, f32[4,4,16,128]{3,2,1,0:T(8,128)S(1)}, u32[]{:S(2)}, u32[]{:S(2)}) collective-permute-start(f32[4,4,16,128]{3,2,1,0:T(8,128)S(1)} %get-tuple-element.28.after.refs_0_), channel_id=1, source_target_pairs={{0,2},{1,3},{2,0},{3,1},{4,6},{5,7},{6,4},{7,5},{8,10},{9,11},{10,... | collective-permute-start | bytes 393224 | tf_op jit(solution)/shard_map/ppermute | solution.py:580
  12.2 1.6 %collective-permute-start.5 = (f32[4,4,16,128]{3,2,1,0:T(8,128)S(1)}, f32[4,4,16,128]{3,2,1,0:T(8,128)S(1)}, u32[]{:S(2)}, u32[]{:S(2)}) collective-permute-start(f32[4,4,16,128]{3,2,1,0:T(8,128)S(1)} %collective-permute-done.2.refs_2_), channel_id=1, source_target_pairs={{0,1},{1,0},{2,3},{3,2},{4,5},{5,4},{6,7},{7,6},{8,9},{9,8},{10,11... | collective-permute-start | bytes 393224 | tf_op jit(solution)/shard_map/ppermute | solution.py:580
  12.5 1.3 %collective-permute-start.4 = (f32[4,4,16,128]{3,2,1,0:T(8,128)S(1)}, f32[4,4,16,128]{3,2,1,0:T(8,128)S(1)}, u32[]{:S(2)}, u32[]{:S(2)}) collective-permute-start(f32[4,4,16,128]{3,2,1,0:T(8,128)S(1)} %collective-permute-done.refs_1_), channel_id=1, source_target_pairs={{0,1},{1,0},{2,3},{3,2},{4,5},{5,4},{6,7},{7,6},{8,9},{9,8},{10,11... | collective-permute-start | bytes 393224 | tf_op jit(solution)/shard_map/ppermute | solution.py:580
  12.7 1.3 %collective-permute-start.6 = (f32[4,4,16,128]{3,2,1,0:T(8,128)S(1)}, f32[4,4,16,128]{3,2,1,0:T(8,128)S(1)}, u32[]{:S(2)}, u32[]{:S(2)}) collective-permute-start(f32[4,4,16,128]{3,2,1,0:T(8,128)S(1)} %collective-permute-done.3.refs_3_), channel_id=1, source_target_pairs={{0,1},{1,0},{2,3},{3,2},{4,5},{5,4},{6,7},{7,6},{8,9},{9,8},{10,11... | collective-permute-start | bytes 393224 | tf_op jit(solution)/shard_map/ppermute | solution.py:580
  14.9 5.4 %collective-permute-start.7 = (f32[4,5,8,128]{3,2,1,0:T(8,128)S(1)}, f32[4,5,8,128]{3,2,1,0:T(8,128)S(1)}, u32[]{:S(2)}, u32[]{:S(2)}) collective-permute-start(f32[4,5,8,128]{3,2,1,0:T(8,128)S(1)} %get-tuple-element.46), channel_id=1, source_target_pairs={{0,8},{8,0},{16,24},{24,16},{1,9},{9,1},{17,25},{25,17},{2,10},{10... | collective-permute-start | bytes 245768 | tf_op jit(solution)/shard_map/ppermute | solution.py:580
  16.8 3.6 %collective-permute-start.8 = (f32[4,5,8,128]{3,2,1,0:T(8,128)S(1)}, f32[4,5,8,128]{3,2,1,0:T(8,128)S(1)}, u32[]{:S(2)}, u32[]{:S(2)}) collective-permute-start(f32[4,5,8,128]{3,2,1,0:T(8,128)S(1)} %get-tuple-element.43.rest_6_), channel_id=1, source_target_pairs={{0,1},{1,0},{2,3},{3,2},{4,5},{5,4},{6,7},{7,6},{8,16},{9,17},{10,... | collective-permute-start | bytes 245768 | tf_op jit(solution)/shard_map/ppermute | solution.py:627
  32.8 1.2 %collective-permute-start.9 = (f32[16,1,128]{2,0,1:T(8,128)S(1)}, f32[16,1,128]{2,0,1:T(8,128)S(1)}, u32[]{:S(2)}, u32[]{:S(2)}) collective-permute-start(f32[16,1,128]{2,0,1:T(8,128)S(1)} %bitcast.3), channel_id=1, source_target_pairs={{0,1},{1,0},{2,3},{3,2},{4,5},{5,4},{6,7},{7,6},{8,9},{9,8},{10,11... | collective-permute-start | bytes 24584 | tf_op jit(solution)/shard_map/ppermute | solution.py:580
